TPU v7x, 32 devices: a whole 2x2x4 slice. The times are simulated.
32 devices in a mesh: dp: 4 (over x, core), fsdp: 8 (over z, y).
Axes of the slice: x: 2, y: 2, z: 4, core: 2. Of those that a mesh axis runs over, the one named last changes fastest.
Arguments:
- patch_embeddings: bfloat16 [59392, 384], P(('dp', 'fsdp')), may hold values from -25 to 25, as said below
- view_side_tokens: int32 [512], P(('dp', 'fsdp')), may hold values from 6 to 14, as said below
- projection_masters: float32 [12, 384, 384], P(None, 'fsdp'), may hold values from -2 to 2, as said below
- channel_coefficients: float32 [29, 384], P(None, 'fsdp'), may hold values from -1.2 to 1.3, as said below
- head_sharpness: float32 [8], replicated, may hold values from 12 to 24
- output_adjoint: bfloat16 [59392, 384], P(('dp', 'fsdp')), may hold values from -6 to 6
- leading_covariance: float32 [16, 384, 384], P('fsdp'), as said below
- trailing_covariance: float32 [16, 384, 384], P('fsdp'), as said below
- leading_root_preconditioner: float32 [16, 384, 384], P('fsdp'), as said below
- trailing_root_preconditioner: float32 [16, 384, 384], P('fsdp'), as said below
- channel_energy_average: float32 [29, 384], P(None, 'fsdp'), as said below
- sharpness_energy_average: float32 [8], replicated, as said below
- storage_position_map: int32 [12], replicated, may hold values from 0 to 15, as said below
Outputs:
- layer_output: bfloat16 [59392, 384], P(('dp', 'fsdp'))
- incoming_tokens_grad: bfloat16 [59392, 384], P(('dp', 'fsdp'))
- projection_derivative_sum: float32 [12, 384, 384], P(None, 'fsdp')
- leading_covariance_renewed: float32 [16, 384, 384], P('fsdp')
- trailing_covariance_renewed: float32 [16, 384, 384], P('fsdp')
- projection_updated: float32 [12, 384, 384], P(None, 'fsdp')
- weight_copy: bfloat16 [12, 384, 384], P(None, 'fsdp')
- channel_params_grad: float32 [29, 384], P(None, 'fsdp')
- channel_energy_renewed: float32 [29, 384], P(None, 'fsdp')
- channel_params_updated: float32 [29, 384], P(None, 'fsdp')
- sharpness_derivative: float32 [8], replicated
- sharpness_energy_renewed: float32 [8], replicated
- sharpness_updated: float32 [8], replicated
Inputs may be any that keep to these rules, and one draw needn't show every extreme that they name: `view_side_tokens`: the crops of one device fill its first rows in order, a crop of side s holding s * s rows; the rows after them are not read; on some device they fill all 1856 rows. Distinct. Block b's statistics and roots are in slot storage_position_map[b], which index storage_position_map[b] // 2 of fsdp holds; some index of fsdp holds 2 blocks; the roots of slots without a block are not read. `patch_embeddings`: Activations. `projection_masters`: blocks of weights. `channel_coefficients`: Gains, biases and taps. `leading_covariance`: Symmetric. `trailing_covariance`: Symmetric. `leading_root_preconditioner`: Symmetric. `trailing_root_preconditioner`: Symmetric. `channel_energy_average`: Positive. `sharpness_energy_average`: Positive.
All inputs are finite; a program needn't handle non-finite values.
Results may differ from a plain program's by a relative error of at most 0.007.
The roundings to bfloat16 on the way count: a program that leaves them out, or rounds other values in their place, can miss the bound.
Values may be sent and summed in bfloat16 or wider, within the bound.
A program may use at most 256 MiB of HBM per device.

v0:
```python
import jax
import jax.numpy as jnp
from jax import lax
from jax.sharding import PartitionSpec as P

HEAD_NUMBER = 8
HDIM = 48
GSIDE = 14


exact_multiply = lax.Precision.HIGHEST
norm_epsilon = 1e-06
batch_epsilon = 1e-05
attention_epsilon = 1e-06
covariance_forgetting = 0.5
weight_rate = 0.5
vector_rate = 0.1
sharpness_step_size = 2.0
energy_epsilon = 1e-08


def crop_layout(view_sides_sequence, tok_rows):
    crop_total = view_sides_sequence.shape[0]
    crop_cells = view_sides_sequence * view_sides_sequence
    crop_ends = jnp.cumsum(crop_cells)
    crop_starts = crop_ends - crop_cells
    position = jnp.arange(GSIDE * GSIDE, dtype=jnp.int32)
    grid_row = position // GSIDE
    grid_column = position % GSIDE
    inside = (grid_row[None, :] < view_sides_sequence[:, None]) & (
        grid_column[None, :] < view_sides_sequence[:, None]
    )
    incoming_tensor = jnp.where(
        inside,
        crop_starts[:, None]
        + grid_row[None, :] * view_sides_sequence[:, None]
        + grid_column[None, :],
        tok_rows,
    )
    row_index = jnp.arange(tok_rows, dtype=jnp.int32)
    crop_index = jnp.sum((crop_ends[None, :] <= row_index[:, None]).astype(jnp.int32), axis=1)
    live_rows = row_index < crop_ends[-1]
    crop_safe = jnp.minimum(crop_index, crop_total - 1)
    crop_match = crop_safe[:, None] == jnp.arange(crop_total, dtype=jnp.int32)[None, :]
    row_side = jnp.sum(jnp.where(crop_match, view_sides_sequence[None, :], 0), axis=1)
    row_start = jnp.sum(jnp.where(crop_match, crop_starts[None, :], 0), axis=1)
    offset = row_index - row_start
    target = jnp.where(
        live_rows,
        crop_safe * (GSIDE * GSIDE) + offset // row_side * GSIDE + offset % row_side,
        crop_total * GSIDE * GSIDE,
    )
    return (inside, incoming_tensor, target, live_rows)


def regroup_into_grid(values, incoming_tensor):
    padded = jnp.concatenate([values, jnp.zeros((1, values.shape[1]), values.dtype)], axis=0)
    return jnp.take(padded, incoming_tensor, axis=0)


def into_rows(grid_cells, target):
    flattened = grid_cells.reshape(-1, grid_cells.shape[-1])
    padded = jnp.concatenate(
        [flattened, jnp.zeros((1, flattened.shape[1]), flattened.dtype)], axis=0
    )
    return jnp.take(padded, target, axis=0)


def layer_norm(skip_path_sum, norm_gain, norm_bias):
    center = jnp.mean(skip_path_sum, axis=-1, keepdims=True)
    shifted = skip_path_sum - center
    spread = jnp.mean(shifted * shifted, axis=-1, keepdims=True)
    return shifted * lax.rsqrt(spread + norm_epsilon) * norm_gain + norm_bias


def exact_gelu(values):
    return jax.nn.gelu(values, approximate=False)


def depthwise(grid_cells, tap_table):
    grid_side = grid_cells.shape[1]
    padded = jnp.pad(grid_cells, ((0, 0), (1, 1), (1, 1), (0, 0)))
    result = jnp.zeros_like(grid_cells)
    for row_shift in range(3):
        for column_shift in range(3):
            result = (
                result
                + padded[
                    :, row_shift : row_shift + grid_side, column_shift : column_shift + grid_side, :
                ]
                * tap_table[3 * row_shift + column_shift]
            )
    return result


def channel_covariance_mixing(asking_grid, lookup_grid, content_grid, head_sharpness):
    crop_count, place_count, feature_count = asking_grid.shape
    split_shape = (crop_count, place_count, HEAD_NUMBER, HDIM)
    query_heads = asking_grid.reshape(split_shape)
    key_heads = lookup_grid.reshape(split_shape)
    value_heads = content_grid.reshape(split_shape)
    asking_unit_lines = query_heads * lax.rsqrt(
        jnp.sum(query_heads * query_heads, axis=1, keepdims=True) + attention_epsilon
    )
    lookup_unit_lines = key_heads * lax.rsqrt(
        jnp.sum(key_heads * key_heads, axis=1, keepdims=True) + attention_epsilon
    )
    affinity_grid = (
        jnp.einsum(
            "xpom,xpoy->xomy", asking_unit_lines, lookup_unit_lines, precision=exact_multiply
        )
        * head_sharpness[None, :, None, None]
    )
    row_max = jnp.max(affinity_grid, axis=-1, keepdims=True)
    exp_scores = jnp.exp(affinity_grid - row_max)
    attention = exp_scores / jnp.sum(exp_scores, axis=-1, keepdims=True)
    mixed = jnp.einsum("chij,cphj->cphi", attention, value_heads, precision=exact_multiply)
    return mixed.reshape(crop_count, place_count, feature_count)


def shards(
    patch_embeddings,
    view_side_tokens,
    projection_masters,
    channel_coefficients,
    head_sharpness,
    output_adjoint,
    leading_covariance,
    trailing_covariance,
    leading_root_preconditioner,
    trailing_root_preconditioner,
    channel_energy_average,
    sharpness_energy_average,
    storage_position_map,
):
    row_count, feature_count = patch_embeddings.shape
    crop_count = view_side_tokens.shape[0]
    block_count = projection_masters.shape[0]
    expand = (block_count - 4) // 2
    shard_rows = projection_masters.shape[1]
    slot_count = leading_covariance.shape[0]
    inside, incoming_tensor, target, live_rows = crop_layout(view_side_tokens, row_count)
    live_float = live_rows.astype(jnp.float32)[:, None]
    valid_mask = inside.astype(jnp.float32).reshape(crop_count, GSIDE, GSIDE, 1)
    weight_low = projection_masters.astype(jnp.bfloat16)
    full_blocks, full_table = (
        lax.all_gather(weight_low, "fsdp", axis=1, tiled=True),
        lax.all_gather(channel_coefficients.astype(jnp.bfloat16), "fsdp", axis=1, tiled=True),
    )
    coefficient_catalog = full_table.astype(jnp.float32)
    skip_path_sum = patch_embeddings.astype(jnp.float32)
    first_norm, first_pull = jax.vjp(
        layer_norm, skip_path_sum, coefficient_catalog[0], coefficient_catalog[1]
    )
    first_low = first_norm.astype(jnp.bfloat16)
    query_rows = jnp.dot(first_low, full_blocks[0], preferred_element_type=jnp.float32)
    key_rows = jnp.dot(first_low, full_blocks[1], preferred_element_type=jnp.float32)
    value_rows = jnp.dot(first_low, full_blocks[2], preferred_element_type=jnp.float32)
    combined_grid, mixing_backprop = jax.vjp(
        channel_covariance_mixing,
        regroup_into_grid(query_rows, incoming_tensor),
        regroup_into_grid(key_rows, incoming_tensor),
        regroup_into_grid(value_rows, incoming_tensor),
        head_sharpness,
    )
    mixed_low = into_rows(combined_grid, target).astype(jnp.bfloat16)
    attention_out = jnp.dot(mixed_low, full_blocks[3], preferred_element_type=jnp.float32)
    after_attention = skip_path_sum + coefficient_catalog[2] * attention_out
    second_norm, second_pull = jax.vjp(
        layer_norm, after_attention, coefficient_catalog[3], coefficient_catalog[4]
    )
    conv_grid = regroup_into_grid(second_norm, incoming_tensor).reshape(
        crop_count, GSIDE, GSIDE, feature_count
    )
    conv_first, first_conv_pull = jax.vjp(depthwise, conv_grid, coefficient_catalog[11:20])
    activated, activation_pull = jax.vjp(exact_gelu, conv_first)
    masked = activated * valid_mask
    batch_sum, batch_square, cell_count = lax.psum(
        (
            jnp.sum(masked, axis=(0, 1, 2)),
            jnp.sum(masked * activated, axis=(0, 1, 2)),
            jnp.sum(valid_mask),
        ),
        ("dp", "fsdp"),
    )
    batch_center = batch_sum / cell_count
    batch_scale = lax.rsqrt(batch_square / cell_count - batch_center * batch_center + batch_epsilon)
    standard = (activated - batch_center) * batch_scale
    batch_out = (standard * coefficient_catalog[5] + coefficient_catalog[6]) * valid_mask
    conv_second, second_conv_pull = jax.vjp(depthwise, batch_out, coefficient_catalog[20:29])
    local_out = into_rows(conv_second.reshape(crop_count, GSIDE * GSIDE, feature_count), target)
    after_local = after_attention + coefficient_catalog[7] * local_out
    third_norm, third_pull = jax.vjp(
        layer_norm, after_local, coefficient_catalog[8], coefficient_catalog[9]
    )
    third_low = third_norm.astype(jnp.bfloat16)
    hidden_pre = jnp.einsum(
        "td,rde->tre", third_low, full_blocks[4 : 4 + expand], preferred_element_type=jnp.float32
    )
    hidden_act, hidden_pull = jax.vjp(exact_gelu, hidden_pre)
    hidden_low = hidden_act.astype(jnp.bfloat16)
    feed_out = jnp.einsum(
        "trd,rde->te", hidden_low, full_blocks[4 + expand :], preferred_element_type=jnp.float32
    )
    layer_output = ((after_local + coefficient_catalog[10] * feed_out) * live_float).astype(
        jnp.bfloat16
    )
    back_blocks = lax.all_gather(weight_low, "fsdp", axis=1, tiled=True)
    incoming_entry = output_adjoint.astype(jnp.float32) * live_float
    scale_three_grad = jnp.sum(incoming_entry * feed_out, axis=0)
    feed_grad = (incoming_entry * coefficient_catalog[10]).astype(jnp.bfloat16)
    hidden_grad = jnp.einsum(
        "te,rde->trd", feed_grad, back_blocks[4 + expand :], preferred_element_type=jnp.float32
    )
    down_grad = jnp.einsum("trd,te->rde", hidden_low, feed_grad, preferred_element_type=jnp.float32)
    pre_grad = hidden_pull(hidden_grad)[0].astype(jnp.bfloat16)
    third_grad = jnp.einsum(
        "tre,rde->td", pre_grad, back_blocks[4 : 4 + expand], preferred_element_type=jnp.float32
    )
    up_grad = jnp.einsum("td,tre->rde", third_low, pre_grad, preferred_element_type=jnp.float32)
    local_grad, gain_three, bias_three = third_pull(third_grad)
    local_total = incoming_entry + local_grad
    scale_two_grad = jnp.sum(local_total * local_out, axis=0)
    conv_back = regroup_into_grid(local_total * coefficient_catalog[7], incoming_tensor).reshape(
        crop_count, GSIDE, GSIDE, feature_count
    )
    batch_grad, taps_two = second_conv_pull(conv_back)
    batch_masked = batch_grad * valid_mask
    beta_part = jnp.sum(batch_masked, axis=(0, 1, 2))
    gamma_part = jnp.sum(batch_masked * standard, axis=(0, 1, 2))
    beta_total, gamma_total = lax.psum((beta_part, gamma_part), ("dp", "fsdp"))
    activated_grad = (
        valid_mask
        * batch_scale
        * coefficient_catalog[5]
        * (batch_masked - (beta_total + standard * gamma_total) / cell_count)
    )
    conv_first_grad = activation_pull(activated_grad)[0]
    norm_two_grad, taps_one = first_conv_pull(conv_first_grad)
    second_grad = into_rows(norm_two_grad.reshape(crop_count, GSIDE * GSIDE, feature_count), target)
    attention_grad, gain_two, bias_two = second_pull(second_grad)
    attention_total = local_total + attention_grad
    scale_one_grad = jnp.sum(attention_total * attention_out, axis=0)
    output_grad_low = (attention_total * coefficient_catalog[2]).astype(jnp.bfloat16)
    mixed_grad = jnp.einsum(
        "te,de->td", output_grad_low, back_blocks[3], preferred_element_type=jnp.float32
    )
    output_weight_grad = jnp.einsum(
        "td,te->de", mixed_low, output_grad_low, preferred_element_type=jnp.float32
    )
    asking_backprop, lookup_backprop, content_backprop, sharpness_share = mixing_backprop(
        regroup_into_grid(mixed_grad, incoming_tensor)
    )
    query_low = into_rows(asking_backprop, target).astype(jnp.bfloat16)
    key_low = into_rows(lookup_backprop, target).astype(jnp.bfloat16)
    value_low = into_rows(content_backprop, target).astype(jnp.bfloat16)
    first_grad = jnp.einsum(
        "te,de->td", query_low, back_blocks[0], preferred_element_type=jnp.float32
    )
    first_grad = first_grad + jnp.einsum(
        "te,de->td", key_low, back_blocks[1], preferred_element_type=jnp.float32
    )
    first_grad = first_grad + jnp.einsum(
        "te,de->td", value_low, back_blocks[2], preferred_element_type=jnp.float32
    )
    query_weight_grad = jnp.einsum(
        "td,te->de", first_low, query_low, preferred_element_type=jnp.float32
    )
    key_weight_grad = jnp.einsum(
        "td,te->de", first_low, key_low, preferred_element_type=jnp.float32
    )
    value_weight_grad = jnp.einsum(
        "td,te->de", first_low, value_low, preferred_element_type=jnp.float32
    )
    input_part, gain_one, bias_one = first_pull(first_grad)
    incoming_tokens_grad = (attention_total + input_part).astype(jnp.bfloat16)
    table_grad = jnp.concatenate(
        [
            jnp.stack(
                [
                    gain_one,
                    bias_one,
                    scale_one_grad,
                    gain_two,
                    bias_two,
                    gamma_part,
                    beta_part,
                    scale_two_grad,
                    gain_three,
                    bias_three,
                    scale_three_grad,
                ]
            ),
            taps_one,
            taps_two,
        ],
        axis=0,
    )
    block_grad = jnp.concatenate(
        [
            jnp.stack([query_weight_grad, key_weight_grad, value_weight_grad, output_weight_grad]),
            up_grad,
            down_grad,
        ],
        axis=0,
    )
    denominator_sum = lax.axis_size("fsdp")
    tiled_part = jnp.broadcast_to(
        sharpness_share[None, :], (denominator_sum, sharpness_share.shape[0])
    )
    portion_derivative, catalog_portion, sharpness_normalizer = (
        lax.psum_scatter(block_grad, "fsdp", scatter_dimension=1, tiled=True),
        lax.psum_scatter(table_grad, "fsdp", scatter_dimension=1, tiled=True),
        lax.psum_scatter(tiled_part, "fsdp", scatter_dimension=0, tiled=True),
    )
    portion_derivative, catalog_portion, sharpness_normalizer = lax.psum(
        (portion_derivative, catalog_portion, sharpness_normalizer), "dp"
    )
    sharpness_derivative = sharpness_normalizer[0]
    shard_place = lax.axis_index("fsdp")
    slot_index = jnp.arange(denominator_sum * slot_count, dtype=jnp.int32)
    slot_match = storage_position_map[None, :] == slot_index[:, None]
    slot_filled = jnp.any(slot_match, axis=1).astype(jnp.float32)[:, None, None]
    slot_block = jnp.sum(
        jnp.where(slot_match, jnp.arange(block_count, dtype=jnp.int32)[None, :], 0), axis=1
    )
    my_filled = lax.dynamic_slice_in_dim(slot_filled, shard_place * slot_count, slot_count, 0)
    my_block = lax.dynamic_slice_in_dim(slot_block, shard_place * slot_count, slot_count, 0)
    whole_grad = lax.all_gather(portion_derivative, "fsdp", axis=1, tiled=True)
    owned_grad = jnp.take(whole_grad, my_block, axis=0) * my_filled
    leading_covariance_renewed = covariance_forgetting * leading_covariance + (
        1.0 - covariance_forgetting
    ) * jnp.einsum("sij,skj->sik", owned_grad, owned_grad, precision=exact_multiply)
    trailing_covariance_renewed = covariance_forgetting * trailing_covariance + (
        1.0 - covariance_forgetting
    ) * jnp.einsum("sji,sjk->sik", owned_grad, owned_grad, precision=exact_multiply)
    halfway = jnp.einsum(
        "sij,sjk->sik", leading_root_preconditioner, owned_grad, precision=exact_multiply
    )
    conditioned = jnp.einsum(
        "sij,sjk->sik", halfway, trailing_root_preconditioner, precision=exact_multiply
    )
    every_update = lax.all_gather(conditioned, "fsdp", axis=0, tiled=True)
    my_rows = lax.dynamic_slice_in_dim(every_update, shard_place * shard_rows, shard_rows, 1)
    update = jnp.take(my_rows, storage_position_map, axis=0)
    projection_updated = projection_masters - weight_rate * update
    channel_energy_renewed = (
        covariance_forgetting * channel_energy_average
        + (1.0 - covariance_forgetting) * catalog_portion * catalog_portion
    )
    channel_params_updated = channel_coefficients - vector_rate * catalog_portion / (
        jnp.sqrt(channel_energy_renewed) + energy_epsilon
    )
    sharpness_energy_renewed = (
        covariance_forgetting * sharpness_energy_average
        + (1.0 - covariance_forgetting) * sharpness_derivative * sharpness_derivative
    )
    sharpness_updated = head_sharpness - sharpness_step_size * sharpness_derivative / (
        jnp.sqrt(sharpness_energy_renewed) + energy_epsilon
    )
    return (
        layer_output,
        incoming_tokens_grad,
        portion_derivative,
        leading_covariance_renewed,
        trailing_covariance_renewed,
        projection_updated,
        projection_updated.astype(jnp.bfloat16),
        catalog_portion,
        channel_energy_renewed,
        channel_params_updated,
        sharpness_derivative,
        sharpness_energy_renewed,
        sharpness_updated,
    )


def solution(mesh):
    in_specs = (
        P(("dp", "fsdp"), None),
        P(("dp", "fsdp")),
        P(None, "fsdp", None),
        P(None, "fsdp"),
        P(),
        P(("dp", "fsdp"), None),
        P("fsdp", None, None),
        P("fsdp", None, None),
        P("fsdp", None, None),
        P("fsdp", None, None),
        P(None, "fsdp"),
        P(),
        P(),
    )
    out_specs = (
        P(("dp", "fsdp"), None),
        P(("dp", "fsdp"), None),
        P(None, "fsdp", None),
        P("fsdp", None, None),
        P("fsdp", None, None),
        P(None, "fsdp", None),
        P(None, "fsdp", None),
        P(None, "fsdp"),
        P(None, "fsdp"),
        P(None, "fsdp"),
        P(),
        P(),
        P(),
    )
    return jax.shard_map(shards, mesh=mesh, in_specs=in_specs, out_specs=out_specs, check_vma=False)
```

profile of v0, /device:TPU:1, one launch (start us, length us, event | category | flops | bytes accessed | tf_op | source)
XLA Modules:
  0.0 1363.8 jit_solution(15871071977524032583)
XLA Ops:
  11.6 25.8 %all-gather = bf16[8,48,29]{1,2,0:T(8,128)(2,1)S(1)} all-gather(bf16[1,48,29]{1,2,0:T(8,128)(2,1)S(1)} %convert_bitcast_fusion), channel_id=1, replica_groups=mesh['dp'=4,'fsdp'=8] {'fsdp'}, dimensions={0}, use_global_device_ids=true | all-gather | bytes 25056 | tf_op jit(solution)/shard_map/all_gather | solution.py:148
  49.3 28.2 %all-gather.5.cloned.1.call-done = bf16[12,384,384]{2,1,0:T(8,128)(2,1)} async-done(((bf16[12,48,384]{2,1,0:T(8,128)(2,1)}), bf16[12,384,384]{2,1,0:T(8,128)(2,1)}) %all-gather.5.cloned.1.call-update) | async-done | bytes 3538960 | tf_op jit(solution)/shard_map/all_gather | solution.py:147
  81.8 11.8 gather_fusion.2
  103.0 11.7 gather_fusion.4
  124.1 11.7 gather_fusion.3
  141.0 9.9 multiply_reduce_fusion.2
  170.0 10.8 multiply_reduce_fusion.33
  182.6 8.3 convolution_bitcast_fusion.3
  190.9 8.2 copy.201
  199.1 9.3 reshape.610
  211.7 8.6 gather_fusion.5
  229.2 11.7 gather_fusion.6
  249.8 16.0 %multiply_reduce_fusion = (f32[384]{0:T(512)S(1)}, f32[384]{0:T(512)S(1)}, f32[16,14,14,384]{3,0,2,1:T(8,128)}, f32[16,14,14,384]{3,0,2,1:T(8,128)}) fusion(f32[16,14,14]{0,2,1:T(8,128)S(1)} %and_convert_fusion.3, f32[384]{0:T(512)S(1)} %get-tuple-element.143, f32[384]{0:T(512)S(1)} %get-tuple-element.144, f32[384]{0:T(512)S(1)} %get-tuple-element.145, ...), kind=kLoop, calls=%fused_computation.55 | loop fusion | flops 102358272 | bytes 14480128 | tf_op jit(solution)/shard_map/reduce_sum | solution.py:180
  265.8 39.6 %all-reduce.52 = (f32[384]{0:T(512)S(1)}, f32[]{:T(128)}, f32[384]{0:T(512)S(1)}) all-reduce(f32[384]{0:T(512)S(1)} %get-tuple-element.96, f32[]{:T(128)} %fusion.79, f32[384]{0:T(512)S(1)} %get-tuple-element.95), channel_id=1, replica_groups=mesh['dp'=4,'fsdp'=8] {'dp','fsdp'}, use_global_device_ids=true, to_apply=%region_17.20 | all-reduce | flops 769 | bytes 6152 | tf_op jit(solution)/shard_map/psum | solution.py:178
  334.3 9.0 gather_fusion.7
  353.6 27.0 %multiply_convert_fusion = (bf16[1856,4,384]{2,0,1:T(8,128)(2,1)}, f32[1856,4,384]{2,0,1:T(8,128)}) fusion(f32[1856,4,384]{2,0,1:T(8,128)S(1)} %get-tuple-element.232, u8[1856,384]{1,0:T(8,128)(4,1)S(1)} %get-tuple-element.94, u8[1856,384]{1,0:T(8,128)(4,1)S(1)} %get-tuple-element.93), kind=kLoop, calls=%fused_computation.22 | loop fusion | flops 199557120 | bytes 29933568 | tf_op jit(solution)/shard_map/convert_element_type | solution.py:201
  380.6 11.4 add_convert_fusion
  405.3 11.7 gather_fusion.8
  428.0 30.6 %multiply_reduce_fusion.11 = (f32[384]{0:T(512)}, f32[384]{0:T(512)}, f32[384]{0:T(512)}, f32[384]{0:T(512)}, f32[384]{0:T(512)}, /*index=5*/f32[384]{0:T(512)},...) fusion(f32[16,14,14,384]{3,0,2,1:T(8,128)} %bitcast.138, ...), kind=kLoop, calls=%fused_computation.96 | loop fusion | flops 32510592 | bytes 53013504 | tf_op jit(solution)/shard_map/transpose(jvp())/reduce_sum | solution.py:88
  464.8 15.2 %fusion.110 = (f32[384]{0:T(512)S(1)}, f32[384]{0:T(512)S(1)}, f32[16,14,14,384]{3,0,2,1:T(8,128)}) fusion(f32[384]{0:T(512)S(1)} %get-tuple-element.228, f32[384]{0:T(512)S(1)} %get-tuple-element.227, f32[16,14,14,384]{3,0,2,1:T(8,128)} %get-tuple-element.194, f32[16,14,14,384]{3,0,2,1:T(8,128)} %get-tuple-element.195, ...), kind=kLoop, calls=%fused_computation.394 | loop fusion | flops 16858368 | bytes 48187648 | tf_op jit(solution)/shard_map/reduce_sum | solution.py:229
  480.0 40.5 %all-reduce.51 = (f32[384]{0:T(512)S(1)}, f32[384]{0:T(512)S(1)}) all-reduce(f32[384]{0:T(512)S(1)} %get-tuple-element.120, f32[384]{0:T(512)S(1)} %get-tuple-element.119), channel_id=1, replica_groups=mesh['dp'=4,'fsdp'=8] {'dp','fsdp'}, use_global_device_ids=true, to_apply=%region_25.28 | all-reduce | flops 768 | bytes 6144 | tf_op jit(solution)/shard_map/psum | solution.py:231
  520.5 22.3 %multiply_reduce_fusion.20 = (f32[384]{0:T(512)}, f32[384]{0:T(512)}, f32[384]{0:T(512)}, f32[384]{0:T(512)}, f32[384]{0:T(512)}, /*index=5*/f32[384]{0:T(512)},...) fusion(f32[16,14,14,384]{3,0,2,1:T(8,128)} %bitcast.133, ...), kind=kLoop, calls=%fused_computation.105 | loop fusion | flops 49369728 | bytes 24118532 | tf_op jit(solution)/shard_map/transpose(jvp())/reduce_sum | solution.py:88
  542.8 13.9 %broadcast_multiply_fusion.9 = (f32[16,14,14,384]{3,0,2,1:T(8,128)}, f32[16,14,14,384]{3,0,2,1:T(8,128)}, f32[16,14,14,384]{3,0,2,1:T(8,128)}, f32[16,14,14,384]...) fusion(f32[16,14,14,384]{3,0,2,1:T(8,128)S(1)} %get-tuple-eleme, ...), kind=kLoop, calls=%fused_computation.203 | loop fusion | flops 10838016 | bytes 48182784 | tf_op jit(solution)/shard_map/transpose(jvp())/mul | solution.py:88
  562.9 9.7 pad_add_fusion.2
  587.8 9.0 gather_fusion.9
  596.8 11.8 multiply_reduce_fusion.24
  618.3 11.7 gather_fusion.10
  645.8 12.2 convolution_bitcast_fusion.2
  658.0 14.6 %convert_reduce_fusion.1 = (f32[16,8,48]{2,1,0:T(8,128)S(1)}, pred[16,8,48,48]{2,3,1,0:T(8,128)(4,1)S(1)}, f32[16,8,48]{2,1,0:T(8,128)S(1)}, f32[16,8,48,48]{2,3,1,0:T(8,128)}) fusion(f32[16,8,48]{2,1,0:T(8,128)S(1)} %copy-done.32, f32[16,8,48,48]{2,3,1,0:T(8,128)S(1)} %copy-done.2, f32[8]{0:T(128)S(1)} %copy-done.71, f32[16,8,48]{2,1,0:T(8,128)S(1)} %copy-done.47, ...), kind=kOutput, calls=%fused_computation.140 | convolution fusion | flops 695980032 | bytes 12386336 | tf_op jit(solution)/shard_map/transpose(jvp(chij,cphj->cphi))/dot_general | solution.py:117
  676.2 11.7 fusion.6
  687.9 11.3 fusion.7
  699.2 8.3 copy.204
  707.5 9.3 reshape.613
  720.1 8.3 gather_fusion.13
  736.2 8.3 copy.203
  744.4 9.3 reshape.612
  757.0 8.3 gather_fusion.12
  772.9 8.2 copy.202
  781.1 9.4 reshape.611
  793.9 8.4 gather_fusion.11
  824.7 10.1 copy.189
  835.0 163.9 %reduce-scatter.5.cloned.1.call-done = f32[12,48,384]{2,0,1:T(8,128)} async-done(((f32[12,384,384]{2,0,1:T(8,128)}), f32[12,48,384]{2,0,1:T(8,128)}) %reduce-scatter.5.cloned.1.call-update) | async-done | bytes 884752 | tf_op jit(solution)/shard_map/reduce_scatter | solution.py:312
  999.0 38.6 %all-reduce.56.cloned.1.call-done = f32[12,48,384]{2,0,1:T(8,128)} async-done(((f32[12,48,384]{2,0,1:T(8,128)}), f32[12,48,384]{2,0,1:T(8,128)}) %all-reduce.56.cloned.1.call-update) | async-done | bytes 884752 | tf_op jit(solution)/shard_map/psum | solution.py:316
  1065.4 83.4 %all-gather.7.cloned.1.call-done = f32[12,384,384]{2,1,0:T(8,128)} async-done(((f32[12,48,384]{2,1,0:T(8,128)}), f32[12,384,384]{2,1,0:T(8,128)}) %all-gather.7.cloned.1.call-update) | async-done | bytes 7077904 | tf_op jit(solution)/shard_map/all_gather | solution.py:329
  1167.8 15.4 %all-reduce.50 = f32[8,8]{1,0:T(8,128)S(1)} all-reduce(f32[8,8]{1,0:T(8,128)S(1)} %broadcast_in_dim.252), channel_id=4, replica_groups=mesh['dp'=4,'fsdp'=8] {'fsdp'}, use_global_device_ids=true, to_apply=%region_69.72.clone | all-reduce | flops 64 | bytes 512
  1188.1 22.3 %reduce-scatter.7.cloned.1.call-done = f32[48,29]{1,0:T(8,128)} async-done(((f32[384,29]{1,0:T(8,128)}), f32[48,29]{1,0:T(8,128)}) %reduce-scatter.7.cloned.1.call-update) | async-done | bytes 5584
  1211.2 12.7 all-reduce.53
  1236.4 114.6 %all-gather.9.cloned.1.call-done = f32[16,384,384]{2,1,0:T(8,128)} async-done(((f32[2,384,384]{2,1,0:T(8,128)}), f32[16,384,384]{2,1,0:T(8,128)}) %all-gather.9.cloned.1.call-update) | async-done | bytes 9437200 | tf_op jit(solution)/shard_map/all_gather | solution.py:343
  (441 shorter events, 323.4 us)
Async XLA Ops:
  7.2 1146.5 %copy-start = (f32[2,384,384]{2,1,0:T(8,128)S(1)}, f32[2,384,384]{2,1,0:T(8,128)}, u32[]{:S(2)}) copy-start(f32[2,384,384]{2,1,0:T(8,128)} %param.25) | copy-start | bytes 3538948
  7.2 70.3 %all-gather.5.cloned.1.call-start = ((), (), s32[]{:S(2)}) async-start(), calls=%async_computation.2 | async-start | bytes 3981312 | tf_op jit(solution)/shard_map/all_gather | solution.py:147
  9.4 989.5 %reduce-scatter.5.cloned.1.call-start = ((), (), s32[]{:S(2)}) async-start(), calls=%async_computation.3 | async-start | bytes 10616832 | tf_op jit(solution)/shard_map/reduce_scatter | solution.py:312
  41.3 302.0 %copy-start.52 = (pred[1856]{0:T(1024)(128)(4,1)}, pred[1856]{0:T(1024)(128)(4,1)S(1)}, u32[]{:S(2)}) copy-start(pred[1856]{0:T(1024)(128)(4,1)S(1)} %get-tuple-element.198) | copy-start | bytes 5572
  41.3 293.0 %copy-start.43 = (s32[2048]{0:T(1024)}, s32[2048]{0:T(1024)S(1)}, u32[]{:S(2)}) copy-start(s32[2048]{0:T(1024)S(1)} %pad_clamp_fusion.1) | copy-start | bytes 24580
  42.0 178.4 %copy-start.73 = (f32[384]{0:T(512)}, f32[384]{0:T(512)S(1)}, u32[]{:S(2)}) copy-start(f32[384]{0:T(512)S(1)} %get-tuple-element.157) | copy-start | bytes 4612
  42.0 183.3 %copy-start.79 = (f32[384]{0:T(512)}, f32[384]{0:T(512)S(1)}, u32[]{:S(2)}) copy-start(f32[384]{0:T(512)S(1)} %get-tuple-element.154) | copy-start | bytes 4612
  346.9 52.2 %copy-start.11 = (f32[1856,384]{1,0:T(8,128)}, f32[1856,384]{1,0:T(8,128)S(1)}, u32[]{:S(2)}) copy-start(f32[1856,384]{1,0:T(8,128)S(1)} %get-tuple-element.193) | copy-start | bytes 8552452
  480.0 62.8 %copy-start.75 = (f32[384]{0:T(512)}, f32[384]{0:T(512)S(1)}, u32[]{:S(2)}) copy-start(f32[384]{0:T(512)S(1)} %get-tuple-element.119) | copy-start | bytes 4612
  480.0 62.8 %copy-start.77 = (f32[384]{0:T(512)}, f32[384]{0:T(512)S(1)}, u32[]{:S(2)}) copy-start(f32[384]{0:T(512)S(1)} %get-tuple-element.120) | copy-start | bytes 4612
  834.8 205.4 %copy-start.119 = (s32[12]{0:T(128)S(1)}, s32[12]{0:T(128)}, u32[]{:S(2)}) copy-start(s32[12]{0:T(128)} %param.29) | copy-start | bytes 148
  834.8 207.5 %copy-start.78 = (f32[384]{0:T(512)S(1)}, f32[384]{0:T(512)}, u32[]{:S(2)}) copy-start(f32[384]{0:T(512)} %copy-done.77) | copy-start | bytes 4612
  834.8 208.1 %copy-start.76 = (f32[384]{0:T(512)S(1)}, f32[384]{0:T(512)}, u32[]{:S(2)}) copy-start(f32[384]{0:T(512)} %copy-done.75) | copy-start | bytes 4612
  834.8 208.7 %copy-start.105 = (f32[384]{0:T(512)S(1)}, f32[384]{0:T(512)}, u32[]{:S(2)}) copy-start(f32[384]{0:T(512)} %get-tuple-element.97) | copy-start | bytes 4612
  834.8 208.7 %copy-start.104 = (f32[384]{0:T(512)S(1)}, f32[384]{0:T(512)}, u32[]{:S(2)}) copy-start(f32[384]{0:T(512)} %get-tuple-element.105) | copy-start | bytes 4612
  834.8 208.7 %copy-start.103 = (f32[384]{0:T(512)S(1)}, f32[384]{0:T(512)}, u32[]{:S(2)}) copy-start(f32[384]{0:T(512)} %get-tuple-element.104) | copy-start | bytes 4612
  834.8 208.7 %copy-start.102 = (f32[384]{0:T(512)S(1)}, f32[384]{0:T(512)}, u32[]{:S(2)}) copy-start(f32[384]{0:T(512)} %get-tuple-element.103) | copy-start | bytes 4612
  834.8 208.7 %copy-start.101 = (f32[384]{0:T(512)S(1)}, f32[384]{0:T(512)}, u32[]{:S(2)}) copy-start(f32[384]{0:T(512)} %get-tuple-element.102) | copy-start | bytes 4612
  834.8 208.7 %copy-start.100 = (f32[384]{0:T(512)S(1)}, f32[384]{0:T(512)}, u32[]{:S(2)}) copy-start(f32[384]{0:T(512)} %get-tuple-element.101) | copy-start | bytes 4612
  834.8 208.7 %copy-start.99 = (f32[384]{0:T(512)S(1)}, f32[384]{0:T(512)}, u32[]{:S(2)}) copy-start(f32[384]{0:T(512)} %get-tuple-element.100) | copy-start | bytes 4612
  834.8 208.7 %copy-start.98 = (f32[384]{0:T(512)S(1)}, f32[384]{0:T(512)}, u32[]{:S(2)}) copy-start(f32[384]{0:T(512)} %get-tuple-element.99) | copy-start | bytes 4612
  834.8 208.8 %copy-start.97 = (f32[384]{0:T(512)S(1)}, f32[384]{0:T(512)}, u32[]{:S(2)}) copy-start(f32[384]{0:T(512)} %get-tuple-element.98) | copy-start | bytes 4612
  834.8 208.8 %copy-start.96 = (f32[384]{0:T(512)S(1)}, f32[384]{0:T(512)}, u32[]{:S(2)}) copy-start(f32[384]{0:T(512)} %get-tuple-element.106) | copy-start | bytes 4612
  834.9 208.8 %copy-start.95 = (f32[384]{0:T(512)S(1)}, f32[384]{0:T(512)}, u32[]{:S(2)}) copy-start(f32[384]{0:T(512)} %get-tuple-element.114) | copy-start | bytes 4612
  834.9 208.8 %copy-start.94 = (f32[384]{0:T(512)S(1)}, f32[384]{0:T(512)}, u32[]{:S(2)}) copy-start(f32[384]{0:T(512)} %get-tuple-element.113) | copy-start | bytes 4612
  834.9 208.8 %copy-start.93 = (f32[384]{0:T(512)S(1)}, f32[384]{0:T(512)}, u32[]{:S(2)}) copy-start(f32[384]{0:T(512)} %get-tuple-element.112) | copy-start | bytes 4612
  834.9 208.8 %copy-start.92 = (f32[384]{0:T(512)S(1)}, f32[384]{0:T(512)}, u32[]{:S(2)}) copy-start(f32[384]{0:T(512)} %get-tuple-element.111) | copy-start | bytes 4612
  834.9 208.8 %copy-start.91 = (f32[384]{0:T(512)S(1)}, f32[384]{0:T(512)}, u32[]{:S(2)}) copy-start(f32[384]{0:T(512)} %get-tuple-element.110) | copy-start | bytes 4612
  834.9 208.8 %copy-start.90 = (f32[384]{0:T(512)S(1)}, f32[384]{0:T(512)}, u32[]{:S(2)}) copy-start(f32[384]{0:T(512)} %get-tuple-element.109) | copy-start | bytes 4612
  834.9 208.8 %copy-start.89 = (f32[384]{0:T(512)S(1)}, f32[384]{0:T(512)}, u32[]{:S(2)}) copy-start(f32[384]{0:T(512)} %get-tuple-element.108) | copy-start | bytes 4612
  834.9 208.9 %copy-start.88 = (f32[384]{0:T(512)S(1)}, f32[384]{0:T(512)}, u32[]{:S(2)}) copy-start(f32[384]{0:T(512)} %get-tuple-element.107) | copy-start | bytes 4612
  834.9 208.9 %copy-start.28 = (bf16[1856,384]{1,0:T(8,128)(2,1)S(1)}, bf16[1856,384]{1,0:T(8,128)(2,1)}, u32[]{:S(2)}) copy-start(bf16[1856,384]{1,0:T(8,128)(2,1)} %gather_fusion.11) | copy-start | bytes 4276228
  835.0 202.6 %all-reduce.56.cloned.1.call-start = ((), (), s32[]{:S(2)}) async-start(), calls=%async_computation.4 | async-start | bytes 2359296 | tf_op jit(solution)/shard_map/psum | solution.py:316
  998.9 149.9 %all-gather.7.cloned.1.call-start = ((), (), s32[]{:S(2)}) async-start(), calls=%async_computation.5 | async-start | bytes 7962624 | tf_op jit(solution)/shard_map/all_gather | solution.py:329
  1040.1 170.3 %reduce-scatter.7.cloned.1.call-start = ((), (), s32[]{:S(2)}) async-start(), calls=%async_computation.7 | async-start | bytes 221184
  1065.1 97.1 %copy-start.121 = (u32[32]{0:T(128)S(1)}, u32[32]{0:T(128)}, u32[]{:S(2)}) copy-start(u32[32]{0:T(128)} %constant.350) | copy-start | bytes 388
  1065.1 97.7 %copy-start.120 = (s32[12]{0:T(128)S(1)}, s32[12]{0:T(128)}, u32[]{:S(2)}) copy-start(s32[12]{0:T(128)} %param.29) | copy-start | bytes 148
  1065.1 285.9 %all-gather.9.cloned.1.call-start = ((), (), s32[]{:S(2)}) async-start(), calls=%async_computation.6 | async-start | bytes 10616832 | tf_op jit(solution)/shard_map/all_gather | solution.py:343
  1167.7 56.2 %copy-start.72 = (f32[8]{0:T(128)S(1)}, f32[8]{0:T(128)}, u32[]{:S(2)}) copy-start(f32[8]{0:T(128)} %param.21) | copy-start | bytes 100
  1167.7 56.2 %copy-start.117 = (f32[8]{0:T(128)S(1)}, f32[8]{0:T(128)}, u32[]{:S(2)}) copy-start(f32[8]{0:T(128)} %param.28) | copy-start | bytes 100
  1167.7 56.7 %copy-start.63 = (f32[29,48]{1,0:T(8,128)S(1)}, f32[29,48]{1,0:T(8,128)}, u32[]{:S(2)}) copy-start(f32[29,48]{1,0:T(8,128)} %param.20) | copy-start | bytes 16708
  1167.7 56.7 %copy-start.82 = (f32[29,48]{1,0:T(8,128)S(1)}, f32[29,48]{1,0:T(8,128)}, u32[]{:S(2)}) copy-start(f32[29,48]{1,0:T(8,128)} %param.27) | copy-start | bytes 16708
  1167.7 57.4 %copy-start.85 = (pred[2]{0:T(512)(128)(4,1)S(1)}, pred[2]{0:T(512)(128)(4,1)}, u32[]{:S(2)}) copy-start(pred[2]{0:T(512)(128)(4,1)} %get-tuple-element.179) | copy-start | bytes 10
  1167.7 57.4 %copy-start.106 = (f32[2]{0:T(128)S(1)}, f32[2]{0:T(128)}, u32[]{:S(2)}) copy-start(f32[2]{0:T(128)} %dynamic_slice.10) | copy-start | bytes 28
  1223.9 130.1 %copy-start.83 = (f32[29,48]{1,0:T(8,128)}, f32[29,48]{1,0:T(8,128)S(1)}, u32[]{:S(2)}) copy-start(f32[29,48]{1,0:T(8,128)S(1)} %get-tuple-element.168) | copy-start | bytes 16708
  1223.9 130.1 %copy-start.118 = (f32[8]{0:T(128)}, f32[8]{0:T(128)S(1)}, u32[]{:S(2)}) copy-start(f32[8]{0:T(128)S(1)} %get-tuple-element.169) | copy-start | bytes 100
  1225.1 128.9 %copy-start.29 = (f32[12,48,384]{2,1,0:T(8,128)S(1)}, f32[12,48,384]{2,1,0:T(8,128)}, u32[]{:S(2)}) copy-start(f32[12,48,384]{2,1,0:T(8,128)} %param.19) | copy-start | bytes 2654212
  1225.1 128.9 %copy-start.116 = (pred[12]{0:T(512)(128)(4,1)S(1)}, pred[12]{0:T(512)(128)(4,1)}, u32[]{:S(2)}) copy-start(pred[12]{0:T(512)(128)(4,1)} %compare_and_fusion.2) | copy-start | bytes 40
  (84 other events, 927.9 us)
Sparse Core Ops, SparseCore 0:
  10.9 66.6 all-gather.4
  835.1 163.7 reduce-scatter.4
  1001.3 36.2 all-reduce.55
  1040.2 108.5 all-gather.6
  1152.5 57.7 reduce-scatter.6
  1212.4 138.5 all-gather.8
where the time goes:
time: 1380 us; the launch traced here: 1360 us
  waiting for transfers between devices  451 us (33%)
  local copies, waits for them, and re-layouts  351 us (25%)
  other arithmetic  242 us (18%)
  matrix products  169 us (12%)
  blocking collectives  134 us (10%)
  between operations  16.4 us (1%)
    reduce_scatter x1, waiting for transfers between devices, shards(): lax.psum_scatter(block_grad, 'fsdp', scatter_dimension=1, tiled=True)  164 us
    all_gather x1, waiting for transfers between devices, shards(): every_update = lax.all_gather(conditioned, 'fsdp', axis=0, tiled=True)  115 us
    gather x12, local copies, waits for them, and re-layouts, regroup_into_grid(): return jnp.take(padded, incoming_tensor, axis=0)  102 us
    all_gather x1, waiting for transfers between devices, shards(): whole_grad = lax.all_gather(portion_derivative, 'fsdp', axis=1, tiled=True)  83.4 us
    reshape x8, local copies, waits for them, and re-layouts, into_rows(): flattened = grid_cells.reshape(-1, grid_cells.shape[-1])  70.2 us
    reduce_sum x2, other arithmetic, depthwise(): padded[:, row_shift:row_shift + grid_side, column_shift:column_shift + gr...  52.8 us
    gather x6, local copies, waits for them, and re-layouts, into_rows(): return jnp.take(padded, target, axis=0)  51.5 us
    psum x1, blocking collectives, shards(): beta_total, gamma_total = lax.psum((beta_part, gamma_part), ('dp', 'fsdp'))  40.5 us
  transfers between devices with their start and end apart: 6, of which 6 were waited for; matrix products, arithmetic and copies ran while one was open for 5% of the time, Pallas kernels for 0%

commit v1 on v0

v1 whole, which is shorter than its diff:
```python
import functools

import jax
import jax.numpy as jnp
from jax import lax
from jax.experimental import pallas as pl
from jax.experimental.pallas import tpu as pltpu
from jax.sharding import PartitionSpec as P

HEAD_NUMBER = 8
HDIM = 48
HEAD_PAD = 64
LANES = 128
HEAD_PAIRS = HEAD_NUMBER // 2
PAD_WIDTH = HEAD_NUMBER * HEAD_PAD
HALF_WIDTH = PAD_WIDTH // 2
LEAD = 16
TAIL = 32
SMALL_WINDOW = 48
LARGE_WINDOW = 208
VMEM_LIMIT = 58 * 2**20

norm_epsilon = 1e-06
batch_epsilon = 1e-05
attention_epsilon = 1e-06
covariance_forgetting = 0.5
weight_rate = 0.5
vector_rate = 0.1
sharpness_step_size = 2.0
energy_epsilon = 1e-08

F32 = jnp.float32
BF16 = jnp.bfloat16
VMEM_SPEC = pl.BlockSpec(memory_space=pltpu.VMEM)
ANY_SPEC = pl.BlockSpec(memory_space=pl.ANY)
SMEM_SPEC = pl.BlockSpec(memory_space=pltpu.SMEM)


def dot(left, right):
    return lax.dot_general(left, right, (((1,), (0,)), ((), ())), preferred_element_type=F32)


def dot_rows(left, right):
    return lax.dot_general(left, right, (((0,), (0,)), ((), ())), preferred_element_type=F32)


def dot_lanes(left, right):
    return lax.dot_general(left, right, (((1,), (1,)), ((), ())), preferred_element_type=F32)


def split(values):
    high = values.astype(BF16)
    return high, (values - high.astype(F32)).astype(BF16)


def dot_split(product, left, right):
    return (
        product(left[0], right[0]) + product(left[0], right[1]) + product(left[1], right[0])
    )


def fold(values):
    total = values[0:8]
    for first in range(8, values.shape[0], 8):
        total = total + values[first : first + 8]
    return total


def gelu_parts(values):
    magnitude = jnp.abs(values) * 0.7071067811865476
    base = 1.0 + 0.3275911 * magnitude
    guess = pl.reciprocal(base, approx=True)
    slot = guess * (2.0 - base * guess)
    series = slot * (
        0.127414796
        + slot
        * (-0.142248368 + slot * (0.7107068705 + slot * (-0.7265760135 + slot * 0.5307027145)))
    )
    bell = jnp.exp(-0.5 * values * values)
    lower = series * bell
    return jnp.where(values >= 0, 1.0 - lower, lower), bell


def gelu_slope(values, share, bell):
    return share + values * bell * 0.3989422804014327


def head_map(dtype):
    feature = lax.broadcasted_iota(jnp.int32, (HEAD_NUMBER * HDIM, PAD_WIDTH), 0)
    lane = lax.broadcasted_iota(jnp.int32, (HEAD_NUMBER * HDIM, PAD_WIDTH), 1)
    inner = lane & (HEAD_PAD - 1)
    hit = (inner < HDIM) & ((lane >> 6) * HDIM + inner == feature)
    return hit.astype(F32).astype(dtype)


def centered(values):
    center = jnp.sum(values, axis=-1, keepdims=True) * (1.0 / values.shape[-1])
    shifted = values - center
    spread = jnp.sum(shifted * shifted, axis=-1, keepdims=True) * (1.0 / values.shape[-1])
    scale = lax.rsqrt(spread + norm_epsilon)
    return shifted * scale, scale


def norm_back(grad, unit, scale):
    size = 1.0 / grad.shape[-1]
    middle = jnp.sum(grad, axis=-1, keepdims=True) * size
    slope = jnp.sum(grad * unit, axis=-1, keepdims=True) * size
    return scale * (grad - middle - unit * slope)


def tile_rows(count):
    for parts in range(4, count // 16 + 1):
        if count % (16 * parts) == 0:
            return count // parts
    return count


def live_total(sides_ref):
    return lax.fori_loop(
        0, sides_ref.shape[0], lambda c, t: t + sides_ref[c] * sides_ref[c], jnp.int32(0)
    )


def row_mask(first, rows, width, limit):
    return lax.broadcasted_iota(jnp.int32, (rows, width), 0) + first < limit


def for_groups(sides_ref, step, carry):
    def crop_body(crop, state):
        start, carry = state
        side = sides_ref[crop]
        cells = side * side
        inverse = 1.0 / jnp.full((8, LANES), side, jnp.int32).astype(F32)
        lines = lax.broadcasted_iota(jnp.int32, (8, LANES), 0)

        def group_body(group, carry):
            for part in range(2):
                row = pl.multiple_of((group * 2 + part) * 8, 8)
                place = lines + (row - start)
                line = ((place.astype(F32) + 0.5) * inverse).astype(jnp.int32)
                column = place - line * side
                inside = (place >= 0) & (place < cells)
                masks = (
                    inside,
                    column >= 1,
                    column < side - 1,
                    place >= side,
                    place < cells - side,
                )
                carry = step(row, side, masks, carry)
            return carry

        carry = lax.fori_loop(start // 16, (start + cells + 15) // 16, group_body, carry)
        return start + cells, carry

    return lax.fori_loop(0, sides_ref.shape[0], crop_body, (jnp.int32(0), carry))[1]


def conv_forward(source, chunk, row, side, masks, taps):
    inside, left_ok, right_ok, up_ok, down_ok = masks
    total = None
    for shift in (-1, 0, 1):
        base = LEAD + row + shift * side
        middle = source[chunk, pl.ds(base, 8), :]
        left = jnp.where(left_ok, source[chunk, pl.ds(base - 1, 8), :], 0.0)
        right = jnp.where(right_ok, source[chunk, pl.ds(base + 1, 8), :], 0.0)
        first = 3 * (shift + 1)
        value = taps[first] * left + taps[first + 1] * middle + taps[first + 2] * right
        if shift == -1:
            value = jnp.where(up_ok, value, 0.0)
        if shift == 1:
            value = jnp.where(down_ok, value, 0.0)
        total = value if total is None else total + value
    return total


def conv_backward(source, chunk, row, side, masks, taps, own, tap_sums):
    inside, left_ok, right_ok, up_ok, down_ok = masks
    total = None
    tap_sums = list(tap_sums)
    for shift in (-1, 0, 1):
        base = LEAD + row + shift * side
        row_ok = {-1: up_ok, 0: None, 1: down_ok}[shift]
        for sway in (-1, 0, 1):
            column_ok = {-1: left_ok, 0: None, 1: right_ok}[sway]
            value = source[chunk, pl.ds(base + sway, 8), :]
            keep = inside
            if row_ok is not None:
                keep = keep & row_ok
            if column_ok is not None:
                keep = keep & column_ok
            value = jnp.where(keep, value, 0.0)
            index = 3 * (1 - shift) + (1 - sway)
            term = taps[index] * value
            total = term if total is None else total + term
            tap_sums[index] = tap_sums[index] + own * value
    return total, tuple(tap_sums)


def chunk_lanes(chunk):
    return slice(chunk * LANES, (chunk + 1) * LANES)


def tap_vectors(table_ref, first, chunk):
    return [
        jnp.broadcast_to(table_ref[first + k : first + k + 1, chunk_lanes(chunk)], (8, LANES))
        for k in range(9)
    ]


def for_crops(sides_ref, row_count, step):
    def crop_body(crop, start):
        side = sides_ref[crop]
        cells = side * side
        for window, fits in ((SMALL_WINDOW, side <= 6), (LARGE_WINDOW, side > 6)):

            @pl.when(fits)
            def _():
                first = pl.multiple_of(
                    jnp.minimum(start // 8, (row_count - window) // 8) * 8, 8
                )
                place = lax.broadcasted_iota(jnp.int32, (window, HALF_WIDTH), 0) + (first - start)
                step(crop, pl.ds(first, window), (place >= 0) & (place < cells))

        return start + cells

    lax.fori_loop(0, sides_ref.shape[0], crop_body, jnp.int32(0))


def pair_lanes():
    return lax.broadcasted_iota(jnp.int32, (HDIM, LANES), 1) < HEAD_PAD


def pair_part(block, pair):
    first = pair * LANES
    lanes = slice(first, first + LANES)
    return jnp.where(
        pair_lanes(),
        block[first : first + HDIM, lanes],
        block[first + HEAD_PAD : first + HEAD_PAD + HDIM, lanes],
    )


def spread_pair(target, half, pair, values):
    first = pair * LANES
    lanes = slice(first, first + LANES)
    parts = split(values)
    for index in range(2):
        value = parts[index].astype(F32)
        target[half, index, first : first + HDIM, lanes] = jnp.where(
            pair_lanes(), value, 0.0
        ).astype(BF16)
        target[half, index, first + HEAD_PAD : first + HEAD_PAD + HDIM, lanes] = jnp.where(
            pair_lanes(), 0.0, value
        ).astype(BF16)


def pair_sharpness(sharp_ref, pair):
    lane = lax.broadcasted_iota(jnp.int32, (1, LANES), 1)
    return jnp.where(lane < HEAD_PAD, sharp_ref[2 * pair], sharp_ref[2 * pair + 1])


def units(values):
    scale = lax.rsqrt(jnp.sum(values * values, axis=0, keepdims=True) + attention_epsilon)
    return values * scale, scale


def mixing_forward_kernel(
    sides_ref,
    sharp_ref,
    input_ref,
    weight_ref,
    table_ref,
    x1_ref,
    qkv_ref,
    mixed_ref,
    scores_ref,
    attention_ref,
    u_ref,
    e_ref,
    sums_ref,
    head_weights,
    out_weight,
    first_low,
    mixed,
    attention_out,
    conv_in,
    spread,
):
    row_count, width = input_ref.shape
    chunks = width // LANES
    tile = tile_rows(row_count)
    total_live = live_total(sides_ref)
    mapping = head_map(BF16)
    for part in range(3):
        head_weights[:, part * PAD_WIDTH : (part + 1) * PAD_WIDTH] = dot(
            weight_ref[part], mapping
        ).astype(BF16)
    spread[...] = jnp.zeros_like(spread)

    def first_norm(step, _):
        rows = pl.ds(pl.multiple_of(step * 32, 32), 32)
        unit, _ = centered(input_ref[rows, :].astype(F32))
        first_low[rows, :] = (unit * table_ref[0:1, :] + table_ref[1:2, :]).astype(BF16)
        mixed[rows, :] = jnp.zeros((32, PAD_WIDTH), F32)
        return 0

    lax.fori_loop(0, row_count // 32, first_norm, 0)

    @pl.loop(0, row_count // tile)
    def _(step):
        rows = pl.ds(pl.multiple_of(step * tile, 16), tile)
        for part in range(3):
            lanes = slice(part * PAD_WIDTH, (part + 1) * PAD_WIDTH)
            qkv_ref[rows, lanes] = dot(first_low[rows, :], head_weights[:, lanes])

    def crop_step(crop, rows, keep):
        for half in range(2):
            lanes = [
                slice(part * PAD_WIDTH + half * HALF_WIDTH, part * PAD_WIDTH + (half + 1) * HALF_WIDTH)
                for part in range(3)
            ]
            query = units(jnp.where(keep, qkv_ref[rows, lanes[0]], 0.0))[0]
            key = units(jnp.where(keep, qkv_ref[rows, lanes[1]], 0.0))[0]
            block = dot_split(dot_rows, split(key), split(query))
            for pair in range(2):
                scores = pair_part(block, pair)
                scores_ref[crop, 2 * half + pair] = scores
                scores = scores * pair_sharpness(sharp_ref, 2 * half + pair)
                scores = jnp.exp(scores - jnp.max(scores, axis=0, keepdims=True))
                shares = scores / jnp.sum(scores, axis=0, keepdims=True)
                attention_ref[crop, 2 * half + pair] = shares
                spread_pair(spread, half, pair, shares)
            result = dot_split(
                dot, split(qkv_ref[rows, lanes[2]]), (spread[half, 0], spread[half, 1])
            )
            mixed[rows, lanes[0]] = jnp.where(keep, result, mixed[rows, lanes[0]])

    for_crops(sides_ref, row_count, crop_step)

    out_weight[...] = dot_rows(mapping, weight_ref[3]).astype(BF16)

    @pl.loop(0, row_count // tile)
    def _(step):
        rows = pl.ds(pl.multiple_of(step * tile, 16), tile)
        low = mixed[rows, :].astype(BF16)
        mixed_ref[rows, :] = low
        attention_out[rows, :] = dot(low, out_weight[...])

    def second_norm(step, _):
        first = pl.multiple_of(step * 32, 32)
        rows = pl.ds(first, 32)
        value = input_ref[rows, :].astype(F32) + table_ref[2:3, :] * attention_out[rows, :]
        x1_ref[rows, :] = value
        unit, _ = centered(value)
        value = unit * table_ref[3:4, :] + table_ref[4:5, :]
        for chunk in range(chunks):
            conv_in[chunk, pl.ds(LEAD + first, 32), :] = value[:, chunk_lanes(chunk)]
            u_ref[chunk, rows, :] = jnp.zeros((32, LANES), F32)
            e_ref[chunk, rows, :] = jnp.zeros((32, LANES), F32)
        return 0

    lax.fori_loop(0, row_count // 32, second_norm, 0)

    zero = jnp.zeros((8, LANES), F32)
    sums_ref[...] = zero
    for chunk in range(chunks):
        taps = tap_vectors(table_ref, 11, chunk)

        def conv_step(row, side, masks, carry, chunk=chunk, taps=taps):
            value = conv_forward(conv_in, chunk, row, side, masks, taps)
            share, _ = gelu_parts(value)
            active = value * share
            rows = pl.ds(row, 8)
            u_ref[chunk, rows, :] = jnp.where(masks[0], value, u_ref[chunk, rows, :])
            e_ref[chunk, rows, :] = jnp.where(masks[0], active, e_ref[chunk, rows, :])
            active = jnp.where(masks[0], active, 0.0)
            return carry[0] + active, carry[1] + active * active

        plain, square = for_groups(sides_ref, conv_step, (zero, zero))
        sums_ref[chunk : chunk + 1, :] = jnp.sum(plain, axis=0, keepdims=True)
        sums_ref[chunks + chunk : chunks + chunk + 1, :] = jnp.sum(square, axis=0, keepdims=True)
    sums_ref[2 * chunks : 2 * chunks + 1, :] = jnp.full((1, LANES), total_live, jnp.int32).astype(F32)


def mixing_forward(sides, sharpness, inputs, weights, table):
    row_count, width = inputs.shape
    crops = sides.shape[0]
    chunks = width // LANES
    shape = jax.ShapeDtypeStruct
    return pl.pallas_call(
        mixing_forward_kernel,
        out_shape=(
            shape((row_count, width), F32),
            shape((row_count, 3 * PAD_WIDTH), F32),
            shape((row_count, PAD_WIDTH), BF16),
            shape((crops, HEAD_PAIRS, HDIM, LANES), F32),
            shape((crops, HEAD_PAIRS, HDIM, LANES), F32),
            shape((chunks, row_count, LANES), F32),
            shape((chunks, row_count, LANES), F32),
            shape((8, LANES), F32),
        ),
        in_specs=[SMEM_SPEC, SMEM_SPEC, VMEM_SPEC, VMEM_SPEC, VMEM_SPEC],
        out_specs=(VMEM_SPEC,) * 8,
        scratch_shapes=[
            pltpu.VMEM((width, 3 * PAD_WIDTH), BF16),
            pltpu.VMEM((PAD_WIDTH, width), BF16),
            pltpu.VMEM((row_count, width), BF16),
            pltpu.VMEM((row_count, PAD_WIDTH), F32),
            pltpu.VMEM((row_count, width), F32),
            pltpu.VMEM((chunks, LEAD + row_count + TAIL, LANES), F32),
            pltpu.VMEM((2, 2, HALF_WIDTH, HALF_WIDTH), BF16),
        ],
        compiler_params=pltpu.CompilerParams(vmem_limit_bytes=VMEM_LIMIT),
        name="mixing_forward",
    )(sides, sharpness, inputs, weights, table)


def batch_vectors(bn_ref, chunk, chunks):
    count = bn_ref[2 * chunks : 2 * chunks + 1, :]
    mean = bn_ref[chunk : chunk + 1, :] / count
    scale = lax.rsqrt(bn_ref[chunks + chunk : chunks + chunk + 1, :] / count - mean * mean + batch_epsilon)
    return mean, scale


def feed_kernel(
    sides_ref,
    x1_ref,
    e_ref,
    bn_ref,
    weight_ref,
    table_ref,
    adjoint_ref,
    out_ref,
    dx2_ref,
    dn_ref,
    up_grad_ref,
    down_grad_ref,
    grads_ref,
    n_ref,
    z_ref,
    dw_ref,
    x2,
    unit,
    spread,
    third_low,
    pre,
    hidden_low,
    feed,
    feed_grad,
    pre_grad,
    grads,
):
    row_count, width = x1_ref.shape
    chunks = width // LANES
    expand = weight_ref.shape[0] // 2
    tile = tile_rows(row_count)
    total_live = live_total(sides_ref)
    batch = [batch_vectors(bn_ref, chunk, chunks) for chunk in range(chunks)]
    zero = jnp.zeros((8, LANES), F32)

    def normalize(step, _):
        first = pl.multiple_of(step * 32, 32)
        rows = pl.ds(first, 32)
        live = row_mask(first, 32, LANES, total_live)
        for chunk in range(chunks):
            lanes = chunk_lanes(chunk)
            mean, scale = batch[chunk]
            value = (e_ref[chunk, rows, :] - mean) * scale
            value = value * table_ref[5:6, lanes] + table_ref[6:7, lanes]
            n_ref[chunk, pl.ds(LEAD + first, 32), :] = jnp.where(live, value, 0.0)
            z_ref[chunk, rows, :] = jnp.zeros((32, LANES), F32)
            dn_ref[chunk, rows, :] = jnp.zeros((32, LANES), F32)
        return 0

    lax.fori_loop(0, row_count // 32, normalize, 0)

    for chunk in range(chunks):
        taps = tap_vectors(table_ref, 20, chunk)

        def conv_step(row, side, masks, carry, chunk=chunk, taps=taps):
            value = conv_forward(n_ref, chunk, row, side, masks, taps)
            rows = pl.ds(row, 8)
            z_ref[chunk, rows, :] = jnp.where(masks[0], value, z_ref[chunk, rows, :])
            return carry

        for_groups(sides_ref, conv_step, 0)

    up_grad_ref[...] = jnp.zeros_like(up_grad_ref)
    down_grad_ref[...] = jnp.zeros_like(down_grad_ref)
    grads[...] = jnp.zeros_like(grads)

    def z_rows(rows):
        return jnp.concatenate([z_ref[chunk, rows, :] for chunk in range(chunks)], axis=1)

    @pl.loop(0, row_count // tile)
    def _(step):
        base = pl.multiple_of(step * tile, 16)

        def before(sub, _):
            inner = pl.multiple_of(sub * 16, 16)
            near, rows = pl.ds(inner, 16), pl.ds(base + inner, 16)
            value = x1_ref[rows, :] + table_ref[7:8, :] * z_rows(rows)
            x2[near, :] = value
            value, scale = centered(value)
            unit[near, :] = value
            spread[near, :] = jnp.broadcast_to(scale, (16, LANES))
            third_low[near, :] = (value * table_ref[8:9, :] + table_ref[9:10, :]).astype(BF16)
            return 0

        lax.fori_loop(0, tile // 16, before, 0)
        for part in range(expand):
            lanes = slice(part * width, (part + 1) * width)
            pre[:, lanes] = dot(third_low[...], weight_ref[part])

        def activate(sub, _):
            near = pl.ds(pl.multiple_of(sub * 16, 16), 16)
            for part in range(expand):
                lanes = slice(part * width, (part + 1) * width)
                value = pre[near, lanes]
                share, bell = gelu_parts(value)
                hidden_low[near, lanes] = (value * share).astype(BF16)
                pre[near, lanes] = gelu_slope(value, share, bell)
            return 0

        lax.fori_loop(0, tile // 16, activate, 0)
        total = None
        for part in range(expand):
            lanes = slice(part * width, (part + 1) * width)
            term = dot(hidden_low[:, lanes], weight_ref[expand + part])
            total = term if total is None else total + term
        feed[...] = total

        def output(sub, carry):
            inner = pl.multiple_of(sub * 16, 16)
            near, rows = pl.ds(inner, 16), pl.ds(base + inner, 16)
            live = row_mask(base + inner, 16, width, total_live)
            value = x2[near, :] + table_ref[10:11, :] * feed[near, :]
            out_ref[rows, :] = jnp.where(live, value, 0.0).astype(BF16)
            entry = jnp.where(live, adjoint_ref[rows, :].astype(F32), 0.0)
            feed_grad[near, :] = (entry * table_ref[10:11, :]).astype(BF16)
            return carry + fold(entry * feed[near, :])

        grads[0] += lax.fori_loop(0, tile // 16, output, jnp.zeros((8, width), F32))
        for part in range(expand):
            lanes = slice(part * width, (part + 1) * width)
            hidden_grad = dot_lanes(feed_grad[...], weight_ref[expand + part])
            pre_grad[:, lanes] = (hidden_grad * pre[:, lanes]).astype(BF16)
        for part in range(expand):
            lanes = slice(part * width, (part + 1) * width)
            down_grad_ref[part] += dot_rows(hidden_low[:, lanes], feed_grad[...])
            up_grad_ref[part] += dot_rows(third_low[...], pre_grad[:, lanes])
        total = None
        for part in range(expand):
            lanes = slice(part * width, (part + 1) * width)
            term = dot_lanes(pre_grad[:, lanes], weight_ref[part])
            total = term if total is None else total + term
        feed[...] = total

        def after(sub, carry):
            inner = pl.multiple_of(sub * 16, 16)
            near, rows = pl.ds(inner, 16), pl.ds(base + inner, 16)
            live = row_mask(base + inner, 16, width, total_live)
            entry = jnp.where(live, adjoint_ref[rows, :].astype(F32), 0.0)
            grad = feed[near, :]
            value = unit[near, :]
            total = entry + norm_back(grad * table_ref[8:9, :], value, spread[near, 0:1])
            dx2_ref[rows, :] = total
            scaled = total * table_ref[7:8, :]
            for chunk in range(chunks):
                dw_ref[chunk, pl.ds(LEAD + base + inner, 16), :] = scaled[:, chunk_lanes(chunk)]
            return (
                carry[0] + fold(total * z_rows(rows)),
                carry[1] + fold(grad * value),
                carry[2] + fold(grad),
            )

        wide = jnp.zeros((8, width), F32)
        sums = lax.fori_loop(0, tile // 16, after, (wide, wide, wide))
        for index in range(3):
            grads[1 + index] += sums[index]

    for index, source in enumerate((1, 2, 3, 0)):
        grads_ref[index : index + 1, :] = jnp.sum(grads[source], axis=0, keepdims=True)
    for chunk in range(chunks):
        taps = tap_vectors(table_ref, 20, chunk)
        mean, scale = batch[chunk]

        def back_step(row, side, masks, carry, chunk=chunk, taps=taps, mean=mean, scale=scale):
            own = jnp.where(masks[0], n_ref[chunk, pl.ds(LEAD + row, 8), :], 0.0)
            total, tap_sums = conv_backward(dw_ref, chunk, row, side, masks, taps, own, carry[0])
            rows = pl.ds(row, 8)
            dn_ref[chunk, rows, :] = jnp.where(masks[0], total, dn_ref[chunk, rows, :])
            total = jnp.where(masks[0], total, 0.0)
            standard = (e_ref[chunk, rows, :] - mean) * scale
            return tap_sums, carry[1] + total * standard, carry[2] + total

        tap_sums, gamma, beta = for_groups(sides_ref, back_step, ((zero,) * 9, zero, zero))
        lanes = chunk_lanes(chunk)
        for index, value in enumerate((*tap_sums, gamma, beta)):
            grads_ref[4 + index : 5 + index, lanes] = jnp.sum(value, axis=0, keepdims=True)


def feed_forward(sides, x1, e, batch_sums, weights, table, adjoint):
    row_count, width = x1.shape
    chunks = width // LANES
    expand = weights.shape[0] // 2
    tile = tile_rows(row_count)
    shape = jax.ShapeDtypeStruct
    return pl.pallas_call(
        feed_kernel,
        out_shape=(
            shape((row_count, width), BF16),
            shape((row_count, width), F32),
            shape((chunks, row_count, LANES), F32),
            shape((expand, width, width), F32),
            shape((expand, width, width), F32),
            shape((16, width), F32),
        ),
        in_specs=[SMEM_SPEC] + [VMEM_SPEC] * 6,
        out_specs=(VMEM_SPEC,) * 6,
        scratch_shapes=[
            pltpu.VMEM((chunks, LEAD + row_count + TAIL, LANES), F32),
            pltpu.VMEM((chunks, row_count, LANES), F32),
            pltpu.VMEM((chunks, LEAD + row_count + TAIL, LANES), F32),
            pltpu.VMEM((tile, width), F32),
            pltpu.VMEM((tile, width), F32),
            pltpu.VMEM((tile, LANES), F32),
            pltpu.VMEM((tile, width), BF16),
            pltpu.VMEM((tile, expand * width), F32),
            pltpu.VMEM((tile, expand * width), BF16),
            pltpu.VMEM((tile, width), F32),
            pltpu.VMEM((tile, width), BF16),
            pltpu.VMEM((tile, expand * width), BF16),
            pltpu.VMEM((4, 8, width), F32),
        ],
        compiler_params=pltpu.CompilerParams(vmem_limit_bytes=VMEM_LIMIT),
        name="feed_forward",
    )(sides, x1, e, batch_sums, weights, table, adjoint)


def mixing_backward_kernel(
    sides_ref,
    sharp_ref,
    input_ref,
    weight_ref,
    table_ref,
    x1_ref,
    qkv_ref,
    mixed_ref,
    scores_ref,
    attention_ref,
    u_hbm,
    bn_ref,
    dx2_ref,
    dn_hbm,
    back_ref,
    out_ref,
    head_grad_ref,
    out_grad_ref,
    grads_ref,
    sharp_grad_ref,
    head_weights,
    out_weight,
    pool,
    conv_grad,
    dx1,
    mixed_grad,
    low_rows,
    head_low,
    spread,
    out_sum,
    load_sems,
):
    row_count, width = input_ref.shape
    chunks = width // LANES
    u_ref, dn_ref = pool.at[0:chunks], pool.at[chunks : 2 * chunks]
    conv_in, attention_out = pool.at[2 * chunks : 3 * chunks], pool.at[3 * chunks : 4 * chunks]
    loads = [
        pltpu.make_async_copy(u_hbm, u_ref, load_sems.at[0]),
        pltpu.make_async_copy(dn_hbm, dn_ref, load_sems.at[1]),
    ]
    for load in loads:
        load.start()
    tile = tile_rows(row_count)
    total_live = live_total(sides_ref)
    batch = [batch_vectors(bn_ref, chunk, chunks) for chunk in range(chunks)]
    zero = jnp.zeros((8, LANES), F32)
    wide = jnp.zeros((8, width), F32)
    mapping = head_map(BF16)
    for part in range(3):
        head_weights[:, part * PAD_WIDTH : (part + 1) * PAD_WIDTH] = dot(
            weight_ref[part], mapping
        ).astype(BF16)
    out_weight[...] = dot_rows(mapping, weight_ref[3]).astype(BF16)
    spread[...] = jnp.zeros_like(spread)

    for load in loads:
        load.wait()

    def batch_back(step, _):
        first = pl.multiple_of(step * 32, 32)
        rows = pl.ds(first, 32)
        live = row_mask(first, 32, LANES, total_live)
        unit, _ = centered(x1_ref[rows, :])
        value = unit * table_ref[3:4, :] + table_ref[4:5, :]
        for chunk in range(chunks):
            lanes = chunk_lanes(chunk)
            mean, scale = batch[chunk]
            count = bn_ref[2 * chunks : 2 * chunks + 1, :]
            u = u_ref[chunk, rows, :]
            share, bell = gelu_parts(u)
            standard = (u * share - mean) * scale
            inner = (
                back_ref[chunk : chunk + 1, :]
                + standard * back_ref[chunks + chunk : chunks + chunk + 1, :]
            ) / count
            grad = scale * table_ref[5:6, lanes] * (dn_ref[chunk, rows, :] - inner)
            grad = grad * gelu_slope(u, share, bell)
            conv_grad[chunk, pl.ds(LEAD + first, 32), :] = jnp.where(live, grad, 0.0)
            conv_in[chunk, pl.ds(first, 32), :] = value[:, lanes]
        return 0

    lax.fori_loop(0, row_count // 32, batch_back, 0)

    for chunk in range(chunks):
        taps = tap_vectors(table_ref, 11, chunk)

        def back_step(row, side, masks, carry, chunk=chunk, taps=taps):
            rows = pl.ds(row, 8)
            held = conv_in[chunk, rows, :]
            own = jnp.where(masks[0], held, 0.0)
            total, tap_sums = conv_backward(conv_grad, chunk, row, side, masks, taps, own, carry)
            conv_in[chunk, rows, :] = jnp.where(masks[0], total, held)
            return tap_sums

        tap_sums = for_groups(sides_ref, back_step, (zero,) * 9)
        for index, value in enumerate(tap_sums):
            grads_ref[5 + index : 6 + index, chunk_lanes(chunk)] = jnp.sum(
                value, axis=0, keepdims=True
            )

    @pl.loop(0, row_count // tile)
    def _(step):
        rows = pl.ds(pl.multiple_of(step * tile, 16), tile)
        result = dot(mixed_ref[rows, :], out_weight[...])
        for chunk in range(chunks):
            attention_out[chunk, rows, :] = result[:, chunk_lanes(chunk)]

    def second_back(step, carry):
        first = pl.multiple_of(step * 16, 16)
        rows = pl.ds(first, 16)
        live = row_mask(first, 16, width, total_live)
        grad = jnp.concatenate([conv_in[chunk, rows, :] for chunk in range(chunks)], axis=1)
        grad = jnp.where(live, grad, 0.0)
        unit, scale = centered(x1_ref[rows, :])
        total = dx2_ref[rows, :] + norm_back(grad * table_ref[3:4, :], unit, scale)
        dx1[rows, :] = total
        low_rows[rows, :] = (total * table_ref[2:3, :]).astype(BF16)
        held = jnp.concatenate([attention_out[chunk, rows, :] for chunk in range(chunks)], axis=1)
        return (
            carry[0] + fold(total * held),
            carry[1] + fold(grad * unit),
            carry[2] + fold(grad),
        )

    sums = lax.fori_loop(0, row_count // 16, second_back, (wide, wide, wide))
    for index in range(3):
        grads_ref[2 + index : 3 + index, :] = jnp.sum(sums[index], axis=0, keepdims=True)

    out_sum[...] = jnp.zeros_like(out_sum)

    @pl.loop(0, row_count // tile)
    def _(step):
        rows = pl.ds(pl.multiple_of(step * tile, 16), tile)
        mixed_grad[rows, :] = dot_lanes(low_rows[rows, :], out_weight[...])
        out_sum[...] += dot_rows(mixed_ref[rows, :], low_rows[rows, :])

    pool[...] = jnp.zeros_like(pool)

    low = out_sum[...].astype(BF16)
    out_grad_ref[...] = dot(mapping, low).astype(BF16)
    sharp_grad_ref[...] = jnp.zeros_like(sharp_grad_ref)

    def crop_step(crop, rows, keep):
        for half in range(2):
            lanes = [
                slice(part * PAD_WIDTH + half * HALF_WIDTH, part * PAD_WIDTH + (half + 1) * HALF_WIDTH)
                for part in range(3)
            ]
            query, query_scale = units(jnp.where(keep, qkv_ref[rows, lanes[0]], 0.0))
            key, key_scale = units(jnp.where(keep, qkv_ref[rows, lanes[1]], 0.0))
            value = split(jnp.where(keep, qkv_ref[rows, lanes[2]], 0.0))
            grad = split(jnp.where(keep, mixed_grad[rows, lanes[0]], 0.0))
            block = dot_split(dot_rows, value, grad)
            query_sums = []
            for pair in range(2):
                index = 2 * half + pair
                shares = attention_ref[crop, index]
                scores = scores_ref[crop, index]
                part = pair_part(block, pair)
                part = shares * (part - jnp.sum(part * shares, axis=0, keepdims=True))
                spread_pair(spread, half, pair, shares)
                sharp_grad_ref[index : index + 1, :] += jnp.sum(part * scores, axis=0, keepdims=True)
                part = part * pair_sharpness(sharp_ref, index)
                query_sums.append(jnp.sum(part * scores, axis=0, keepdims=True))
                spread_pair(spread, 2 + half, pair, part)
            shares = (spread[half, 0], spread[half, 1])
            slopes = (spread[2 + half, 0], spread[2 + half, 1])
            value_grad = dot_split(dot_lanes, grad, shares)
            query_grad = dot_split(dot, split(key), slopes)
            query_grad = query_scale * (query_grad - query * jnp.concatenate(query_sums, axis=1))
            key_grad = dot_split(dot_lanes, split(query), slopes)
            key_grad = key_scale * (
                key_grad - key * jnp.sum(key_grad * key, axis=0, keepdims=True)
            )
            for part, result in enumerate((query_grad, key_grad, value_grad)):
                for side in range(HALF_WIDTH // LANES):
                    chunk = (part * PAD_WIDTH + half * HALF_WIDTH) // LANES + side
                    pool[chunk, rows, :] = jnp.where(
                        keep[:, 0:LANES], result[:, chunk_lanes(side)], pool[chunk, rows, :]
                    )

    for_crops(sides_ref, row_count, crop_step)

    def first_norm(step, _):
        rows = pl.ds(pl.multiple_of(step * 32, 32), 32)
        unit, _ = centered(input_ref[rows, :].astype(F32))
        low_rows[rows, :] = (unit * table_ref[0:1, :] + table_ref[1:2, :]).astype(BF16)
        return 0

    lax.fori_loop(0, row_count // 32, first_norm, 0)

    for part in range(3):
        lanes = slice(part * PAD_WIDTH, (part + 1) * PAD_WIDTH)
        out_sum[...] = jnp.zeros_like(out_sum)

        @pl.loop(0, row_count // tile)
        def _(step, lanes=lanes, part=part):
            rows = pl.ds(pl.multiple_of(step * tile, 16), tile)
            first = part * PAD_WIDTH // LANES
            for chunk in range(PAD_WIDTH // LANES):
                head_low[rows, chunk_lanes(chunk)] = pool[first + chunk, rows, :].astype(BF16)
            term = dot_lanes(head_low[rows, :], head_weights[:, lanes])
            mixed_grad[rows, 0:width] = term if part == 0 else mixed_grad[rows, 0:width] + term

        @pl.loop(0, row_count // tile)
        def _(step, lanes=lanes):
            rows = pl.ds(pl.multiple_of(step * tile, 16), tile)
            out_sum[...] += dot_rows(head_low[rows, :], low_rows[rows, :])

        low = out_sum[...].astype(BF16)
        head_grad_ref[part] = lax.dot_general(
            low, mapping, (((0,), (1,)), ((), ())), preferred_element_type=F32
        ).astype(BF16)

    def first_back(step, carry):
        rows = pl.ds(pl.multiple_of(step * 16, 16), 16)
        unit, scale = centered(input_ref[rows, :].astype(F32))
        grad = mixed_grad[rows, 0:width]
        total = dx1[rows, :] + norm_back(grad * table_ref[0:1, :], unit, scale)
        out_ref[rows, :] = total.astype(BF16)
        return carry[0] + fold(grad * unit), carry[1] + fold(grad)

    sums = lax.fori_loop(0, row_count // 16, first_back, (wide, wide))
    for index in range(2):
        grads_ref[index : index + 1, :] = jnp.sum(sums[index], axis=0, keepdims=True)


def mixing_backward(sides, sharpness, inputs, weights, table, saved, batch_sums, dx2, dn, back_sums):
    row_count, width = inputs.shape
    chunks = width // LANES
    shape = jax.ShapeDtypeStruct
    x1, qkv, mixed, scores, attention, u = saved
    return pl.pallas_call(
        mixing_backward_kernel,
        out_shape=(
            shape((row_count, width), BF16),
            shape((3, width, width), BF16),
            shape((width, width), BF16),
            shape((16, width), F32),
            shape((HEAD_PAIRS, LANES), F32),
        ),
        in_specs=[SMEM_SPEC, SMEM_SPEC]
        + [VMEM_SPEC] * 8
        + [ANY_SPEC, VMEM_SPEC, VMEM_SPEC, ANY_SPEC, VMEM_SPEC],
        out_specs=(VMEM_SPEC,) * 5,
        scratch_shapes=[
            pltpu.VMEM((width, 3 * PAD_WIDTH), BF16),
            pltpu.VMEM((PAD_WIDTH, width), BF16),
            pltpu.VMEM((3 * PAD_WIDTH // LANES, row_count, LANES), F32),
            pltpu.VMEM((chunks, LEAD + row_count + TAIL, LANES), F32),
            pltpu.VMEM((row_count, width), F32),
            pltpu.VMEM((row_count, PAD_WIDTH), F32),
            pltpu.VMEM((row_count, width), BF16),
            pltpu.VMEM((row_count, PAD_WIDTH), BF16),
            pltpu.VMEM((4, 2, HALF_WIDTH, HALF_WIDTH), BF16),
            pltpu.VMEM((PAD_WIDTH, width), F32),
            pltpu.SemaphoreType.DMA((2,)),
        ],
        compiler_params=pltpu.CompilerParams(vmem_limit_bytes=VMEM_LIMIT),
        name="mixing_backward",
    )(
        sides,
        sharpness,
        inputs,
        weights,
        table,
        x1,
        qkv,
        mixed,
        scores,
        attention,
        u,
        batch_sums,
        dx2,
        dn,
        back_sums,
    )


def shards(
    patch_embeddings,
    view_side_tokens,
    projection_masters,
    channel_coefficients,
    head_sharpness,
    output_adjoint,
    leading_covariance,
    trailing_covariance,
    leading_root_preconditioner,
    trailing_root_preconditioner,
    channel_energy_average,
    sharpness_energy_average,
    storage_position_map,
):
    row_count, feature_count = patch_embeddings.shape
    chunks = feature_count // LANES
    block_count = projection_masters.shape[0]
    shard_rows = projection_masters.shape[1]
    slot_count = leading_covariance.shape[0]
    weight_low = projection_masters.astype(BF16)
    full_table = lax.all_gather(channel_coefficients.astype(BF16), "fsdp", axis=1, tiled=True)
    table = full_table.astype(F32)
    mixing_blocks = lax.all_gather(weight_low[:4], "fsdp", axis=1, tiled=True)
    feed_blocks = lax.all_gather(weight_low[4:], "fsdp", axis=1, tiled=True)
    x1, qkv, mixed, scores, attention, u, e, sums = mixing_forward(
        view_side_tokens, head_sharpness, patch_embeddings, mixing_blocks, table
    )
    batch_sums = lax.psum(sums, ("dp", "fsdp"))
    layer_output, dx2, dn, up_grad, down_grad, feed_table = feed_forward(
        view_side_tokens, x1, e, batch_sums, feed_blocks, table, output_adjoint
    )
    gamma_part, beta_part = feed_table[13], feed_table[14]
    back_sums = lax.psum(
        jnp.concatenate(
            [beta_part.reshape(chunks, LANES), gamma_part.reshape(chunks, LANES), jnp.zeros((8 - 2 * chunks, LANES), F32)]
        ),
        ("dp", "fsdp"),
    )
    incoming_tokens_grad, head_grad, out_grad, mixing_table, sharp_lanes = mixing_backward(
        view_side_tokens,
        head_sharpness,
        patch_embeddings,
        mixing_blocks,
        table,
        (x1, qkv, mixed, scores, attention, u),
        batch_sums,
        dx2,
        dn,
        back_sums,
    )
    sharpness_share = jnp.sum(sharp_lanes.reshape(HEAD_NUMBER, HEAD_PAD), axis=1)
    table_grad = jnp.concatenate(
        [
            mixing_table[0:5],
            feed_table[13:15],
            feed_table[0:4],
            mixing_table[5:14],
            feed_table[4:13],
        ],
        axis=0,
    )
    block_grad = jnp.concatenate(
        [head_grad.astype(F32), out_grad.astype(F32)[None], up_grad, down_grad], axis=0
    )
    denominator_sum = lax.axis_size("fsdp")
    tiled_part = jnp.broadcast_to(
        sharpness_share[None, :], (denominator_sum, sharpness_share.shape[0])
    )
    portion_derivative, catalog_portion, sharpness_normalizer = (
        lax.psum_scatter(block_grad, "fsdp", scatter_dimension=1, tiled=True),
        lax.psum_scatter(table_grad, "fsdp", scatter_dimension=1, tiled=True),
        lax.psum_scatter(tiled_part, "fsdp", scatter_dimension=0, tiled=True),
    )
    portion_derivative, catalog_portion, sharpness_normalizer = lax.psum(
        (portion_derivative, catalog_portion, sharpness_normalizer), "dp"
    )
    sharpness_derivative = sharpness_normalizer[0]
    shard_place = lax.axis_index("fsdp")
    slot_index = jnp.arange(denominator_sum * slot_count, dtype=jnp.int32)
    slot_match = storage_position_map[None, :] == slot_index[:, None]
    slot_filled = jnp.any(slot_match, axis=1).astype(jnp.float32)[:, None, None]
    slot_block = jnp.sum(
        jnp.where(slot_match, jnp.arange(block_count, dtype=jnp.int32)[None, :], 0), axis=1
    )
    my_filled = lax.dynamic_slice_in_dim(slot_filled, shard_place * slot_count, slot_count, 0)
    my_block = lax.dynamic_slice_in_dim(slot_block, shard_place * slot_count, slot_count, 0)
    whole_grad = lax.all_gather(portion_derivative, "fsdp", axis=1, tiled=True)
    owned_grad = jnp.take(whole_grad, my_block, axis=0) * my_filled
    leading_covariance_renewed = covariance_forgetting * leading_covariance + (
        1.0 - covariance_forgetting
    ) * jnp.einsum("sij,skj->sik", owned_grad, owned_grad, precision=lax.Precision.HIGHEST)
    trailing_covariance_renewed = covariance_forgetting * trailing_covariance + (
        1.0 - covariance_forgetting
    ) * jnp.einsum("sji,sjk->sik", owned_grad, owned_grad, precision=lax.Precision.HIGHEST)
    halfway = jnp.einsum(
        "sij,sjk->sik", leading_root_preconditioner, owned_grad, precision=lax.Precision.HIGHEST
    )
    conditioned = jnp.einsum(
        "sij,sjk->sik", halfway, trailing_root_preconditioner, precision=lax.Precision.HIGHEST
    )
    every_update = lax.all_gather(conditioned, "fsdp", axis=0, tiled=True)
    my_rows = lax.dynamic_slice_in_dim(every_update, shard_place * shard_rows, shard_rows, 1)
    update = jnp.take(my_rows, storage_position_map, axis=0)
    projection_updated = projection_masters - weight_rate * update
    channel_energy_renewed = (
        covariance_forgetting * channel_energy_average
        + (1.0 - covariance_forgetting) * catalog_portion * catalog_portion
    )
    channel_params_updated = channel_coefficients - vector_rate * catalog_portion / (
        jnp.sqrt(channel_energy_renewed) + energy_epsilon
    )
    sharpness_energy_renewed = (
        covariance_forgetting * sharpness_energy_average
        + (1.0 - covariance_forgetting) * sharpness_derivative * sharpness_derivative
    )
    sharpness_updated = head_sharpness - sharpness_step_size * sharpness_derivative / (
        jnp.sqrt(sharpness_energy_renewed) + energy_epsilon
    )
    return (
        layer_output,
        incoming_tokens_grad,
        portion_derivative,
        leading_covariance_renewed,
        trailing_covariance_renewed,
        projection_updated,
        projection_updated.astype(jnp.bfloat16),
        catalog_portion,
        channel_energy_renewed,
        channel_params_updated,
        sharpness_derivative,
        sharpness_energy_renewed,
        sharpness_updated,
    )


def solution(mesh):
    in_specs = (
        P(("dp", "fsdp"), None),
        P(("dp", "fsdp")),
        P(None, "fsdp", None),
        P(None, "fsdp"),
        P(),
        P(("dp", "fsdp"), None),
        P("fsdp", None, None),
        P("fsdp", None, None),
        P("fsdp", None, None),
        P("fsdp", None, None),
        P(None, "fsdp"),
        P(),
        P(),
    )
    out_specs = (
        P(("dp", "fsdp"), None),
        P(("dp", "fsdp"), None),
        P(None, "fsdp", None),
        P("fsdp", None, None),
        P("fsdp", None, None),
        P(None, "fsdp", None),
        P(None, "fsdp", None),
        P(None, "fsdp"),
        P(None, "fsdp"),
        P(None, "fsdp"),
        P(),
        P(),
        P(),
    )
    return jax.shard_map(shards, mesh=mesh, in_specs=in_specs, out_specs=out_specs, check_vma=False)
```

time: 1380 us -> 956 us (0.69)
  local copies, waits for them, and re-layouts: 351 us -> 19.8 us
  Pallas kernels: 0 us -> 292 us
  other arithmetic: 242 us -> 15.2 us
  matrix products: 169 us -> 14.1 us
  blocking collectives: 134 us -> 156 us
    pallas_call x0 -> x3, Pallas kernels: none -> 292 us  [the longest x1 137 us: mixing_backward(): pl.pallas_call(mixing_backward_kernel, out_shape=(shape((row_count, width...]
    gather x18 -> x0, local copies, waits for them, and re-layouts: 153 us -> none  [the longest x12 102 us: regroup_into_grid(): return jnp.take(padded, incoming_tensor, axis=0)]
    dot_general x26 -> x2, matrix products: 160 us -> 8.05 us  [the longest x1 4.42 us: shards(): jnp.einsum('sji,sjk->sik', owned_grad, owned_grad, precision=lax.Precisio...]
    reduce_sum x20 -> x1, other arithmetic: 120 us -> 1.31 us  [shards(): jnp.sum(sharp_lanes.reshape(HEAD_NUMBER, HEAD_PAD), axis=1)]
    reshape x15 -> x1, local copies, waits for them, and re-layouts: 73.7 us -> 1.35 us  [shards(): sharp_lanes.reshape(HEAD_NUMBER, HEAD_PAD)]
    concatenate x14 -> x2, local copies, waits for them, and re-layouts: 46.3 us -> 0.47 us  [the longest x1 0.39 us: shards(): jnp.concatenate([mixing_table[0:5], feed_table[13:15], feed_table[0:4], m...]
    add_any x7 -> x0, other arithmetic: 38.1 us -> none  [the longest x3 22.1 us: depthwise(): padded[:, row_shift:row_shift + grid_side, column_shift:column_shift + gr...]
    convert_element_type x6 -> x3, other arithmetic: 35.6 us -> 2.76 us  [the longest x1 1.44 us: shards(): head_grad.astype(F32)]
  transfers between devices with their start and end apart: 6 -> 7, of which waited for: 6 -> 6; matrix products, arithmetic and copies ran while one was open for 5% -> 4% of each run, Pallas kernels for 0% -> 7%
where the time goes in v1:
time: 956 us; the launch traced here: 952 us
  waiting for transfers between devices  441 us (46%)
  Pallas kernels  292 us (31%)
  blocking collectives  156 us (16%)
  local copies, waits for them, and re-layouts  19.8 us (2%)
  other arithmetic  15.2 us (2%)
  between operations  14.5 us (2%)
  matrix products  14.1 us (1%)
    pallas_call x1, Pallas kernels, mixing_backward(): pl.pallas_call(mixing_backward_kernel, out_shape=(shape((row_count, width...  137 us
    reduce_scatter x1, waiting for transfers between devices, shards(): lax.psum_scatter(block_grad, 'fsdp', scatter_dimension=1, tiled=True)  136 us
    all_gather x1, waiting for transfers between devices, shards(): every_update = lax.all_gather(conditioned, 'fsdp', axis=0, tiled=True)  115 us
    all_gather x1, waiting for transfers between devices, shards(): whole_grad = lax.all_gather(portion_derivative, 'fsdp', axis=1, tiled=True)  110 us
    pallas_call x1, Pallas kernels, feed_forward(): pl.pallas_call(feed_kernel, out_shape=(shape((row_count, width), BF16), s...  90.4 us
    pallas_call x1, Pallas kernels, mixing_forward(): pl.pallas_call(mixing_forward_kernel, out_shape=(shape((row_count, width)...  64 us
    psum x1, blocking collectives, shards(): lax.psum(jnp.concatenate([beta_part.reshape(chunks, LANES), gamma_part.re...  50.5 us
    psum x1, blocking collectives, shards(): batch_sums = lax.psum(sums, ('dp', 'fsdp'))  49.8 us
  transfers between devices with their start and end apart: 7, of which 6 were waited for; matrix products, arithmetic and copies ran while one was open for 4% of the time, Pallas kernels for 7%

profile of v1, /device:TPU:1, one launch (start us, length us, event | category | flops | bytes accessed | tf_op | source)
XLA Modules:
  0.0 952.2 jit_solution(14711631723236444729)
XLA Ops:
  7.2 1.3 convert_element_type.19
  8.6 0.7 slice.40
  9.3 0.7 slice.41
  10.1 25.6 %all-gather = bf16[8,48,29]{1,2,0:T(8,128)(2,1)S(1)} all-gather(bf16[1,48,29]{1,2,0:T(8,128)(2,1)S(1)} %convert_bitcast_fusion), channel_id=1, replica_groups=mesh['dp'=4,'fsdp'=8] {'fsdp'}, dimensions={0}, use_global_device_ids=true | all-gather | bytes 25056 | tf_op jit(solution)/shard_map/all_gather | solution.py:943
  35.8 0.7 reshape.65
  36.6 16.3 %all-gather.6.cloned.1.call-done.weight_ref = bf16[4,384,384]{2,1,0:T(8,128)(2,1)} async-done(((bf16[4,48,384]{2,1,0:T(8,128)(2,1)}), bf16[4,384,384]{2,1,0:T(8,128)(2,1)}) %all-gather.6.cloned.1.call-update) | async-done | bytes 1179664 | tf_op jit(solution)/shard_map/all_gather | solution.py:945
  52.8 64.0 %mixing_forward.1 = (f32[1856,384]{1,0:T(8,128)}, f32[1856,1536]{1,0:T(8,128)}, bf16[1856,512]{1,0:T(8,128)(2,1)}, f32[16,4,48,128]{3,2,1,0:T(8,128)}, f32[16,4,...) custom-call(s32[16]{0:T(128)} %sides_ref.5, f32[8]{0:T(128)} %sharp_ref.3, ...), custom_call_target="tpu_custom_call" | custom-call | tf_op jit(solution)/shard_map/mixing_forward/pallas_call | solution.py:391
  116.8 49.8 %psum.35.bn_ref = f32[8,128]{1,0:T(8,128)} all-reduce(f32[8,128]{1,0:T(8,128)} %get-tuple-element.34), channel_id=1, replica_groups=mesh['dp'=4,'fsdp'=8] {'dp','fsdp'}, use_global_device_ids=true, to_apply=%region_0.0 | all-reduce | flops 1024 | bytes 8192 | tf_op jit(solution)/shard_map/psum | solution.py:950
  166.6 90.4 %feed_forward.1 = (bf16[1856,384]{1,0:T(8,128)(2,1)}, f32[1856,384]{1,0:T(8,128)}, f32[3,1856,128]{2,1,0:T(8,128)}, f32[4,384,384]{2,1,0:T(8,128)}, f32[4,384,384]{2,1,0:T(8,128)}, /*index=5*/f32[16,384]{1,0:T(8,128)}) custom-call(s32[16]{0:T(128)} %sides_ref.5, f32[1856,384]{1,0:T(8,128)} %get-tuple-element.32.x1_ref, ...), custom_call_target="tpu_custom_call" | custom-call | tf_op jit(solution)/shard_map/feed_forward/pallas_call | solution.py:610
  257.0 0.8 slice_reduce_fusion.1
  257.9 50.5 %psum.36.back_ref = f32[8,128]{1,0:T(8,128)} all-reduce(f32[8,128]{1,0:T(8,128)S(1)} %maximum_maximum_fusion), channel_id=1, replica_groups=mesh['dp'=4,'fsdp'=8] {'dp','fsdp'}, use_global_device_ids=true, to_apply=%region_1.0 | all-reduce | flops 1024 | bytes 8192 | tf_op jit(solution)/shard_map/psum | solution.py:955
  308.4 137.4 %mixing_backward.1 = (bf16[1856,384]{1,0:T(8,128)(2,1)}, bf16[3,384,384]{2,1,0:T(8,128)(2,1)}, bf16[384,384]{1,0:T(8,128)(2,1)}, f32[16,384]{1,0:T(8,128)}, f32[4,128]{1,0:T(4,128)}) custom-call(s32[16]{0:T(128)} %sides_ref.5, f32[8]{0:T(128)} %sharp_ref.3, bf16[1856,384]{1,0:T(8,128)(2,1)} %input_ref.3, ...), custom_call_target="tpu_custom_call" | custom-call | tf_op jit(solution)/shard_map/mixing_backward/pallas_call | solution.py:875
  445.9 1.4 convert_element_type.22
  447.4 0.5 copy-done.3
  447.9 3.1 pad_maximum_fusion
  451.1 136.5 %reduce-scatter.5.cloned.1.call-done = f32[12,48,384]{2,1,0:T(8,128)} async-done(((f32[12,384,384]{2,1,0:T(8,128)}), f32[12,48,384]{2,1,0:T(8,128)}) %reduce-scatter.5.cloned.1.call-update) | async-done | bytes 884752 | tf_op jit(solution)/shard_map/reduce_scatter | solution.py:992
  587.6 36.2 %all-reduce.4.cloned.1.call-done = f32[12,48,384]{2,1,0:T(8,128)} async-done(((f32[12,48,384]{2,1,0:T(8,128)}), f32[12,48,384]{2,1,0:T(8,128)}) %all-reduce.4.cloned.1.call-update) | async-done | bytes 884752 | tf_op jit(solution)/shard_map/psum | solution.py:996
  623.9 0.1 fusion.13
  624.1 0.1 select_reduce_fusion
  624.2 0.1 compare_and_fusion.1
  624.4 0.4 concatenate.11
  624.8 0.8 copy.41
  625.6 0.3 all-gather.12.cloned.1.call-start
  625.9 110.0 %all-gather.10.cloned.1.call-done = f32[12,384,384]{2,1,0:T(8,128)} async-done(((f32[12,48,384]{2,1,0:T(8,128)}), f32[12,384,384]{2,1,0:T(8,128)}) %all-gather.10.cloned.1.call-update) | async-done | bytes 7077904 | tf_op jit(solution)/shard_map/all_gather | solution.py:1009
  735.9 3.6 gather_fusion
  739.6 2.6 fusion.2
  742.2 3.4 fusion.21
  745.7 1.3 dynamic-slice.1
  747.0 0.7 compare_select_fusion
  747.7 0.6 pad_clamp_fusion
  748.3 1.2 compare_and_fusion
  749.5 1.3 reshape.43
  750.8 1.3 reduce_sum.19
  752.1 1.2 broadcast_in_dim.66
  753.4 16.1 %all-reduce = f32[8,8]{1,0:T(8,128)} all-reduce(f32[8,8]{1,0:T(8,128)} %broadcast_in_dim.66), channel_id=4, replica_groups=mesh['dp'=4,'fsdp'=8] {'fsdp'}, use_global_device_ids=true, to_apply=%region_9.0.clone | all-reduce | flops 64 | bytes 512
  769.4 1.8 dynamic-slice_bitcast_fusion
  771.3 26.5 %reduce-scatter.7.cloned.1.call-done = f32[48,29]{1,0:T(8,128)} async-done(((f32[384,29]{1,0:T(8,128)}), f32[48,29]{1,0:T(8,128)}) %reduce-scatter.7.cloned.1.call-update) | async-done | bytes 5584
  797.8 1.4 copy.42
  799.2 13.6 %all-reduce.1 = (f32[29,48]{1,0:T(8,128)}, f32[8]{0:T(128)}) all-reduce(f32[29,48]{1,0:T(8,128)} %copy.42, f32[8]{0:T(128)} %dynamic-slice_bitcast_fusion), channel_id=1, replica_groups=mesh['dp'=4,'fsdp'=8] {'dp'}, use_global_device_ids=true, to_apply=%region_7.0 | all-reduce | flops 1400 | bytes 11200 | tf_op jit(solution)/shard_map/psum | solution.py:996
  812.8 1.2 divide_subtract_fusion.1
  814.0 1.4 divide_subtract_fusion
  815.4 4.4 fusion
  819.8 3.6 fusion.1
  823.4 115.4 %all-gather.12.cloned.1.call-done = f32[16,384,384]{2,1,0:T(8,128)} async-done(((f32[2,384,384]{2,1,0:T(8,128)}), f32[16,384,384]{2,1,0:T(8,128)}) %all-gather.12.cloned.1.call-update) | async-done | bytes 9437200 | tf_op jit(solution)/shard_map/all_gather | solution.py:1023
  938.8 1.3 constant_dynamic-slice_fusion
  940.2 1.8 gather_fusion.1
  941.9 2.5 fusion.20
  944.4 0.9 copy.45
  (63 shorter events, 0.8 us)
Async XLA Ops:
  7.2 732.4 %copy-start = (f32[2,384,384]{2,1,0:T(8,128)S(1)}, f32[2,384,384]{2,1,0:T(8,128)}, u32[]{:S(2)}) copy-start(f32[2,384,384]{2,1,0:T(8,128)} %param.21) | copy-start | bytes 3538948
  7.2 2.9 copy-start.9
  7.2 45.6 %all-gather.6.cloned.1.call-start = ((), (), s32[]{:S(2)}) async-start(), calls=%async_computation.2 | async-start | bytes 1327104 | tf_op jit(solution)/shard_map/all_gather | solution.py:945
  9.3 157.4 %all-gather.8.cloned.1.call-start = ((), (), s32[]{:S(2)}) async-start(), calls=%async_computation.3 | async-start | bytes 2654208 | tf_op jit(solution)/shard_map/all_gather | solution.py:946
  10.1 577.5 %reduce-scatter.5.cloned.1.call-start = ((), (), s32[]{:S(2)}) async-start(), calls=%async_computation.4 | async-start | bytes 7962624 | tf_op jit(solution)/shard_map/reduce_scatter | solution.py:992
  308.4 138.9 %copy-start.4 = (f32[4,384,384]{2,1,0:T(8,128)S(1)}, f32[4,384,384]{2,1,0:T(8,128)}, u32[]{:S(2)}) copy-start(f32[4,384,384]{2,1,0:T(8,128)} %get-tuple-element.48) | copy-start | bytes 7077892
  445.8 1.5 copy-start.8
  445.8 2.0 copy-start.3
  451.0 172.9 %copy-start.17 = (s32[12]{0:T(128)S(1)}, s32[12]{0:T(128)}, u32[]{:S(2)}) copy-start(s32[12]{0:T(128)} %param.25) | copy-start | bytes 148
  451.0 173.3 %copy-start.11 = (f32[16,384]{1,0:T(8,128)S(1)}, f32[16,384]{1,0:T(8,128)}, u32[]{:S(2)}) copy-start(f32[16,384]{1,0:T(8,128)} %get-tuple-element.49) | copy-start | bytes 73732
  451.0 173.3 %copy-start.10 = (f32[16,384]{1,0:T(8,128)S(1)}, f32[16,384]{1,0:T(8,128)}, u32[]{:S(2)}) copy-start(f32[16,384]{1,0:T(8,128)} %get-tuple-element.43) | copy-start | bytes 73732
  451.0 172.8 %all-reduce.4.cloned.1.call-start = ((), (), s32[]{:S(2)}) async-start(), calls=%async_computation.5 | async-start | bytes 1769472 | tf_op jit(solution)/shard_map/psum | solution.py:996
  587.6 148.3 %all-gather.10.cloned.1.call-start = ((), (), s32[]{:S(2)}) async-start(), calls=%async_computation.6 | async-start | bytes 7962624 | tf_op jit(solution)/shard_map/all_gather | solution.py:1009
  623.8 174.0 %reduce-scatter.7.cloned.1.call-start = ((), (), s32[]{:S(2)}) async-start(), calls=%async_computation.8 | async-start | bytes 221184
  624.1 115.5 %copy-start.14 = (f32[2]{0:T(128)}, f32[2]{0:T(128)S(1)}, u32[]{:S(2)}) copy-start(f32[2]{0:T(128)S(1)} %dynamic_slice.10) | copy-start | bytes 28
  624.3 115.3 %copy-start.12 = (pred[2]{0:T(512)(128)(4,1)}, pred[2]{0:T(512)(128)(4,1)S(1)}, u32[]{:S(2)}) copy-start(pred[2]{0:T(512)(128)(4,1)S(1)} %get-tuple-element.61) | copy-start | bytes 10
  625.6 313.2 %all-gather.12.cloned.1.call-start = ((), (), s32[]{:S(2)}) async-start(), calls=%async_computation.7 | async-start | bytes 10616832 | tf_op jit(solution)/shard_map/all_gather | solution.py:1023
  739.6 2.6 copy-start.5
  745.6 69.7 %copy-start.6 = (f32[2,384,384]{2,1,0:T(8,128)S(1)}, f32[2,384,384]{2,1,0:T(8,128)}, u32[]{:S(2)}) copy-start(f32[2,384,384]{2,1,0:T(8,128)} %param.20) | copy-start | bytes 3538948
  815.3 4.4 copy-start.7
  815.3 4.4 copy-start.13
  815.3 4.4 copy-start.15
  940.1 1.8 copy-start.2
  940.1 1.8 copy-start.16
  941.9 2.5 copy-start.1
Sparse Core Ops, SparseCore 0:
  10.9 41.9 all-gather.5
  55.6 51.1 all-gather.7
  451.1 136.3 reduce-scatter.4
  589.9 33.8 all-reduce.3
  626.1 109.7 all-gather.9
  739.9 57.7 reduce-scatter.6
  800.2 138.5 all-gather.11

commit v2 on v1

--- a/solution.py
+++ b/solution.py
@@ -434,9 +434,9 @@
     out_ref,
     dx2_ref,
     dn_ref,
-    up_grad_ref,
-    down_grad_ref,
+    weight_grad_ref,
     grads_ref,
+    back_sums_ref,
     n_ref,
     z_ref,
     dw_ref,
@@ -450,6 +450,7 @@
     feed_grad,
     pre_grad,
     grads,
+    weight_sums,
 ):
     row_count, width = x1_ref.shape
     chunks = width // LANES
@@ -486,8 +487,7 @@
 
         for_groups(sides_ref, conv_step, 0)
 
-    up_grad_ref[...] = jnp.zeros_like(up_grad_ref)
-    down_grad_ref[...] = jnp.zeros_like(down_grad_ref)
+    weight_sums[...] = jnp.zeros_like(weight_sums)
     grads[...] = jnp.zeros_like(grads)
 
     def z_rows(rows):
@@ -548,8 +548,8 @@
             pre_grad[:, lanes] = (hidden_grad * pre[:, lanes]).astype(BF16)
         for part in range(expand):
             lanes = slice(part * width, (part + 1) * width)
-            down_grad_ref[part] += dot_rows(hidden_low[:, lanes], feed_grad[...])
-            up_grad_ref[part] += dot_rows(third_low[...], pre_grad[:, lanes])
+            weight_sums[expand + part] += dot_rows(hidden_low[:, lanes], feed_grad[...])
+            weight_sums[part] += dot_rows(third_low[...], pre_grad[:, lanes])
         total = None
         for part in range(expand):
             lanes = slice(part * width, (part + 1) * width)
@@ -580,6 +580,16 @@
         for index in range(3):
             grads[1 + index] += sums[index]
 
+    owners, pieces, shard, _ = weight_grad_ref.shape
+    inner = width // shard
+    for owner in range(owners):
+        rows = slice(owner % inner * shard, (owner % inner + 1) * shard)
+        for piece in range(pieces):
+            weight_grad_ref[owner, piece] = weight_sums[
+                owner // inner * pieces + piece, rows, :
+            ].astype(BF16)
+
+    back_sums_ref[...] = zero
     for index, source in enumerate((1, 2, 3, 0)):
         grads_ref[index : index + 1, :] = jnp.sum(grads[source], axis=0, keepdims=True)
     for chunk in range(chunks):
@@ -598,10 +608,15 @@
         tap_sums, gamma, beta = for_groups(sides_ref, back_step, ((zero,) * 9, zero, zero))
         lanes = chunk_lanes(chunk)
         for index, value in enumerate((*tap_sums, gamma, beta)):
-            grads_ref[4 + index : 5 + index, lanes] = jnp.sum(value, axis=0, keepdims=True)
-
-
-def feed_forward(sides, x1, e, batch_sums, weights, table, adjoint):
+            value = jnp.sum(value, axis=0, keepdims=True)
+            grads_ref[4 + index : 5 + index, lanes] = value
+            if index == 9:
+                back_sums_ref[chunks + chunk : chunks + chunk + 1, :] = value
+            if index == 10:
+                back_sums_ref[chunk : chunk + 1, :] = value
+
+
+def feed_forward(sides, x1, e, batch_sums, weights, table, adjoint, grad_shape):
     row_count, width = x1.shape
     chunks = width // LANES
     expand = weights.shape[0] // 2
@@ -613,9 +628,9 @@
             shape((row_count, width), BF16),
             shape((row_count, width), F32),
             shape((chunks, row_count, LANES), F32),
-            shape((expand, width, width), F32),
-            shape((expand, width, width), F32),
+            shape(grad_shape, BF16),
             shape((16, width), F32),
+            shape((8, LANES), F32),
         ),
         in_specs=[SMEM_SPEC] + [VMEM_SPEC] * 6,
         out_specs=(VMEM_SPEC,) * 6,
@@ -633,6 +648,7 @@
             pltpu.VMEM((tile, width), BF16),
             pltpu.VMEM((tile, expand * width), BF16),
             pltpu.VMEM((4, 8, width), F32),
+            pltpu.VMEM((2 * expand, width, width), F32),
         ],
         compiler_params=pltpu.CompilerParams(vmem_limit_bytes=VMEM_LIMIT),
         name="feed_forward",
@@ -656,10 +672,8 @@
     dn_hbm,
     back_ref,
     out_ref,
-    head_grad_ref,
-    out_grad_ref,
+    weight_grad_ref,
     grads_ref,
-    sharp_grad_ref,
     head_weights,
     out_weight,
     pool,
@@ -670,6 +684,7 @@
     head_low,
     spread,
     out_sum,
+    sharp_sums,
     load_sems,
 ):
     row_count, width = input_ref.shape
@@ -779,8 +794,8 @@
     pool[...] = jnp.zeros_like(pool)
 
     low = out_sum[...].astype(BF16)
-    out_grad_ref[...] = dot(mapping, low).astype(BF16)
-    sharp_grad_ref[...] = jnp.zeros_like(sharp_grad_ref)
+    weight_grad_ref[3] = dot(mapping, low).astype(BF16)
+    sharp_sums[...] = jnp.zeros_like(sharp_sums)
 
     def crop_step(crop, rows, keep):
         for half in range(2):
@@ -801,7 +816,7 @@
                 part = pair_part(block, pair)
                 part = shares * (part - jnp.sum(part * shares, axis=0, keepdims=True))
                 spread_pair(spread, half, pair, shares)
-                sharp_grad_ref[index : index + 1, :] += jnp.sum(part * scores, axis=0, keepdims=True)
+                sharp_sums[index : index + 1, :] += jnp.sum(part * scores, axis=0, keepdims=True)
                 part = part * pair_sharpness(sharp_ref, index)
                 query_sums.append(jnp.sum(part * scores, axis=0, keepdims=True))
                 spread_pair(spread, 2 + half, pair, part)
@@ -823,6 +838,15 @@
 
     for_crops(sides_ref, row_count, crop_step)
 
+    grads_ref[14:16, :] = jnp.zeros((2, width), F32)
+    lane = lax.broadcasted_iota(jnp.int32, (1, LANES), 1)
+    total = jnp.zeros((1, LANES), F32)
+    for head in range(HEAD_NUMBER):
+        row = sharp_sums[head // 2 : head // 2 + 1, :]
+        row = jnp.where((lane >> 6) == head % 2, row, 0.0)
+        total = jnp.where(lane == head, jnp.sum(row, axis=1, keepdims=True), total)
+    grads_ref[14:15, 0:LANES] = total
+
     def first_norm(step, _):
         rows = pl.ds(pl.multiple_of(step * 32, 32), 32)
         unit, _ = centered(input_ref[rows, :].astype(F32))
@@ -850,7 +874,7 @@
             out_sum[...] += dot_rows(head_low[rows, :], low_rows[rows, :])
 
         low = out_sum[...].astype(BF16)
-        head_grad_ref[part] = lax.dot_general(
+        weight_grad_ref[part] = lax.dot_general(
             low, mapping, (((0,), (1,)), ((), ())), preferred_element_type=F32
         ).astype(BF16)
 
@@ -876,15 +900,13 @@
         mixing_backward_kernel,
         out_shape=(
             shape((row_count, width), BF16),
-            shape((3, width, width), BF16),
-            shape((width, width), BF16),
+            shape((4, width, width), BF16),
             shape((16, width), F32),
-            shape((HEAD_PAIRS, LANES), F32),
         ),
         in_specs=[SMEM_SPEC, SMEM_SPEC]
         + [VMEM_SPEC] * 8
         + [ANY_SPEC, VMEM_SPEC, VMEM_SPEC, ANY_SPEC, VMEM_SPEC],
-        out_specs=(VMEM_SPEC,) * 5,
+        out_specs=(VMEM_SPEC,) * 3,
         scratch_shapes=[
             pltpu.VMEM((width, 3 * PAD_WIDTH), BF16),
             pltpu.VMEM((PAD_WIDTH, width), BF16),
@@ -896,6 +918,7 @@
             pltpu.VMEM((row_count, PAD_WIDTH), BF16),
             pltpu.VMEM((4, 2, HALF_WIDTH, HALF_WIDTH), BF16),
             pltpu.VMEM((PAD_WIDTH, width), F32),
+            pltpu.VMEM((HEAD_PAIRS, LANES), F32),
             pltpu.SemaphoreType.DMA((2,)),
         ],
         compiler_params=pltpu.CompilerParams(vmem_limit_bytes=VMEM_LIMIT),
@@ -919,6 +942,606 @@
     )
 
 
+MESH = pl.DeviceIdType.MESH
+
+
+def greet(peers):
+    barrier = pltpu.get_barrier_semaphore()
+    for peer in peers:
+        pl.semaphore_signal(barrier, inc=1, device_id=peer, device_id_type=MESH)
+    pl.semaphore_wait(barrier, len(peers))
+
+
+def push(source, target, send, receive, peer):
+    copy = pltpu.make_async_remote_copy(
+        src_ref=source,
+        dst_ref=target,
+        send_sem=send,
+        recv_sem=receive,
+        device_id=peer,
+        device_id_type=MESH,
+    )
+    copy.start()
+    return copy
+
+
+def turned(place, step, count):
+    return lax.rem(place + step, count)
+
+
+def ring_peers(axis, count):
+    place = lax.axis_index(axis)
+    return [{axis: turned(place, step, count)} for step in range(1, count)]
+
+
+def comm_params(identity):
+    return pltpu.CompilerParams(
+        collective_id=identity, has_side_effects=True, vmem_limit_bytes=VMEM_LIMIT
+    )
+
+
+def sum_all_kernel(
+    counts, part_ref, total_ref, outer, inner, middle, outer_send, outer_recv, inner_send, inner_recv
+):
+    n_dp, n_fsdp = counts
+    dp, fsdp = lax.axis_index("dp"), lax.axis_index("fsdp")
+    inner_peers, outer_peers = ring_peers("fsdp", n_fsdp), ring_peers("dp", n_dp)
+    greet(inner_peers + outer_peers)
+    inner[fsdp] = part_ref[...]
+    copies = [
+        push(part_ref, inner.at[fsdp], inner_send.at[k], inner_recv.at[k], peer)
+        for k, peer in enumerate(inner_peers)
+    ]
+    for copy in copies:
+        copy.wait()
+    total = inner[0]
+    for k in range(1, n_fsdp):
+        total = total + inner[k]
+    middle[...] = total
+    outer[dp] = total
+    copies = [
+        push(middle, outer.at[dp], outer_send.at[k], outer_recv.at[k], peer)
+        for k, peer in enumerate(outer_peers)
+    ]
+    for copy in copies:
+        copy.wait()
+    total = outer[0]
+    for k in range(1, n_dp):
+        total = total + outer[k]
+    total_ref[...] = total
+
+
+def sum_all(part, counts, identity):
+    n_dp, n_fsdp = counts
+    return pl.pallas_call(
+        functools.partial(sum_all_kernel, counts),
+        out_shape=jax.ShapeDtypeStruct(part.shape, F32),
+        in_specs=[VMEM_SPEC],
+        out_specs=VMEM_SPEC,
+        scratch_shapes=[
+            pltpu.VMEM((n_dp, *part.shape), F32),
+            pltpu.VMEM((n_fsdp, *part.shape), F32),
+            pltpu.VMEM(part.shape, F32),
+            pltpu.SemaphoreType.DMA((n_dp - 1,)),
+            pltpu.SemaphoreType.DMA((n_dp - 1,)),
+            pltpu.SemaphoreType.DMA((n_fsdp - 1,)),
+            pltpu.SemaphoreType.DMA((n_fsdp - 1,)),
+        ],
+        compiler_params=comm_params(identity),
+        name="sum_all",
+    )(part)
+
+
+def gather_kernel(
+    counts,
+    masters_ref,
+    table_ref,
+    blocks_ref,
+    full_table_ref,
+    blocks,
+    tables,
+    stage,
+    ring_send,
+    ring_recv,
+    table_send,
+    table_recv,
+    cross_send,
+    cross_recv,
+    pair_send,
+    pair_recv,
+):
+    n_dp, n_fsdp = counts
+    dp, fsdp = lax.axis_index("dp"), lax.axis_index("fsdp")
+    shard, width = masters_ref.shape[1:]
+    columns = table_ref.shape[1]
+    across = lax.rem(dp + 2, 4)
+    pair = dp + 1 - 2 * lax.rem(dp, 2)
+    peers = ring_peers("fsdp", n_fsdp)
+    greet(peers + [{"dp": across}, {"dp": pair}])
+
+    def piece(block, owner):
+        return blocks.at[block, pl.ds(pl.multiple_of(owner * shard, 16), shard), :]
+
+    def origin(step):
+        return lax.rem(fsdp + n_fsdp - step, n_fsdp)
+
+    stage[...] = jnp.zeros_like(stage)
+    stage[0 : table_ref.shape[0], 0:columns] = table_ref[...]
+    tables[fsdp] = stage[...].astype(BF16)
+    blocks[dp, pl.ds(pl.multiple_of(fsdp * shard, 16), shard), :] = masters_ref[dp].astype(BF16)
+    own = piece(dp, fsdp)
+    ring = [
+        push(own, own, ring_send.at[k], ring_recv.at[k], peer) for k, peer in enumerate(peers)
+    ]
+    table_copies = [
+        push(tables.at[fsdp], tables.at[fsdp], table_send.at[k], table_recv.at[k], peer)
+        for k, peer in enumerate(peers)
+    ]
+    crossing, pairing = [], []
+    for step in range(n_fsdp):
+        if step:
+            ring[step - 1].wait_recv()
+        part = piece(dp, origin(step))
+        crossing.append(push(part, part, cross_send.at[step], cross_recv.at[step], {"dp": across}))
+        pairing.append(
+            push(part, part, pair_send.at[0, step], pair_recv.at[0, step], {"dp": pair})
+        )
+    for step in range(n_fsdp):
+        crossing[step].wait_recv()
+        part = piece(across, origin(step))
+        pairing.append(
+            push(part, part, pair_send.at[1, step], pair_recv.at[1, step], {"dp": pair})
+        )
+    for copy in table_copies:
+        copy.wait_recv()
+    total = None
+    for owner in range(n_fsdp):
+        lane = lax.broadcasted_iota(jnp.int32, (LANES, width), 0)
+        target = lax.broadcasted_iota(jnp.int32, (LANES, width), 1)
+        hit = (lane < columns) & (lane + owner * columns == target)
+        term = dot(tables[owner], hit.astype(F32).astype(BF16))
+        total = term if total is None else total + term
+    full_table_ref[...] = total
+    for copy in pairing:
+        copy.wait_recv()
+    blocks_ref[...] = blocks[...]
+    for copy in ring + table_copies + crossing + pairing:
+        copy.wait_send()
+
+
+def gather_start(masters, coefficients, counts, identity):
+    n_dp, n_fsdp = counts
+    width = masters.shape[2]
+    shape = jax.ShapeDtypeStruct
+    dma = pltpu.SemaphoreType.DMA
+    return pl.pallas_call(
+        functools.partial(gather_kernel, counts),
+        out_shape=(shape((4, width, width), BF16), shape((32, width), F32)),
+        in_specs=[VMEM_SPEC, VMEM_SPEC],
+        out_specs=(VMEM_SPEC, VMEM_SPEC),
+        scratch_shapes=[
+            pltpu.VMEM((4, width, width), BF16),
+            pltpu.VMEM((n_fsdp, 32, LANES), BF16),
+            pltpu.VMEM((32, LANES), F32),
+            dma((n_fsdp - 1,)),
+            dma((n_fsdp - 1,)),
+            dma((n_fsdp - 1,)),
+            dma((n_fsdp - 1,)),
+            dma((n_fsdp,)),
+            dma((n_fsdp,)),
+            dma((2, n_fsdp)),
+            dma((2, n_fsdp)),
+        ],
+        compiler_params=comm_params(identity),
+        name="gather_start",
+    )(masters, coefficients)
+
+
+def owner_rows(owner, shard):
+    return pl.ds(pl.multiple_of(owner * shard, 16), shard)
+
+
+def reduce_kernel(
+    counts,
+    place_ref,
+    mix_ref,
+    feed_ref,
+    mix_table_ref,
+    feed_table_ref,
+    energy_ref,
+    coefficient_ref,
+    sharp_ref,
+    grad_ref,
+    slots_ref,
+    table_grad_ref,
+    energy_out_ref,
+    coefficient_out_ref,
+    sharp_out_ref,
+    pair_buf,
+    cross_out,
+    cross_buf,
+    ring_out,
+    ring_buf,
+    feed_buf,
+    dp_buf,
+    slot_out,
+    slots,
+    table_stage,
+    table_out,
+    table_buf,
+    table_part,
+    table_dp,
+    pair_send,
+    pair_recv,
+    cross_send,
+    cross_recv,
+    ring_send,
+    ring_recv,
+    feed_send,
+    feed_recv,
+    dp_send,
+    dp_recv,
+    slot_send,
+    slot_recv,
+    twin_send,
+    twin_recv,
+    table_send,
+    table_recv,
+    table_dp_send,
+    table_dp_recv,
+):
+    n_dp, n_fsdp = counts
+    dp, fsdp = lax.axis_index("dp"), lax.axis_index("fsdp")
+    width = mix_ref.shape[2]
+    shard = width // n_fsdp
+    core = lax.rem(dp, 2)
+    across = lax.rem(dp + 2, 4)
+    pair = dp + 1 - 2 * core
+    pair_across = lax.rem(pair + 2, 4)
+    peers, dp_peers = ring_peers("fsdp", n_fsdp), ring_peers("dp", n_dp)
+    to_pair, to_across = {"dp": pair}, {"dp": across}
+    greet(peers + dp_peers)
+
+    parts = 4
+    deep = width // parts
+    pairing = []
+    for part in range(parts):
+        rows = pl.ds(part * deep, deep)
+        for side, block in enumerate((pair_across, pair)):
+            pairing.append(
+                push(
+                    mix_ref.at[block, rows],
+                    pair_buf.at[side, rows],
+                    pair_send.at[side, part],
+                    pair_recv.at[side, part],
+                    to_pair,
+                )
+            )
+    feed_buf[dp] = feed_ref[...]
+    feeding = [
+        push(feed_ref, feed_buf.at[dp], feed_send.at[k], feed_recv.at[k], peer)
+        for k, peer in enumerate(dp_peers)
+    ]
+
+    table_stage[...] = jnp.zeros_like(table_stage)
+    for row, (source, first) in enumerate(TABLE_ROWS):
+        ref = mix_table_ref if source == 0 else feed_table_ref
+        table_stage[row : row + 1, :] = ref[first : first + 1, :]
+    terms, rest = [], table_stage[...]
+    for _ in range(3):
+        term = rest.astype(BF16)
+        terms.append(term)
+        rest = rest - term.astype(F32)
+    columns = width // n_fsdp
+    sharp_row = lax.broadcasted_iota(jnp.int32, (32, LANES), 0) == 31
+    sharp_values = jnp.broadcast_to(mix_table_ref[14:15, 0:LANES], (32, LANES))
+    for owner in range(n_fsdp):
+        lane = lax.broadcasted_iota(jnp.int32, (width, LANES), 1)
+        source = lax.broadcasted_iota(jnp.int32, (width, LANES), 0)
+        hit = ((lane < columns) & (lane + owner * columns == source)).astype(F32).astype(BF16)
+        value = dot(terms[0], hit) + dot(terms[1], hit) + dot(terms[2], hit)
+        table_out[owner] = jnp.where(sharp_row, sharp_values, value)
+    table_buf[fsdp] = table_out[fsdp]
+    tabling = [
+        push(
+            table_out.at[turned(fsdp, k + 1, n_fsdp)],
+            table_buf.at[fsdp],
+            table_send.at[k],
+            table_recv.at[k],
+            peer,
+        )
+        for k, peer in enumerate(peers)
+    ]
+
+    crossing = []
+    for part in range(parts):
+        rows = pl.ds(part * deep, deep)
+        pairing[2 * part].wait_recv()
+        cross_out[rows, :] = (
+            mix_ref[across, rows, :].astype(F32) + pair_buf[0, rows, :].astype(F32)
+        ).astype(BF16)
+        crossing.append(
+            push(
+                cross_out.at[rows],
+                cross_buf.at[rows],
+                cross_send.at[part],
+                cross_recv.at[part],
+                to_across,
+            )
+        )
+    for part in range(parts):
+        rows = pl.ds(part * deep, deep)
+        pairing[2 * part + 1].wait_recv()
+        crossing[part].wait_recv()
+        ring_out[rows, :] = (
+            mix_ref[dp, rows, :].astype(F32)
+            + pair_buf[1, rows, :].astype(F32)
+            + cross_buf[rows, :].astype(F32)
+        ).astype(BF16)
+    ring = [
+        push(
+            ring_out.at[owner_rows(turned(fsdp, k + 1, n_fsdp), shard)],
+            ring_buf.at[fsdp],
+            ring_send.at[k],
+            ring_recv.at[k],
+            peer,
+        )
+        for k, peer in enumerate(peers)
+    ]
+    ring_buf[fsdp] = ring_out[owner_rows(fsdp, shard), :]
+
+    for copy in tabling:
+        copy.wait_recv()
+    total = table_buf[0]
+    for owner in range(1, n_fsdp):
+        total = total + table_buf[owner]
+    table_part[...] = total
+    table_dp[dp] = total
+    table_dps = [
+        push(table_part, table_dp.at[dp], table_dp_send.at[k], table_dp_recv.at[k], peer)
+        for k, peer in enumerate(dp_peers)
+    ]
+
+    for copy in ring:
+        copy.wait_recv()
+    total = ring_buf[0].astype(F32)
+    for owner in range(1, n_fsdp):
+        total = total + ring_buf[owner].astype(F32)
+    dp_buf[dp] = total
+    gathering = [
+        push(dp_buf.at[dp], dp_buf.at[dp], dp_send.at[k], dp_recv.at[k], peer)
+        for k, peer in enumerate(dp_peers)
+    ]
+    for copy in feeding:
+        copy.wait_recv()
+    pieces = feed_ref.shape[0]
+    for place in range(n_dp):
+        for piece in range(pieces):
+            grad_ref[n_dp + place * pieces + piece] = feed_buf[place, piece].astype(F32)
+    for copy in gathering:
+        copy.wait_recv()
+    for place in range(n_dp):
+        grad_ref[place] = dp_buf[place]
+
+    slot_count = 2 * n_fsdp
+    block_count = grad_ref.shape[0]
+    for slot in range(slot_count):
+        block, filled = jnp.int32(0), jnp.int32(0)
+        for index in range(block_count):
+            here = place_ref[index] == slot
+            block = jnp.where(here, index, block)
+            filled = jnp.where(here, 1, filled)
+        rows = grad_ref[block]
+        slot_out[slot] = (rows * filled.astype(F32)).astype(BF16)
+    slots[core, owner_rows(fsdp, shard), :] = slot_out[2 * fsdp + core]
+    slotting = [
+        push(
+            slot_out.at[2 * turned(fsdp, k + 1, n_fsdp) + core],
+            slots.at[core, owner_rows(fsdp, shard), :],
+            slot_send.at[k],
+            slot_recv.at[k],
+            peer,
+        )
+        for k, peer in enumerate(peers)
+    ]
+    twins = []
+    for step in range(n_fsdp):
+        if step:
+            slotting[step - 1].wait_recv()
+        owner = lax.rem(fsdp + n_fsdp - step, n_fsdp)
+        part = slots.at[core, owner_rows(owner, shard), :]
+        twins.append(push(part, part, twin_send.at[step], twin_recv.at[step], to_pair))
+
+    for copy in table_dps:
+        copy.wait_recv()
+    total = table_dp[0]
+    for place in range(1, n_dp):
+        total = total + table_dp[place]
+    count = energy_ref.shape[0]
+    grad = total[0:count, 0:columns]
+    table_grad_ref[...] = grad
+    energy = covariance_forgetting * energy_ref[...] + (1.0 - covariance_forgetting) * grad * grad
+    energy_out_ref[...] = energy
+    coefficient_out_ref[...] = coefficient_ref[...] - vector_rate * grad / (
+        jnp.sqrt(energy) + energy_epsilon
+    )
+    grad = total[31:32, 0:HEAD_NUMBER]
+    energy = (
+        covariance_forgetting * sharp_ref[1:2, :] + (1.0 - covariance_forgetting) * grad * grad
+    )
+    sharp_out_ref[0:1, :] = grad
+    sharp_out_ref[1:2, :] = energy
+    sharp_out_ref[2:3, :] = sharp_ref[0:1, :] - sharpness_step_size * grad / (
+        jnp.sqrt(energy) + energy_epsilon
+    )
+    for copy in twins:
+        copy.wait_recv()
+    slots_ref[...] = slots[...]
+    for copy in (
+        pairing + feeding + tabling + crossing + ring + table_dps + gathering + slotting + twins
+    ):
+        copy.wait_send()
+
+
+TABLE_ROWS = (
+    [(0, row) for row in range(5)]
+    + [(1, 13), (1, 14)]
+    + [(1, row) for row in range(4)]
+    + [(0, row) for row in range(5, 14)]
+    + [(1, row) for row in range(4, 13)]
+)
+
+
+def reduce_gradients(
+    places, mix, feed, mix_table, feed_table, energy, coefficients, sharps, counts, identity
+):
+    n_dp, n_fsdp = counts
+    width = mix.shape[2]
+    shard = width // n_fsdp
+    blocks = n_dp + feed.shape[0] * n_dp
+    shape = jax.ShapeDtypeStruct
+    dma = pltpu.SemaphoreType.DMA
+    return pl.pallas_call(
+        functools.partial(reduce_kernel, counts),
+        out_shape=(
+            shape((blocks, shard, width), F32),
+            shape((2, width, width), BF16),
+            shape(energy.shape, F32),
+            shape(energy.shape, F32),
+            shape(energy.shape, F32),
+            shape((3, sharps.shape[1]), F32),
+        ),
+        in_specs=[SMEM_SPEC] + [VMEM_SPEC] * 7,
+        out_specs=(VMEM_SPEC,) * 6,
+        scratch_shapes=[
+            pltpu.VMEM((2, width, width), BF16),
+            pltpu.VMEM((width, width), BF16),
+            pltpu.VMEM((width, width), BF16),
+            pltpu.VMEM((width, width), BF16),
+            pltpu.VMEM((n_fsdp, shard, width), BF16),
+            pltpu.VMEM((n_dp, *feed.shape), BF16),
+            pltpu.VMEM((n_dp, shard, width), F32),
+            pltpu.VMEM((2 * n_fsdp, shard, width), BF16),
+            pltpu.VMEM((2, width, width), BF16),
+            pltpu.VMEM((32, width), F32),
+            pltpu.VMEM((n_fsdp, 32, LANES), F32),
+            pltpu.VMEM((n_fsdp, 32, LANES), F32),
+            pltpu.VMEM((32, LANES), F32),
+            pltpu.VMEM((n_dp, 32, LANES), F32),
+            dma((2, 4)),
+            dma((2, 4)),
+            dma((4,)),
+            dma((4,)),
+            dma((n_fsdp - 1,)),
+            dma((n_fsdp - 1,)),
+            dma((n_dp - 1,)),
+            dma((n_dp - 1,)),
+            dma((n_dp - 1,)),
+            dma((n_dp - 1,)),
+            dma((n_fsdp - 1,)),
+            dma((n_fsdp - 1,)),
+            dma((n_fsdp,)),
+            dma((n_fsdp,)),
+            dma((n_fsdp - 1,)),
+            dma((n_fsdp - 1,)),
+            dma((n_dp - 1,)),
+            dma((n_dp - 1,)),
+        ],
+        compiler_params=comm_params(identity),
+        name="reduce_gradients",
+    )(places, mix, feed, mix_table, feed_table, energy, coefficients, sharps)
+
+
+def shampoo_kernel(grad_ref, left_ref, right_ref, left_root, right_root, left_out, right_out, step_ref):
+    grad = grad_ref[...]
+    left_out[...] = covariance_forgetting * left_ref[...] + (
+        1.0 - covariance_forgetting
+    ) * dot_lanes(grad, grad)
+    right_out[...] = covariance_forgetting * right_ref[...] + (
+        1.0 - covariance_forgetting
+    ) * dot_rows(grad, grad)
+    root = split(left_root[...])
+    half = split(dot(root[0], grad) + dot(root[1], grad))
+    step_ref[...] = dot_split(dot, half, split(right_root[...])).astype(BF16)
+
+
+def shampoo(grads, left, right, left_root, right_root):
+    slots, width, _ = grads.shape
+    shape = jax.ShapeDtypeStruct
+    spec = pl.BlockSpec((pl.Squeezed(), width, width), lambda slot: (slot, 0, 0))
+    return pl.pallas_call(
+        shampoo_kernel,
+        grid=(slots,),
+        out_shape=(
+            shape(grads.shape, F32),
+            shape(grads.shape, F32),
+            shape(grads.shape, BF16),
+        ),
+        in_specs=[spec] * 5,
+        out_specs=(spec,) * 3,
+        compiler_params=pltpu.CompilerParams(vmem_limit_bytes=VMEM_LIMIT),
+        name="shampoo",
+    )(grads, left, right, left_root, right_root)
+
+
+def return_kernel(
+    counts, steps_ref, rows_ref, rows_buf, ring_send, ring_recv, twin_send, twin_recv
+):
+    n_dp, n_fsdp = counts
+    dp, fsdp = lax.axis_index("dp"), lax.axis_index("fsdp")
+    width = steps_ref.shape[2]
+    shard = width // n_fsdp
+    core = lax.rem(dp, 2)
+    to_pair = {"dp": dp + 1 - 2 * core}
+    peers = ring_peers("fsdp", n_fsdp)
+    greet(peers + [to_pair])
+    ring = [
+        push(
+            steps_ref.at[core, owner_rows(turned(fsdp, k + 1, n_fsdp), shard)],
+            rows_buf.at[2 * fsdp + core],
+            ring_send.at[k],
+            ring_recv.at[k],
+            peer,
+        )
+        for k, peer in enumerate(peers)
+    ]
+    rows_buf[2 * fsdp + core] = steps_ref[core, owner_rows(fsdp, shard), :]
+    twins = []
+    for step in range(n_fsdp):
+        if step:
+            ring[step - 1].wait_recv()
+        owner = lax.rem(fsdp + n_fsdp - step, n_fsdp)
+        part = rows_buf.at[2 * owner + core]
+        twins.append(push(part, part, twin_send.at[step], twin_recv.at[step], to_pair))
+    for copy in twins:
+        copy.wait_recv()
+    rows_ref[...] = rows_buf[...]
+    for copy in ring + twins:
+        copy.wait_send()
+
+
+def return_steps(steps, counts, identity):
+    n_dp, n_fsdp = counts
+    width = steps.shape[2]
+    shard = width // n_fsdp
+    dma = pltpu.SemaphoreType.DMA
+    return pl.pallas_call(
+        functools.partial(return_kernel, counts),
+        out_shape=jax.ShapeDtypeStruct((2 * n_fsdp, shard, width), BF16),
+        in_specs=[VMEM_SPEC],
+        out_specs=VMEM_SPEC,
+        scratch_shapes=[
+            pltpu.VMEM((2 * n_fsdp, shard, width), BF16),
+            dma((n_fsdp - 1,)),
+            dma((n_fsdp - 1,)),
+            dma((n_fsdp,)),
+            dma((n_fsdp,)),
+        ],
+        compiler_params=comm_params(identity),
+        name="return_steps",
+    )(steps)
+
+
 def shards(
     patch_embeddings,
     view_side_tokens,
@@ -935,30 +1558,37 @@
     storage_position_map,
 ):
     row_count, feature_count = patch_embeddings.shape
-    chunks = feature_count // LANES
     block_count = projection_masters.shape[0]
     shard_rows = projection_masters.shape[1]
     slot_count = leading_covariance.shape[0]
-    weight_low = projection_masters.astype(BF16)
-    full_table = lax.all_gather(channel_coefficients.astype(BF16), "fsdp", axis=1, tiled=True)
-    table = full_table.astype(F32)
-    mixing_blocks = lax.all_gather(weight_low[:4], "fsdp", axis=1, tiled=True)
-    feed_blocks = lax.all_gather(weight_low[4:], "fsdp", axis=1, tiled=True)
+    counts = (lax.axis_size("dp"), lax.axis_size("fsdp"))
+    direct = counts[0] == 4 and slot_count == 2 and shard_rows % 16 == 0
+    if direct:
+        mixing_blocks, table = gather_start(projection_masters, channel_coefficients, counts, 0)
+        grad_shape = (counts[0] * counts[1], (block_count - 4) // counts[0], shard_rows, feature_count)
+    else:
+        full_table = lax.all_gather(channel_coefficients.astype(BF16), "fsdp", axis=1, tiled=True)
+        table = full_table.astype(F32)
+        mixing_blocks = lax.all_gather(
+            projection_masters[:4].astype(BF16), "fsdp", axis=1, tiled=True
+        )
+        grad_shape = (1, block_count - 4, feature_count, feature_count)
+    feed_blocks = lax.all_gather(projection_masters[4:].astype(BF16), "fsdp", axis=1, tiled=True)
+
+    def batch_total(part, identity):
+        if direct:
+            return sum_all(part, counts, identity)
+        return lax.psum(part, ("dp", "fsdp"))
+
     x1, qkv, mixed, scores, attention, u, e, sums = mixing_forward(
         view_side_tokens, head_sharpness, patch_embeddings, mixing_blocks, table
     )
-    batch_sums = lax.psum(sums, ("dp", "fsdp"))
-    layer_output, dx2, dn, up_grad, down_grad, feed_table = feed_forward(
-        view_side_tokens, x1, e, batch_sums, feed_blocks, table, output_adjoint
-    )
-    gamma_part, beta_part = feed_table[13], feed_table[14]
-    back_sums = lax.psum(
-        jnp.concatenate(
-            [beta_part.reshape(chunks, LANES), gamma_part.reshape(chunks, LANES), jnp.zeros((8 - 2 * chunks, LANES), F32)]
-        ),
-        ("dp", "fsdp"),
-    )
-    incoming_tokens_grad, head_grad, out_grad, mixing_table, sharp_lanes = mixing_backward(
+    batch_sums = batch_total(sums, 1)
+    layer_output, dx2, dn, feed_grad, feed_table, back_part = feed_forward(
+        view_side_tokens, x1, e, batch_sums, feed_blocks, table, output_adjoint, grad_shape
+    )
+    back_sums = batch_total(back_part, 2)
+    incoming_tokens_grad, mixing_grad, mixing_table = mixing_backward(
         view_side_tokens,
         head_sharpness,
         patch_embeddings,
@@ -970,20 +1600,55 @@
         dn,
         back_sums,
     )
-    sharpness_share = jnp.sum(sharp_lanes.reshape(HEAD_NUMBER, HEAD_PAD), axis=1)
-    table_grad = jnp.concatenate(
-        [
-            mixing_table[0:5],
-            feed_table[13:15],
-            feed_table[0:4],
-            mixing_table[5:14],
-            feed_table[4:13],
-        ],
-        axis=0,
-    )
-    block_grad = jnp.concatenate(
-        [head_grad.astype(F32), out_grad.astype(F32)[None], up_grad, down_grad], axis=0
-    )
+    if direct:
+        feed_grad = lax.psum_scatter(
+            feed_grad, ("dp", "fsdp"), scatter_dimension=0, tiled=True
+        )[0]
+        (
+            portion_derivative,
+            owned_grad,
+            catalog_portion,
+            channel_energy_renewed,
+            channel_params_updated,
+            sharps,
+        ) = reduce_gradients(
+            storage_position_map,
+            mixing_grad,
+            feed_grad,
+            mixing_table,
+            feed_table,
+            channel_energy_average,
+            channel_coefficients,
+            jnp.stack([head_sharpness, sharpness_energy_average]),
+            counts,
+            3,
+        )
+        leading_covariance_renewed, trailing_covariance_renewed, steps = shampoo(
+            owned_grad,
+            leading_covariance,
+            trailing_covariance,
+            leading_root_preconditioner,
+            trailing_root_preconditioner,
+        )
+        my_rows = return_steps(steps, counts, 4)
+        update = jnp.take(my_rows, storage_position_map, axis=0).astype(F32)
+        projection_updated = projection_masters - weight_rate * update
+        return (
+            layer_output,
+            incoming_tokens_grad,
+            portion_derivative,
+            leading_covariance_renewed,
+            trailing_covariance_renewed,
+            projection_updated,
+            projection_updated.astype(BF16),
+            catalog_portion,
+            channel_energy_renewed,
+            channel_params_updated,
+            *sharps,
+        )
+    sharpness_share = mixing_table[14, 0:HEAD_NUMBER]
+    table_grad = jnp.stack([(mixing_table, feed_table)[source][row] for source, row in TABLE_ROWS])
+    block_grad = jnp.concatenate([mixing_grad, feed_grad[0]], axis=0).astype(F32)
     denominator_sum = lax.axis_size("fsdp")
     tiled_part = jnp.broadcast_to(
         sharpness_share[None, :], (denominator_sum, sharpness_share.shape[0])

time: 956 us -> 448 us (0.47)
  waiting for transfers between devices: 441 us -> 0.08 us
  blocking collectives: 156 us -> 0 us
  Pallas kernels: 292 us -> 424 us
  matrix products: 14.1 us -> 0 us
  other arithmetic: 15.2 us -> 1.85 us
  local copies, waits for them, and re-layouts: 19.8 us -> 7.43 us
    all_gather x4 -> x1, waiting for transfers between devices: 242 us -> 0.02 us  [shards(): lax.all_gather(projection_masters[4:].astype(BF16), 'fsdp', axis=1, tiled...]
    reduce_scatter x1, waiting for transfers between devices: 136 us -> 0.02 us  [shards(): lax.psum_scatter(feed_grad, ('dp', 'fsdp'), scatter_dimension=0, tiled=True)]
    psum x3 -> x0, blocking collectives: 114 us -> none  [the longest x1 50.5 us: shards(): lax.psum(jnp.concatenate([beta_part.reshape(chunks, LANES), gamma_part.re...]
    pallas_call x0 -> x6, Pallas kernels: none -> 96.8 us  [the longest x1 36.4 us: reduce_gradients(): pl.pallas_call(functools.partial(reduce_kernel, counts), out_shape=(shape...]
    psum x1 -> x0, waiting for transfers between devices: 36.2 us -> none  [shards(): lax.psum((portion_derivative, catalog_portion, sharpness_normalizer), 'dp')]
    unnamed x8 -> x2, waiting for transfers between devices: 26.6 us -> 0.03 us
    all_gather x1 -> x0, blocking collectives: 25.6 us -> none  [shards(): lax.all_gather(channel_coefficients.astype(BF16), 'fsdp', axis=1, tiled=T...]
    unnamed x1 -> x0, blocking collectives: 16.1 us -> none
  transfers between devices with their start and end apart: 7 -> 2, of which waited for: 6 -> 0; matrix products, arithmetic and copies ran while one was open for 4% -> 0% of each run, Pallas kernels for 7% -> 59%
where the time goes in v2:
time: 448 us; the launch traced here: 447 us
  Pallas kernels  424 us (95%)
  between operations  14.2 us (3%)
  local copies, waits for them, and re-layouts  7.43 us (2%)
    pallas_call x1, Pallas kernels, mixing_backward(): pl.pallas_call(mixing_backward_kernel, out_shape=(shape((row_count, width...  147 us
    pallas_call x1, Pallas kernels, feed_forward(): pl.pallas_call(feed_kernel, out_shape=(shape((row_count, width), BF16), s...  102 us
    pallas_call x1, Pallas kernels, mixing_forward(): pl.pallas_call(mixing_forward_kernel, out_shape=(shape((row_count, width)...  77.9 us
    pallas_call x1, Pallas kernels, reduce_gradients(): pl.pallas_call(functools.partial(reduce_kernel, counts), out_shape=(shape...  36.4 us
    pallas_call x2, Pallas kernels, sum_all(): pl.pallas_call(functools.partial(sum_all_kernel, counts), out_shape=jax.S...  20.7 us
    pallas_call x1, Pallas kernels, gather_start(): pl.pallas_call(functools.partial(gather_kernel, counts), out_shape=(shape...  20.3 us
    pallas_call x1, Pallas kernels, return_steps(): pl.pallas_call(functools.partial(return_kernel, counts), out_shape=jax.Sh...  13.7 us
  transfers between devices with their start and end apart: 2, of which 0 were waited for; matrix products, arithmetic and copies ran while one was open for 0% of the time, Pallas kernels for 59%

profile of v2, /device:TPU:1, one launch (start us, length us, event | category | flops | bytes accessed | tf_op | source)
XLA Modules:
  0.0 447.1 jit_solution(4831838834845659103)
XLA Ops:
  7.2 0.0 all-gather.2.cloned.1.call-start
  7.2 1.8 slice.9
  9.0 0.0 all-gather.2.cloned.1.call-update
  9.1 0.0 reduce-scatter.2.cloned.1.call-start
  9.1 20.3 %gather_start.1 = (bf16[4,384,384]{2,1,0:T(8,128)(2,1)}, f32[32,384]{1,0:T(8,128)}) custom-call(f32[12,48,384]{2,1,0:T(8,128)} %masters_ref.1, f32[29,48]{1,0:T(8,128)} %coefficient_ref.1), custom_call_target="tpu_custom_call" | custom-call | tf_op jit(solution)/shard_map/gather_start/pallas_call | solution.py:1117
  29.4 77.9 %mixing_forward.1 = (f32[1856,384]{1,0:T(8,128)}, f32[1856,1536]{1,0:T(8,128)}, bf16[1856,512]{1,0:T(8,128)(2,1)}, f32[16,4,48,128]{3,2,1,0:T(8,128)}, f32[16,4,...) custom-call(s32[16]{0:T(128)} %sides_ref.5, f32[8]{0:T(128)} %sharp_ref.3, ...), custom_call_target="tpu_custom_call" | custom-call | tf_op jit(solution)/shard_map/mixing_forward/pallas_call | solution.py:391
  107.3 13.0 %sum_all.2.bn_ref = f32[8,128]{1,0:T(8,128)} custom-call(f32[8,128]{1,0:T(8,128)} %get-tuple-element.45.part_ref), custom_call_target="tpu_custom_call" | custom-call | tf_op jit(solution)/shard_map/sum_all/pallas_call | solution.py:1016
  120.3 0.0 all-gather.2.cloned.1.call-done.weight_ref
  120.3 102.1 %feed_forward.1 = (bf16[1856,384]{1,0:T(8,128)(2,1)}, f32[1856,384]{1,0:T(8,128)}, f32[3,1856,128]{2,1,0:T(8,128)}, bf16[32,2,48,384]{3,2,1,0:T(8,128)(2,1)}, f32[16,384]{1,0:T(8,128)}, /*index=5*/f32[8,128]{1,0:T(8,128)}) custom-call(s32[16]{0:T(128)} %sides_ref.5, f32[1856,384]{1,0:T(8,128)} %get-tuple-element.43.x1_ref, ...), custom_call_target="tpu_custom_call" | custom-call | tf_op jit(solution)/shard_map/feed_forward/pallas_call | solution.py:625
  222.4 0.0 copy-start.5
  222.4 0.0 copy-start.8
  222.4 0.0 copy-start.7
  222.4 0.0 reduce-scatter.2.cloned.1.call-update
  222.4 0.6 copy-done.5
  223.0 0.0 copy-done.8
  223.1 0.6 pad_maximum_fusion.sharp_ref
  223.6 0.0 copy-done.7
  223.7 7.7 %sum_all.3.back_ref = f32[8,128]{1,0:T(8,128)} custom-call(f32[8,128]{1,0:T(8,128)} %get-tuple-element.54.part_ref), custom_call_target="tpu_custom_call" | custom-call | tf_op jit(solution)/shard_map/sum_all/pallas_call | solution.py:1016
  231.4 146.8 %mixing_backward.1 = (bf16[1856,384]{1,0:T(8,128)(2,1)}, bf16[4,384,384]{2,1,0:T(8,128)(2,1)}, f32[16,384]{1,0:T(8,128)}) custom-call(s32[16]{0:T(128)} %sides_ref.5, f32[8]{0:T(128)} %sharp_ref.3, bf16[1856,384]{1,0:T(8,128)(2,1)} %input_ref.3, bf16[4,384,384]{2,1,0:T(8,128)(2,1)} %get-tuple-element.41.weight_ref, f32[32,384]{1,0:T(8,128)} %get-tuple-element.42.table_ref, ...), custom_call_target="tpu_custom_call" | custom-call | tf_op jit(solution)/shard_map/mixing_backward/pallas_call | solution.py:899
  378.2 0.0 reduce-scatter.2.cloned.1.call-done
  378.2 36.4 %reduce_gradients.1 = (f32[12,48,384]{2,1,0:T(8,128)}, bf16[2,384,384]{2,1,0:T(8,128)(2,1)}, f32[29,48]{1,0:T(8,128)}, f32[29,48]{1,0:T(8,128)}, f32[29,48]{1,0:T(8,128)}, /*index=5*/f32[3,8]{1,0:T(4,128)}) custom-call(s32[12]{0:T(128)} %place_ref.1, bf16[4,384,384]{2,1,0:T(8,128)(2,1)} %get-tuple-element.56.mix_ref, bf16[2,48,384]{2,1,0:T(8,128)(2,1)} %bitcast.9, ...), custom_call_target="tpu_custom_call" | custom-call | tf_op jit(solution)/shard_map/reduce_gradients/pallas_call | solution.py:1404
  414.6 0.0 copy-start.6
  414.6 5.7 %shampoo.1 = (f32[2,384,384]{2,1,0:T(8,128)}, f32[2,384,384]{2,1,0:T(8,128)}, bf16[2,384,384]{2,1,0:T(8,128)(2,1)}) custom-call(bf16[2,384,384]{2,1,0:T(8,128)(2,1)} %get-tuple-element.61.grad_ref, f32[2,384,384]{2,1,0:T(8,128)} %left_ref.1, f32[2,384,384]{2,1,0:T(8,128)} %right_ref.1, f32[2,384,384]{2,1,0:T(8,128)} %left_root.1, f32[2,384,384]{2,1,0:T(8,128)} %right_root.1), custom_call_target="tpu_custom_call" | custom-call | tf_op jit(solution)/shard_map/shampoo/pallas_call | solution.py:1472
  420.3 0.0 copy-start
  420.3 13.7 %return_steps.1 = bf16[16,48,384]{2,1,0:T(8,128)(2,1)} custom-call(bf16[2,384,384]{2,1,0:T(8,128)(2,1)} %get-tuple-element.64.steps_ref), custom_call_target="tpu_custom_call" | custom-call | tf_op jit(solution)/shard_map/return_steps/pallas_call | solution.py:1528
  434.0 0.0 copy-done.6
  434.0 0.5 slice_bitcast_fusion
  434.5 1.7 gather_fusion
  436.3 0.0 copy-done
  436.3 0.0 copy-start.1
  436.3 1.3 fusion
  437.5 0.0 copy-start.4
  437.5 0.0 copy-start.3
  437.6 0.0 copy-start.2
  437.6 0.0 copy-done.1
  437.6 0.9 copy.30
  438.5 0.0 copy-done.4
  438.5 0.6 copy.31
  439.1 0.0 copy-done.3
  439.1 0.6 copy.32
  439.7 0.0 copy-done.2
  439.7 0.6 copy.33
  (3 shorter events, 0.0 us)
Async XLA Ops:
  7.2 113.1 %all-gather.2.cloned.1.call-start = ((), (), s32[]{:S(2)}) async-start(), calls=%async_computation.1 | async-start | bytes 2654208 | tf_op jit(solution)/shard_map/all_gather | solution.py:1576
  9.1 369.1 %reduce-scatter.2.cloned.1.call-start = ((), (), s32[]{:S(2)}) async-start(), calls=%async_computation.2 | async-start | bytes 2433024 | tf_op jit(solution)/shard_map/reduce_scatter | solution.py:1604
  222.4 0.7 copy-start.5
  222.4 0.7 copy-start.8
  222.4 1.2 copy-start.7
  414.6 19.4 %copy-start.6 = (f32[3,8]{1,0:T(4,128)S(1)}, f32[3,8]{1,0:T(4,128)}, u32[]{:S(2)}) copy-start(f32[3,8]{1,0:T(4,128)} %get-tuple-element.68) | copy-start | bytes 292
  420.3 15.9 %copy-start = (f32[12,48,384]{2,1,0:T(8,128)S(1)}, f32[12,48,384]{2,1,0:T(8,128)}, u32[]{:S(2)}) copy-start(f32[12,48,384]{2,1,0:T(8,128)} %masters_ref.1) | copy-start | bytes 2654212
  436.3 1.3 copy-start.1
  437.5 0.9 copy-start.4
  437.5 1.5 copy-start.3
  437.6 2.1 copy-start.2
Sparse Core Ops, SparseCore 0:
  10.8 53.8 all-gather.1
  222.6 95.6 reduce-scatter.1

commit v3 on v2

--- a/solution.py
+++ b/solution.py
@@ -18,6 +18,8 @@
 TAIL = 32
 SMALL_WINDOW = 48
 LARGE_WINDOW = 208
+ROW_TILE = 464
+GELU_TILE = 128
 VMEM_LIMIT = 58 * 2**20
 
 norm_epsilon = 1e-06
@@ -113,6 +115,16 @@
         if count % (16 * parts) == 0:
             return count // parts
     return count
+
+
+def for_rows(count, tile, step, carry=0):
+    def body(index, carry):
+        return step(pl.multiple_of(index * tile, tile), tile, carry)
+
+    carry = lax.fori_loop(0, count // tile, body, carry)
+    if count % tile:
+        carry = step(count - count % tile, count % tile, carry)
+    return carry
 
 
 def live_total(sides_ref):
@@ -298,14 +310,14 @@
         ).astype(BF16)
     spread[...] = jnp.zeros_like(spread)
 
-    def first_norm(step, _):
-        rows = pl.ds(pl.multiple_of(step * 32, 32), 32)
+    def first_norm(first, size, _):
+        rows = pl.ds(first, size)
         unit, _ = centered(input_ref[rows, :].astype(F32))
         first_low[rows, :] = (unit * table_ref[0:1, :] + table_ref[1:2, :]).astype(BF16)
-        mixed[rows, :] = jnp.zeros((32, PAD_WIDTH), F32)
+        mixed[rows, :] = jnp.zeros((size, PAD_WIDTH), F32)
         return 0
 
-    lax.fori_loop(0, row_count // 32, first_norm, 0)
+    for_rows(row_count, ROW_TILE, first_norm)
 
     @pl.loop(0, row_count // tile)
     def _(step):
@@ -347,39 +359,41 @@
         mixed_ref[rows, :] = low
         attention_out[rows, :] = dot(low, out_weight[...])
 
-    def second_norm(step, _):
-        first = pl.multiple_of(step * 32, 32)
-        rows = pl.ds(first, 32)
+    def second_norm(first, size, _):
+        rows = pl.ds(first, size)
         value = input_ref[rows, :].astype(F32) + table_ref[2:3, :] * attention_out[rows, :]
         x1_ref[rows, :] = value
         unit, _ = centered(value)
         value = unit * table_ref[3:4, :] + table_ref[4:5, :]
         for chunk in range(chunks):
-            conv_in[chunk, pl.ds(LEAD + first, 32), :] = value[:, chunk_lanes(chunk)]
-            u_ref[chunk, rows, :] = jnp.zeros((32, LANES), F32)
-            e_ref[chunk, rows, :] = jnp.zeros((32, LANES), F32)
+            conv_in[chunk, pl.ds(LEAD + first, size), :] = value[:, chunk_lanes(chunk)]
+            u_ref[chunk, rows, :] = jnp.zeros((size, LANES), F32)
+            e_ref[chunk, rows, :] = jnp.zeros((size, LANES), F32)
         return 0
 
-    lax.fori_loop(0, row_count // 32, second_norm, 0)
+    for_rows(row_count, ROW_TILE, second_norm)
 
     zero = jnp.zeros((8, LANES), F32)
     sums_ref[...] = zero
-    for chunk in range(chunks):
-        taps = tap_vectors(table_ref, 11, chunk)
-
-        def conv_step(row, side, masks, carry, chunk=chunk, taps=taps):
-            value = conv_forward(conv_in, chunk, row, side, masks, taps)
+    taps = [tap_vectors(table_ref, 11, chunk) for chunk in range(chunks)]
+
+    def conv_step(row, side, masks, carry):
+        rows = pl.ds(row, 8)
+        carry = list(carry)
+        for chunk in range(chunks):
+            value = conv_forward(conv_in, chunk, row, side, masks, taps[chunk])
             share, _ = gelu_parts(value)
             active = value * share
-            rows = pl.ds(row, 8)
             u_ref[chunk, rows, :] = jnp.where(masks[0], value, u_ref[chunk, rows, :])
             e_ref[chunk, rows, :] = jnp.where(masks[0], active, e_ref[chunk, rows, :])
             active = jnp.where(masks[0], active, 0.0)
-            return carry[0] + active, carry[1] + active * active
-
-        plain, square = for_groups(sides_ref, conv_step, (zero, zero))
-        sums_ref[chunk : chunk + 1, :] = jnp.sum(plain, axis=0, keepdims=True)
-        sums_ref[chunks + chunk : chunks + chunk + 1, :] = jnp.sum(square, axis=0, keepdims=True)
+            carry[chunk] = carry[chunk] + active
+            carry[chunks + chunk] = carry[chunks + chunk] + active * active
+        return tuple(carry)
+
+    sums = for_groups(sides_ref, conv_step, (zero,) * (2 * chunks))
+    for index, value in enumerate(sums):
+        sums_ref[index : index + 1, :] = jnp.sum(value, axis=0, keepdims=True)
     sums_ref[2 * chunks : 2 * chunks + 1, :] = jnp.full((1, LANES), total_live, jnp.int32).astype(F32)
 
 
@@ -460,32 +474,31 @@
     batch = [batch_vectors(bn_ref, chunk, chunks) for chunk in range(chunks)]
     zero = jnp.zeros((8, LANES), F32)
 
-    def normalize(step, _):
-        first = pl.multiple_of(step * 32, 32)
-        rows = pl.ds(first, 32)
-        live = row_mask(first, 32, LANES, total_live)
+    def normalize(first, size, _):
+        rows = pl.ds(first, size)
+        live = row_mask(first, size, LANES, total_live)
         for chunk in range(chunks):
             lanes = chunk_lanes(chunk)
             mean, scale = batch[chunk]
             value = (e_ref[chunk, rows, :] - mean) * scale
             value = value * table_ref[5:6, lanes] + table_ref[6:7, lanes]
-            n_ref[chunk, pl.ds(LEAD + first, 32), :] = jnp.where(live, value, 0.0)
-            z_ref[chunk, rows, :] = jnp.zeros((32, LANES), F32)
-            dn_ref[chunk, rows, :] = jnp.zeros((32, LANES), F32)
+            n_ref[chunk, pl.ds(LEAD + first, size), :] = jnp.where(live, value, 0.0)
+            z_ref[chunk, rows, :] = jnp.zeros((size, LANES), F32)
+            dn_ref[chunk, rows, :] = jnp.zeros((size, LANES), F32)
         return 0
 
-    lax.fori_loop(0, row_count // 32, normalize, 0)
-
-    for chunk in range(chunks):
-        taps = tap_vectors(table_ref, 20, chunk)
-
-        def conv_step(row, side, masks, carry, chunk=chunk, taps=taps):
-            value = conv_forward(n_ref, chunk, row, side, masks, taps)
-            rows = pl.ds(row, 8)
+    for_rows(row_count, ROW_TILE, normalize)
+
+    taps = [tap_vectors(table_ref, 20, chunk) for chunk in range(chunks)]
+
+    def conv_step(row, side, masks, carry):
+        rows = pl.ds(row, 8)
+        for chunk in range(chunks):
+            value = conv_forward(n_ref, chunk, row, side, masks, taps[chunk])
             z_ref[chunk, rows, :] = jnp.where(masks[0], value, z_ref[chunk, rows, :])
-            return carry
-
-        for_groups(sides_ref, conv_step, 0)
+        return carry
+
+    for_groups(sides_ref, conv_step, 0)
 
     weight_sums[...] = jnp.zeros_like(weight_sums)
     grads[...] = jnp.zeros_like(grads)
@@ -497,24 +510,23 @@
     def _(step):
         base = pl.multiple_of(step * tile, 16)
 
-        def before(sub, _):
-            inner = pl.multiple_of(sub * 16, 16)
-            near, rows = pl.ds(inner, 16), pl.ds(base + inner, 16)
+        def before(inner, size, _):
+            near, rows = pl.ds(inner, size), pl.ds(base + inner, size)
             value = x1_ref[rows, :] + table_ref[7:8, :] * z_rows(rows)
             x2[near, :] = value
             value, scale = centered(value)
             unit[near, :] = value
-            spread[near, :] = jnp.broadcast_to(scale, (16, LANES))
+            spread[near, :] = jnp.broadcast_to(scale, (size, LANES))
             third_low[near, :] = (value * table_ref[8:9, :] + table_ref[9:10, :]).astype(BF16)
             return 0
 
-        lax.fori_loop(0, tile // 16, before, 0)
+        for_rows(tile, ROW_TILE, before)
         for part in range(expand):
             lanes = slice(part * width, (part + 1) * width)
             pre[:, lanes] = dot(third_low[...], weight_ref[part])
 
-        def activate(sub, _):
-            near = pl.ds(pl.multiple_of(sub * 16, 16), 16)
+        def activate(inner, size, _):
+            near = pl.ds(inner, size)
             for part in range(expand):
                 lanes = slice(part * width, (part + 1) * width)
                 value = pre[near, lanes]
@@ -523,7 +535,7 @@
                 pre[near, lanes] = gelu_slope(value, share, bell)
             return 0
 
-        lax.fori_loop(0, tile // 16, activate, 0)
+        for_rows(tile, GELU_TILE, activate)
         total = None
         for part in range(expand):
             lanes = slice(part * width, (part + 1) * width)
@@ -531,17 +543,16 @@
             total = term if total is None else total + term
         feed[...] = total
 
-        def output(sub, carry):
-            inner = pl.multiple_of(sub * 16, 16)
-            near, rows = pl.ds(inner, 16), pl.ds(base + inner, 16)
-            live = row_mask(base + inner, 16, width, total_live)
+        def output(inner, size, carry):
+            near, rows = pl.ds(inner, size), pl.ds(base + inner, size)
+            live = row_mask(base + inner, size, width, total_live)
             value = x2[near, :] + table_ref[10:11, :] * feed[near, :]
             out_ref[rows, :] = jnp.where(live, value, 0.0).astype(BF16)
             entry = jnp.where(live, adjoint_ref[rows, :].astype(F32), 0.0)
             feed_grad[near, :] = (entry * table_ref[10:11, :]).astype(BF16)
             return carry + fold(entry * feed[near, :])
 
-        grads[0] += lax.fori_loop(0, tile // 16, output, jnp.zeros((8, width), F32))
+        grads[0] += for_rows(tile, ROW_TILE, output, jnp.zeros((8, width), F32))
         for part in range(expand):
             lanes = slice(part * width, (part + 1) * width)
             hidden_grad = dot_lanes(feed_grad[...], weight_ref[expand + part])
@@ -557,10 +568,9 @@
             total = term if total is None else total + term
         feed[...] = total
 
-        def after(sub, carry):
-            inner = pl.multiple_of(sub * 16, 16)
-            near, rows = pl.ds(inner, 16), pl.ds(base + inner, 16)
-            live = row_mask(base + inner, 16, width, total_live)
+        def after(inner, size, carry):
+            near, rows = pl.ds(inner, size), pl.ds(base + inner, size)
+            live = row_mask(base + inner, size, width, total_live)
             entry = jnp.where(live, adjoint_ref[rows, :].astype(F32), 0.0)
             grad = feed[near, :]
             value = unit[near, :]
@@ -568,7 +578,7 @@
             dx2_ref[rows, :] = total
             scaled = total * table_ref[7:8, :]
             for chunk in range(chunks):
-                dw_ref[chunk, pl.ds(LEAD + base + inner, 16), :] = scaled[:, chunk_lanes(chunk)]
+                dw_ref[chunk, pl.ds(LEAD + base + inner, size), :] = scaled[:, chunk_lanes(chunk)]
             return (
                 carry[0] + fold(total * z_rows(rows)),
                 carry[1] + fold(grad * value),
@@ -576,7 +586,7 @@
             )
 
         wide = jnp.zeros((8, width), F32)
-        sums = lax.fori_loop(0, tile // 16, after, (wide, wide, wide))
+        sums = for_rows(tile, ROW_TILE, after, (wide, wide, wide))
         for index in range(3):
             grads[1 + index] += sums[index]
 
@@ -592,22 +602,26 @@
     back_sums_ref[...] = zero
     for index, source in enumerate((1, 2, 3, 0)):
         grads_ref[index : index + 1, :] = jnp.sum(grads[source], axis=0, keepdims=True)
-    for chunk in range(chunks):
-        taps = tap_vectors(table_ref, 20, chunk)
-        mean, scale = batch[chunk]
-
-        def back_step(row, side, masks, carry, chunk=chunk, taps=taps, mean=mean, scale=scale):
+    def back_step(row, side, masks, carry):
+        rows = pl.ds(row, 8)
+        result = []
+        for chunk in range(chunks):
+            mean, scale = batch[chunk]
+            sums = carry[chunk]
             own = jnp.where(masks[0], n_ref[chunk, pl.ds(LEAD + row, 8), :], 0.0)
-            total, tap_sums = conv_backward(dw_ref, chunk, row, side, masks, taps, own, carry[0])
-            rows = pl.ds(row, 8)
+            total, tap_sums = conv_backward(
+                dw_ref, chunk, row, side, masks, taps[chunk], own, sums[0:9]
+            )
             dn_ref[chunk, rows, :] = jnp.where(masks[0], total, dn_ref[chunk, rows, :])
             total = jnp.where(masks[0], total, 0.0)
             standard = (e_ref[chunk, rows, :] - mean) * scale
-            return tap_sums, carry[1] + total * standard, carry[2] + total
-
-        tap_sums, gamma, beta = for_groups(sides_ref, back_step, ((zero,) * 9, zero, zero))
+            result.append((*tap_sums, sums[9] + total * standard, sums[10] + total))
+        return tuple(result)
+
+    sums = for_groups(sides_ref, back_step, ((zero,) * 11,) * chunks)
+    for chunk in range(chunks):
         lanes = chunk_lanes(chunk)
-        for index, value in enumerate((*tap_sums, gamma, beta)):
+        for index, value in enumerate(sums[chunk]):
             value = jnp.sum(value, axis=0, keepdims=True)
             grads_ref[4 + index : 5 + index, lanes] = value
             if index == 9:
@@ -713,10 +727,9 @@
     for load in loads:
         load.wait()
 
-    def batch_back(step, _):
-        first = pl.multiple_of(step * 32, 32)
-        rows = pl.ds(first, 32)
-        live = row_mask(first, 32, LANES, total_live)
+    def batch_back(first, size, _):
+        rows = pl.ds(first, size)
+        live = row_mask(first, size, LANES, total_live)
         unit, _ = centered(x1_ref[rows, :])
         value = unit * table_ref[3:4, :] + table_ref[4:5, :]
         for chunk in range(chunks):
@@ -732,25 +745,30 @@
             ) / count
             grad = scale * table_ref[5:6, lanes] * (dn_ref[chunk, rows, :] - inner)
             grad = grad * gelu_slope(u, share, bell)
-            conv_grad[chunk, pl.ds(LEAD + first, 32), :] = jnp.where(live, grad, 0.0)
-            conv_in[chunk, pl.ds(first, 32), :] = value[:, lanes]
+            conv_grad[chunk, pl.ds(LEAD + first, size), :] = jnp.where(live, grad, 0.0)
+            conv_in[chunk, pl.ds(first, size), :] = value[:, lanes]
         return 0
 
-    lax.fori_loop(0, row_count // 32, batch_back, 0)
-
-    for chunk in range(chunks):
-        taps = tap_vectors(table_ref, 11, chunk)
-
-        def back_step(row, side, masks, carry, chunk=chunk, taps=taps):
-            rows = pl.ds(row, 8)
+    for_rows(row_count, ROW_TILE, batch_back)
+
+    taps = [tap_vectors(table_ref, 11, chunk) for chunk in range(chunks)]
+
+    def back_step(row, side, masks, carry):
+        rows = pl.ds(row, 8)
+        result = []
+        for chunk in range(chunks):
             held = conv_in[chunk, rows, :]
             own = jnp.where(masks[0], held, 0.0)
-            total, tap_sums = conv_backward(conv_grad, chunk, row, side, masks, taps, own, carry)
+            total, tap_sums = conv_backward(
+                conv_grad, chunk, row, side, masks, taps[chunk], own, carry[chunk]
+            )
             conv_in[chunk, rows, :] = jnp.where(masks[0], total, held)
-            return tap_sums
-
-        tap_sums = for_groups(sides_ref, back_step, (zero,) * 9)
-        for index, value in enumerate(tap_sums):
+            result.append(tap_sums)
+        return tuple(result)
+
+    tap_sums = for_groups(sides_ref, back_step, ((zero,) * 9,) * chunks)
+    for chunk in range(chunks):
+        for index, value in enumerate(tap_sums[chunk]):
             grads_ref[5 + index : 6 + index, chunk_lanes(chunk)] = jnp.sum(
                 value, axis=0, keepdims=True
             )
@@ -762,10 +780,9 @@
         for chunk in range(chunks):
             attention_out[chunk, rows, :] = result[:, chunk_lanes(chunk)]
 
-    def second_back(step, carry):
-        first = pl.multiple_of(step * 16, 16)
-        rows = pl.ds(first, 16)
-        live = row_mask(first, 16, width, total_live)
+    def second_back(first, size, carry):
+        rows = pl.ds(first, size)
+        live = row_mask(first, size, width, total_live)
         grad = jnp.concatenate([conv_in[chunk, rows, :] for chunk in range(chunks)], axis=1)
         grad = jnp.where(live, grad, 0.0)
         unit, scale = centered(x1_ref[rows, :])
@@ -779,7 +796,7 @@
             carry[2] + fold(grad),
         )
 
-    sums = lax.fori_loop(0, row_count // 16, second_back, (wide, wide, wide))
+    sums = for_rows(row_count, ROW_TILE, second_back, (wide, wide, wide))
     for index in range(3):
         grads_ref[2 + index : 3 + index, :] = jnp.sum(sums[index], axis=0, keepdims=True)
 
@@ -847,13 +864,13 @@
         total = jnp.where(lane == head, jnp.sum(row, axis=1, keepdims=True), total)
     grads_ref[14:15, 0:LANES] = total
 
-    def first_norm(step, _):
-        rows = pl.ds(pl.multiple_of(step * 32, 32), 32)
+    def first_norm(first, size, _):
+        rows = pl.ds(first, size)
         unit, _ = centered(input_ref[rows, :].astype(F32))
         low_rows[rows, :] = (unit * table_ref[0:1, :] + table_ref[1:2, :]).astype(BF16)
         return 0
 
-    lax.fori_loop(0, row_count // 32, first_norm, 0)
+    for_rows(row_count, ROW_TILE, first_norm)
 
     for part in range(3):
         lanes = slice(part * PAD_WIDTH, (part + 1) * PAD_WIDTH)
@@ -878,15 +895,15 @@
             low, mapping, (((0,), (1,)), ((), ())), preferred_element_type=F32
         ).astype(BF16)
 
-    def first_back(step, carry):
-        rows = pl.ds(pl.multiple_of(step * 16, 16), 16)
+    def first_back(first, size, carry):
+        rows = pl.ds(first, size)
         unit, scale = centered(input_ref[rows, :].astype(F32))
         grad = mixed_grad[rows, 0:width]
         total = dx1[rows, :] + norm_back(grad * table_ref[0:1, :], unit, scale)
         out_ref[rows, :] = total.astype(BF16)
         return carry[0] + fold(grad * unit), carry[1] + fold(grad)
 
-    sums = lax.fori_loop(0, row_count // 16, first_back, (wide, wide))
+    sums = for_rows(row_count, ROW_TILE, first_back, (wide, wide))
     for index in range(2):
         grads_ref[index : index + 1, :] = jnp.sum(sums[index], axis=0, keepdims=True)
 

time: 448 us -> 319 us (0.71)
  Pallas kernels: 424 us -> 275 us
  waiting for transfers between devices: 0.08 us -> 19.3 us
    pallas_call x1, Pallas kernels: 147 us -> 66 us  [mixing_backward(): pl.pallas_call(mixing_backward_kernel, out_shape=(shape((row_count, width...]
    pallas_call x1, Pallas kernels: 102 us -> 51 us  [feed_forward(): pl.pallas_call(feed_kernel, out_shape=(shape((row_count, width), BF16), s...]
    pallas_call x1, Pallas kernels: 77.9 us -> 41.7 us  [mixing_forward(): pl.pallas_call(mixing_forward_kernel, out_shape=(shape((row_count, width)...]
    reduce_scatter x1, waiting for transfers between devices: 0.02 us -> 19.2 us  [shards(): lax.psum_scatter(feed_grad, ('dp', 'fsdp'), scatter_dimension=0, tiled=True)]
    pallas_call x2, Pallas kernels: 20.7 us -> 38.4 us  [sum_all(): pl.pallas_call(functools.partial(sum_all_kernel, counts), out_shape=jax.S...]
  transfers between devices with their start and end apart: 2 -> 2, of which waited for: 0 -> 1; matrix products, arithmetic and copies ran while one was open for 0% -> 0% of each run, Pallas kernels for 59% -> 52%
where the time goes in v3:
time: 319 us; the launch traced here: 318 us
  Pallas kernels  275 us (86%)
  waiting for transfers between devices  19.3 us (6%)
  between operations  14.2 us (4%)
  local copies, waits for them, and re-layouts  7.43 us (2%)
    pallas_call x1, Pallas kernels, mixing_backward(): pl.pallas_call(mixing_backward_kernel, out_shape=(shape((row_count, width...  66 us
    pallas_call x1, Pallas kernels, feed_forward(): pl.pallas_call(feed_kernel, out_shape=(shape((row_count, width), BF16), s...  51 us
    pallas_call x1, Pallas kernels, mixing_forward(): pl.pallas_call(mixing_forward_kernel, out_shape=(shape((row_count, width)...  41.7 us
    pallas_call x2, Pallas kernels, sum_all(): pl.pallas_call(functools.partial(sum_all_kernel, counts), out_shape=jax.S...  38.4 us
    pallas_call x1, Pallas kernels, reduce_gradients(): pl.pallas_call(functools.partial(reduce_kernel, counts), out_shape=(shape...  38 us
    pallas_call x1, Pallas kernels, gather_start(): pl.pallas_call(functools.partial(gather_kernel, counts), out_shape=(shape...  20.3 us
    reduce_scatter x1, waiting for transfers between devices, shards(): lax.psum_scatter(feed_grad, ('dp', 'fsdp'), scatter_dimension=0, tiled=True)  19.2 us
    pallas_call x1, Pallas kernels, return_steps(): pl.pallas_call(functools.partial(return_kernel, counts), out_shape=jax.Sh...  14.4 us
  transfers between devices with their start and end apart: 2, of which 1 were waited for; matrix products, arithmetic and copies ran while one was open for 0% of the time, Pallas kernels for 52%

profile of v3, /device:TPU:1, one launch (start us, length us, event | category | flops | bytes accessed | tf_op | source)
XLA Modules:
  0.0 318.2 jit_solution(17592056092271295182)
XLA Ops:
  7.2 0.0 all-gather.2.cloned.1.call-start
  7.2 1.8 slice.9
  9.0 0.0 all-gather.2.cloned.1.call-update
  9.1 0.0 reduce-scatter.2.cloned.1.call-start
  9.1 20.3 %gather_start.1 = (bf16[4,384,384]{2,1,0:T(8,128)(2,1)}, f32[32,384]{1,0:T(8,128)}) custom-call(f32[12,48,384]{2,1,0:T(8,128)} %masters_ref.1, f32[29,48]{1,0:T(8,128)} %coefficient_ref.1), custom_call_target="tpu_custom_call" | custom-call | tf_op jit(solution)/shard_map/gather_start/pallas_call | solution.py:1134
  29.4 41.7 %mixing_forward.1 = (f32[1856,384]{1,0:T(8,128)}, f32[1856,1536]{1,0:T(8,128)}, bf16[1856,512]{1,0:T(8,128)(2,1)}, f32[16,4,48,128]{3,2,1,0:T(8,128)}, f32[16,4,...) custom-call(s32[16]{0:T(128)} %sides_ref.5, f32[8]{0:T(128)} %sharp_ref.3, ...), custom_call_target="tpu_custom_call" | custom-call | tf_op jit(solution)/shard_map/mixing_forward/pallas_call | solution.py:405
  71.0 21.0 %sum_all.2.bn_ref = f32[8,128]{1,0:T(8,128)} custom-call(f32[8,128]{1,0:T(8,128)} %get-tuple-element.45.part_ref), custom_call_target="tpu_custom_call" | custom-call | tf_op jit(solution)/shard_map/sum_all/pallas_call | solution.py:1033
  92.1 0.0 all-gather.2.cloned.1.call-done.weight_ref
  92.1 51.0 %feed_forward.1 = (bf16[1856,384]{1,0:T(8,128)(2,1)}, f32[1856,384]{1,0:T(8,128)}, f32[3,1856,128]{2,1,0:T(8,128)}, bf16[32,2,48,384]{3,2,1,0:T(8,128)(2,1)}, f32[16,384]{1,0:T(8,128)}, /*index=5*/f32[8,128]{1,0:T(8,128)}) custom-call(s32[16]{0:T(128)} %sides_ref.5, f32[1856,384]{1,0:T(8,128)} %get-tuple-element.43.x1_ref, ...), custom_call_target="tpu_custom_call" | custom-call | tf_op jit(solution)/shard_map/feed_forward/pallas_call | solution.py:639
  143.0 0.0 copy-start.5
  143.1 0.0 copy-start.8
  143.1 0.0 copy-start.7
  143.1 0.0 reduce-scatter.2.cloned.1.call-update
  143.1 0.6 copy-done.5
  143.7 0.0 copy-done.8
  143.7 0.6 pad_maximum_fusion.sharp_ref
  144.3 0.0 copy-done.7
  144.3 17.4 %sum_all.3.back_ref = f32[8,128]{1,0:T(8,128)} custom-call(f32[8,128]{1,0:T(8,128)} %get-tuple-element.54.part_ref), custom_call_target="tpu_custom_call" | custom-call | tf_op jit(solution)/shard_map/sum_all/pallas_call | solution.py:1033
  161.7 66.0 %mixing_backward.1 = (bf16[1856,384]{1,0:T(8,128)(2,1)}, bf16[4,384,384]{2,1,0:T(8,128)(2,1)}, f32[16,384]{1,0:T(8,128)}) custom-call(s32[16]{0:T(128)} %sides_ref.5, f32[8]{0:T(128)} %sharp_ref.3, bf16[1856,384]{1,0:T(8,128)(2,1)} %input_ref.3, bf16[4,384,384]{2,1,0:T(8,128)(2,1)} %get-tuple-element.41.weight_ref, f32[32,384]{1,0:T(8,128)} %get-tuple-element.42.table_ref, ...), custom_call_target="tpu_custom_call" | custom-call | tf_op jit(solution)/shard_map/mixing_backward/pallas_call | solution.py:916
  227.8 19.2 %reduce-scatter.2.cloned.1.call-done = bf16[1,2,48,384]{3,2,1,0:T(8,128)(2,1)} async-done(((bf16[32,2,48,384]{3,2,1,0:T(8,128)(2,1)}), bf16[1,2,48,384]{3,2,1,0:T(8,128)(2,1)}) %reduce-scatter.2.cloned.1.call-update) | async-done | bytes 73744 | tf_op jit(solution)/shard_map/reduce_scatter | solution.py:1621
  247.0 38.0 %reduce_gradients.1 = (f32[12,48,384]{2,1,0:T(8,128)}, bf16[2,384,384]{2,1,0:T(8,128)(2,1)}, f32[29,48]{1,0:T(8,128)}, f32[29,48]{1,0:T(8,128)}, f32[29,48]{1,0:T(8,128)}, /*index=5*/f32[3,8]{1,0:T(4,128)}) custom-call(s32[12]{0:T(128)} %place_ref.1, bf16[4,384,384]{2,1,0:T(8,128)(2,1)} %get-tuple-element.56.mix_ref, bf16[2,48,384]{2,1,0:T(8,128)(2,1)} %bitcast.9, ...), custom_call_target="tpu_custom_call" | custom-call | tf_op jit(solution)/shard_map/reduce_gradients/pallas_call | solution.py:1421
  284.9 0.0 copy-start.6
  285.0 5.7 %shampoo.1 = (f32[2,384,384]{2,1,0:T(8,128)}, f32[2,384,384]{2,1,0:T(8,128)}, bf16[2,384,384]{2,1,0:T(8,128)(2,1)}) custom-call(bf16[2,384,384]{2,1,0:T(8,128)(2,1)} %get-tuple-element.61.grad_ref, f32[2,384,384]{2,1,0:T(8,128)} %left_ref.1, f32[2,384,384]{2,1,0:T(8,128)} %right_ref.1, f32[2,384,384]{2,1,0:T(8,128)} %left_root.1, f32[2,384,384]{2,1,0:T(8,128)} %right_root.1), custom_call_target="tpu_custom_call" | custom-call | tf_op jit(solution)/shard_map/shampoo/pallas_call | solution.py:1489
  290.7 0.0 copy-start
  290.7 14.4 %return_steps.1 = bf16[16,48,384]{2,1,0:T(8,128)(2,1)} custom-call(bf16[2,384,384]{2,1,0:T(8,128)(2,1)} %get-tuple-element.64.steps_ref), custom_call_target="tpu_custom_call" | custom-call | tf_op jit(solution)/shard_map/return_steps/pallas_call | solution.py:1545
  305.1 0.0 copy-done.6
  305.1 0.5 slice_bitcast_fusion
  305.6 1.7 gather_fusion
  307.4 0.0 copy-done
  307.4 0.0 copy-start.1
  307.4 1.3 fusion
  308.6 0.0 copy-start.4
  308.6 0.0 copy-start.3
  308.6 0.0 copy-start.2
  308.6 0.0 copy-done.1
  308.6 0.9 copy.30
  309.6 0.0 copy-done.4
  309.6 0.6 copy.31
  310.2 0.0 copy-done.3
  310.2 0.6 copy.32
  310.8 0.0 copy-done.2
  310.8 0.6 copy.33
  (3 shorter events, 0.0 us)
Async XLA Ops:
  7.2 84.9 %all-gather.2.cloned.1.call-start = ((), (), s32[]{:S(2)}) async-start(), calls=%async_computation.1 | async-start | bytes 2654208 | tf_op jit(solution)/shard_map/all_gather | solution.py:1593
  9.1 237.9 %reduce-scatter.2.cloned.1.call-start = ((), (), s32[]{:S(2)}) async-start(), calls=%async_computation.2 | async-start | bytes 2433024 | tf_op jit(solution)/shard_map/reduce_scatter | solution.py:1621
  143.0 0.7 copy-start.5
  143.1 0.7 copy-start.8
  143.1 1.2 copy-start.7
  284.9 20.2 %copy-start.6 = (f32[3,8]{1,0:T(4,128)S(1)}, f32[3,8]{1,0:T(4,128)}, u32[]{:S(2)}) copy-start(f32[3,8]{1,0:T(4,128)} %get-tuple-element.68) | copy-start | bytes 292
  290.7 16.7 %copy-start = (f32[12,48,384]{2,1,0:T(8,128)S(1)}, f32[12,48,384]{2,1,0:T(8,128)}, u32[]{:S(2)}) copy-start(f32[12,48,384]{2,1,0:T(8,128)} %masters_ref.1) | copy-start | bytes 2654212
  307.4 1.3 copy-start.1
  308.6 0.9 copy-start.4
  308.6 1.5 copy-start.3
  308.6 2.1 copy-start.2
Sparse Core Ops, SparseCore 0:
  10.8 53.3 all-gather.1
  143.2 103.7 reduce-scatter.1

commit v4 on v3

--- a/solution.py
+++ b/solution.py
@@ -16,8 +16,10 @@
 HALF_WIDTH = PAD_WIDTH // 2
 LEAD = 16
 TAIL = 32
+SMALL_SIDE = 6
 SMALL_WINDOW = 48
 LARGE_WINDOW = 208
+CROP_GROUP = 2
 ROW_TILE = 464
 GELU_TILE = 128
 VMEM_LIMIT = 58 * 2**20
@@ -56,9 +58,14 @@
 
 
 def dot_split(product, left, right):
-    return (
-        product(left[0], right[0]) + product(left[0], right[1]) + product(left[1], right[0])
-    )
+    if product is dot_rows:
+        return product(
+            jnp.concatenate([left[0], left[0], left[1]], axis=0),
+            jnp.concatenate([right[0], right[1], right[0]], axis=0),
+        )
+    rows = left[0].shape[0]
+    both = product(jnp.concatenate(left, axis=0), right[0])
+    return both[:rows] + both[rows:] + product(left[0], right[1])
 
 
 def fold(values):
@@ -110,8 +117,8 @@
     return scale * (grad - middle - unit * slope)
 
 
-def tile_rows(count):
-    for parts in range(4, count // 16 + 1):
+def tile_rows(count, least):
+    for parts in range(least, count // 16 + 1):
         if count % (16 * parts) == 0:
             return count // parts
     return count
@@ -121,7 +128,10 @@
     def body(index, carry):
         return step(pl.multiple_of(index * tile, tile), tile, carry)
 
-    carry = lax.fori_loop(0, count // tile, body, carry)
+    if count // tile == 1:
+        carry = step(0, tile, carry)
+    else:
+        carry = lax.fori_loop(0, count // tile, body, carry)
     if count % tile:
         carry = step(count - count % tile, count % tile, carry)
     return carry
@@ -220,23 +230,43 @@
     ]
 
 
-def for_crops(sides_ref, row_count, step):
-    def crop_body(crop, start):
+def for_crops(sides_ref, row_count, order_ref, start_ref, step):
+    crops = sides_ref.shape[0]
+
+    def scan(crop, state):
+        start, large, small = state
         side = sides_ref[crop]
-        cells = side * side
-        for window, fits in ((SMALL_WINDOW, side <= 6), (LARGE_WINDOW, side > 6)):
-
-            @pl.when(fits)
-            def _():
-                first = pl.multiple_of(
-                    jnp.minimum(start // 8, (row_count - window) // 8) * 8, 8
-                )
-                place = lax.broadcasted_iota(jnp.int32, (window, HALF_WIDTH), 0) + (first - start)
-                step(crop, pl.ds(first, window), (place >= 0) & (place < cells))
-
-        return start + cells
-
-    lax.fori_loop(0, sides_ref.shape[0], crop_body, jnp.int32(0))
+        start_ref[crop] = start
+        is_small = side <= SMALL_SIDE
+        order_ref[jnp.where(is_small, crops + small, large)] = crop
+        return (
+            start + side * side,
+            large + jnp.where(is_small, 0, 1),
+            small + jnp.where(is_small, 1, 0),
+        )
+
+    zero = jnp.int32(0)
+    _, large, small = lax.fori_loop(0, crops, scan, (zero, zero, zero))
+    for window, first, count in ((LARGE_WINDOW, 0, large), (SMALL_WINDOW, crops, small)):
+
+        def group_body(group, _, window=window, first=first, count=count):
+            members = []
+            for member in range(CROP_GROUP):
+                crop = order_ref[first + jnp.minimum(group * CROP_GROUP + member, count - 1)]
+                start = start_ref[crop]
+                side = sides_ref[crop]
+                row = pl.multiple_of(jnp.minimum(start // 8, (row_count - window) // 8) * 8, 8)
+                place = lax.broadcasted_iota(jnp.int32, (window, HALF_WIDTH), 0) + (row - start)
+                members.append((crop, pl.ds(row, window), (place >= 0) & (place < side * side)))
+            step(members)
+            return 0
+
+        lax.fori_loop(0, (count + CROP_GROUP - 1) // CROP_GROUP, group_body, 0)
+
+
+def half_lanes(half):
+    starts = [part * PAD_WIDTH + half * HALF_WIDTH for part in range(3)]
+    return [slice(start, start + HALF_WIDTH) for start in starts]
 
 
 def pair_lanes():
@@ -253,16 +283,16 @@
     )
 
 
-def spread_pair(target, half, pair, values):
+def spread_pair(target, member, half, pair, values):
     first = pair * LANES
     lanes = slice(first, first + LANES)
     parts = split(values)
     for index in range(2):
         value = parts[index].astype(F32)
-        target[half, index, first : first + HDIM, lanes] = jnp.where(
+        target[member, half, index, first : first + HDIM, lanes] = jnp.where(
             pair_lanes(), value, 0.0
         ).astype(BF16)
-        target[half, index, first + HEAD_PAD : first + HEAD_PAD + HDIM, lanes] = jnp.where(
+        target[member, half, index, first + HEAD_PAD : first + HEAD_PAD + HDIM, lanes] = jnp.where(
             pair_lanes(), 0.0, value
         ).astype(BF16)
 
@@ -283,6 +313,14 @@
     input_ref,
     weight_ref,
     table_ref,
+    x1_hbm,
+    qkv_hbm,
+    mixed_hbm,
+    scores_hbm,
+    attention_hbm,
+    u_hbm,
+    e_hbm,
+    sums_ref,
     x1_ref,
     qkv_ref,
     mixed_ref,
@@ -290,7 +328,6 @@
     attention_ref,
     u_ref,
     e_ref,
-    sums_ref,
     head_weights,
     out_weight,
     first_low,
@@ -298,10 +335,27 @@
     attention_out,
     conv_in,
     spread,
+    order_ref,
+    start_ref,
+    sems,
 ):
     row_count, width = input_ref.shape
     chunks = width // LANES
-    tile = tile_rows(row_count)
+    tile = tile_rows(row_count, 2)
+    saves = [
+        pltpu.make_async_copy(source, target, sems.at[index])
+        for index, (source, target) in enumerate(
+            (
+                (qkv_ref, qkv_hbm),
+                (scores_ref, scores_hbm),
+                (attention_ref, attention_hbm),
+                (mixed_ref, mixed_hbm),
+                (x1_ref, x1_hbm),
+                (u_ref, u_hbm),
+                (e_ref, e_hbm),
+            )
+        )
+    ]
     total_live = live_total(sides_ref)
     mapping = head_map(BF16)
     for part in range(3):
@@ -326,15 +380,19 @@
             lanes = slice(part * PAD_WIDTH, (part + 1) * PAD_WIDTH)
             qkv_ref[rows, lanes] = dot(first_low[rows, :], head_weights[:, lanes])
 
-    def crop_step(crop, rows, keep):
-        for half in range(2):
-            lanes = [
-                slice(part * PAD_WIDTH + half * HALF_WIDTH, part * PAD_WIDTH + (half + 1) * HALF_WIDTH)
-                for part in range(3)
-            ]
+    saves[0].start()
+
+    def crop_step(members):
+        units_of = [(member, half) for member in range(len(members)) for half in range(2)]
+        blocks, results = [], []
+        for member, half in units_of:
+            crop, rows, keep = members[member]
+            lanes = half_lanes(half)
             query = units(jnp.where(keep, qkv_ref[rows, lanes[0]], 0.0))[0]
             key = units(jnp.where(keep, qkv_ref[rows, lanes[1]], 0.0))[0]
-            block = dot_split(dot_rows, split(key), split(query))
+            blocks.append(dot_split(dot_rows, split(key), split(query)))
+        for (member, half), block in zip(units_of, blocks):
+            crop = members[member][0]
             for pair in range(2):
                 scores = pair_part(block, pair)
                 scores_ref[crop, 2 * half + pair] = scores
@@ -342,14 +400,20 @@
                 scores = jnp.exp(scores - jnp.max(scores, axis=0, keepdims=True))
                 shares = scores / jnp.sum(scores, axis=0, keepdims=True)
                 attention_ref[crop, 2 * half + pair] = shares
-                spread_pair(spread, half, pair, shares)
-            result = dot_split(
-                dot, split(qkv_ref[rows, lanes[2]]), (spread[half, 0], spread[half, 1])
-            )
-            mixed[rows, lanes[0]] = jnp.where(keep, result, mixed[rows, lanes[0]])
-
-    for_crops(sides_ref, row_count, crop_step)
-
+                spread_pair(spread, member, half, pair, shares)
+        for member, half in units_of:
+            rows = members[member][1]
+            shares = (spread[member, half, 0], spread[member, half, 1])
+            results.append(dot_split(dot, split(qkv_ref[rows, half_lanes(half)[2]]), shares))
+        for (member, half), result in zip(units_of, results):
+            _, rows, keep = members[member]
+            lanes = half_lanes(half)[0]
+            mixed[rows, lanes] = jnp.where(keep, result, mixed[rows, lanes])
+
+    for_crops(sides_ref, row_count, order_ref, start_ref, crop_step)
+
+    saves[1].start()
+    saves[2].start()
     out_weight[...] = dot_rows(mapping, weight_ref[3]).astype(BF16)
 
     @pl.loop(0, row_count // tile)
@@ -358,6 +422,8 @@
         low = mixed[rows, :].astype(BF16)
         mixed_ref[rows, :] = low
         attention_out[rows, :] = dot(low, out_weight[...])
+
+    saves[3].start()
 
     def second_norm(first, size, _):
         rows = pl.ds(first, size)
@@ -372,6 +438,7 @@
         return 0
 
     for_rows(row_count, ROW_TILE, second_norm)
+    saves[4].start()
 
     zero = jnp.zeros((8, LANES), F32)
     sums_ref[...] = zero
@@ -392,9 +459,13 @@
         return tuple(carry)
 
     sums = for_groups(sides_ref, conv_step, (zero,) * (2 * chunks))
+    saves[5].start()
+    saves[6].start()
     for index, value in enumerate(sums):
         sums_ref[index : index + 1, :] = jnp.sum(value, axis=0, keepdims=True)
     sums_ref[2 * chunks : 2 * chunks + 1, :] = jnp.full((1, LANES), total_live, jnp.int32).astype(F32)
+    for save in saves:
+        save.wait()
 
 
 def mixing_forward(sides, sharpness, inputs, weights, table):
@@ -415,15 +486,25 @@
             shape((8, LANES), F32),
         ),
         in_specs=[SMEM_SPEC, SMEM_SPEC, VMEM_SPEC, VMEM_SPEC, VMEM_SPEC],
-        out_specs=(VMEM_SPEC,) * 8,
+        out_specs=(ANY_SPEC,) * 7 + (VMEM_SPEC,),
         scratch_shapes=[
+            pltpu.VMEM((row_count, width), F32),
+            pltpu.VMEM((row_count, 3 * PAD_WIDTH), F32),
+            pltpu.VMEM((row_count, PAD_WIDTH), BF16),
+            pltpu.VMEM((crops, HEAD_PAIRS, HDIM, LANES), F32),
+            pltpu.VMEM((crops, HEAD_PAIRS, HDIM, LANES), F32),
+            pltpu.VMEM((chunks, row_count, LANES), F32),
+            pltpu.VMEM((chunks, row_count, LANES), F32),
             pltpu.VMEM((width, 3 * PAD_WIDTH), BF16),
             pltpu.VMEM((PAD_WIDTH, width), BF16),
             pltpu.VMEM((row_count, width), BF16),
             pltpu.VMEM((row_count, PAD_WIDTH), F32),
             pltpu.VMEM((row_count, width), F32),
             pltpu.VMEM((chunks, LEAD + row_count + TAIL, LANES), F32),
-            pltpu.VMEM((2, 2, HALF_WIDTH, HALF_WIDTH), BF16),
+            pltpu.VMEM((CROP_GROUP, 2, 2, HALF_WIDTH, HALF_WIDTH), BF16),
+            pltpu.SMEM((2 * crops,), jnp.int32),
+            pltpu.SMEM((crops,), jnp.int32),
+            pltpu.SemaphoreType.DMA((7,)),
         ],
         compiler_params=pltpu.CompilerParams(vmem_limit_bytes=VMEM_LIMIT),
         name="mixing_forward",
@@ -439,18 +520,27 @@
 
 def feed_kernel(
     sides_ref,
+    x1_hbm,
+    e_hbm,
+    bn_ref,
+    weight_hbm,
+    table_ref,
+    adjoint_hbm,
+    out_hbm,
+    dx2_hbm,
+    dn_hbm,
+    weight_grad_hbm,
+    grads_ref,
+    back_sums_ref,
+    e_ref,
     x1_ref,
-    e_ref,
-    bn_ref,
     weight_ref,
-    table_ref,
     adjoint_ref,
     out_ref,
     dx2_ref,
     dn_ref,
     weight_grad_ref,
-    grads_ref,
-    back_sums_ref,
+    up_weight,
     n_ref,
     z_ref,
     dw_ref,
@@ -465,14 +555,43 @@
     pre_grad,
     grads,
     weight_sums,
+    sems,
 ):
+    loads = [
+        pltpu.make_async_copy(source, target, sems.at[index])
+        for index, (source, target) in enumerate(
+            (
+                (e_hbm, e_ref),
+                (x1_hbm, x1_ref),
+                (weight_hbm, weight_ref),
+                (adjoint_hbm, adjoint_ref),
+            )
+        )
+    ]
+    saves = [
+        pltpu.make_async_copy(source, target, sems.at[4 + index])
+        for index, (source, target) in enumerate(
+            (
+                (out_ref, out_hbm),
+                (dx2_ref, dx2_hbm),
+                (weight_grad_ref, weight_grad_hbm),
+                (dn_ref, dn_hbm),
+            )
+        )
+    ]
+    for load in loads:
+        load.start()
     row_count, width = x1_ref.shape
     chunks = width // LANES
     expand = weight_ref.shape[0] // 2
-    tile = tile_rows(row_count)
+    tile = tile_rows(row_count, 4)
     total_live = live_total(sides_ref)
+    hidden = expand * width
     batch = [batch_vectors(bn_ref, chunk, chunks) for chunk in range(chunks)]
     zero = jnp.zeros((8, LANES), F32)
+
+    def down_weight():
+        return weight_ref[expand : 2 * expand].reshape(hidden, width)
 
     def normalize(first, size, _):
         rows = pl.ds(first, size)
@@ -487,6 +606,7 @@
             dn_ref[chunk, rows, :] = jnp.zeros((size, LANES), F32)
         return 0
 
+    loads[0].wait()
     for_rows(row_count, ROW_TILE, normalize)
 
     taps = [tap_vectors(table_ref, 20, chunk) for chunk in range(chunks)]
@@ -500,6 +620,10 @@
 
     for_groups(sides_ref, conv_step, 0)
 
+    for load in loads[1:]:
+        load.wait()
+    for part in range(expand):
+        up_weight[:, part * width : (part + 1) * width] = weight_ref[part]
     weight_sums[...] = jnp.zeros_like(weight_sums)
     grads[...] = jnp.zeros_like(grads)
 
@@ -521,27 +645,13 @@
             return 0
 
         for_rows(tile, ROW_TILE, before)
-        for part in range(expand):
-            lanes = slice(part * width, (part + 1) * width)
-            pre[:, lanes] = dot(third_low[...], weight_ref[part])
-
-        def activate(inner, size, _):
-            near = pl.ds(inner, size)
-            for part in range(expand):
-                lanes = slice(part * width, (part + 1) * width)
-                value = pre[near, lanes]
-                share, bell = gelu_parts(value)
-                hidden_low[near, lanes] = (value * share).astype(BF16)
-                pre[near, lanes] = gelu_slope(value, share, bell)
-            return 0
-
-        for_rows(tile, GELU_TILE, activate)
-        total = None
-        for part in range(expand):
-            lanes = slice(part * width, (part + 1) * width)
-            term = dot(hidden_low[:, lanes], weight_ref[expand + part])
-            total = term if total is None else total + term
-        feed[...] = total
+        for part in range(2):
+            lanes = slice(part * hidden // 2, (part + 1) * hidden // 2)
+            value = dot(third_low[...], up_weight[:, lanes])
+            share, bell = gelu_parts(value)
+            hidden_low[:, lanes] = (value * share).astype(BF16)
+            pre[:, lanes] = gelu_slope(value, share, bell)
+        feed[...] = dot(hidden_low[...], down_weight())
 
         def output(inner, size, carry):
             near, rows = pl.ds(inner, size), pl.ds(base + inner, size)
@@ -553,20 +663,14 @@
             return carry + fold(entry * feed[near, :])
 
         grads[0] += for_rows(tile, ROW_TILE, output, jnp.zeros((8, width), F32))
+        pre_grad[...] = (dot_lanes(feed_grad[...], down_weight()) * pre[...]).astype(BF16)
+        weight_sums[expand : 2 * expand] += dot_rows(hidden_low[...], feed_grad[...]).reshape(
+            expand, width, width
+        )
+        up_grad = dot_rows(third_low[...], pre_grad[...])
         for part in range(expand):
-            lanes = slice(part * width, (part + 1) * width)
-            hidden_grad = dot_lanes(feed_grad[...], weight_ref[expand + part])
-            pre_grad[:, lanes] = (hidden_grad * pre[:, lanes]).astype(BF16)
-        for part in range(expand):
-            lanes = slice(part * width, (part + 1) * width)
-            weight_sums[expand + part] += dot_rows(hidden_low[:, lanes], feed_grad[...])
-            weight_sums[part] += dot_rows(third_low[...], pre_grad[:, lanes])
-        total = None
-        for part in range(expand):
-            lanes = slice(part * width, (part + 1) * width)
-            term = dot_lanes(pre_grad[:, lanes], weight_ref[part])
-            total = term if total is None else total + term
-        feed[...] = total
+            weight_sums[part] += up_grad[:, part * width : (part + 1) * width]
+        feed[...] = dot_lanes(pre_grad[...], up_weight[...])
 
         def after(inner, size, carry):
             near, rows = pl.ds(inner, size), pl.ds(base + inner, size)
@@ -590,6 +694,9 @@
         for index in range(3):
             grads[1 + index] += sums[index]
 
+    saves[0].start()
+    saves[1].start()
+
     owners, pieces, shard, _ = weight_grad_ref.shape
     inner = width // shard
     for owner in range(owners):
@@ -598,6 +705,8 @@
             weight_grad_ref[owner, piece] = weight_sums[
                 owner // inner * pieces + piece, rows, :
             ].astype(BF16)
+
+    saves[2].start()
 
     back_sums_ref[...] = zero
     for index, source in enumerate((1, 2, 3, 0)):
@@ -619,6 +728,7 @@
         return tuple(result)
 
     sums = for_groups(sides_ref, back_step, ((zero,) * 11,) * chunks)
+    saves[3].start()
     for chunk in range(chunks):
         lanes = chunk_lanes(chunk)
         for index, value in enumerate(sums[chunk]):
@@ -628,13 +738,15 @@
                 back_sums_ref[chunks + chunk : chunks + chunk + 1, :] = value
             if index == 10:
                 back_sums_ref[chunk : chunk + 1, :] = value
+    for save in saves:
+        save.wait()
 
 
 def feed_forward(sides, x1, e, batch_sums, weights, table, adjoint, grad_shape):
     row_count, width = x1.shape
     chunks = width // LANES
     expand = weights.shape[0] // 2
-    tile = tile_rows(row_count)
+    tile = tile_rows(row_count, 4)
     shape = jax.ShapeDtypeStruct
     return pl.pallas_call(
         feed_kernel,
@@ -646,9 +758,18 @@
             shape((16, width), F32),
             shape((8, LANES), F32),
         ),
-        in_specs=[SMEM_SPEC] + [VMEM_SPEC] * 6,
-        out_specs=(VMEM_SPEC,) * 6,
+        in_specs=[SMEM_SPEC, ANY_SPEC, ANY_SPEC, VMEM_SPEC, ANY_SPEC, VMEM_SPEC, ANY_SPEC],
+        out_specs=(ANY_SPEC,) * 4 + (VMEM_SPEC,) * 2,
         scratch_shapes=[
+            pltpu.VMEM((chunks, row_count, LANES), F32),
+            pltpu.VMEM((row_count, width), F32),
+            pltpu.VMEM(weights.shape, BF16),
+            pltpu.VMEM((row_count, width), BF16),
+            pltpu.VMEM((row_count, width), BF16),
+            pltpu.VMEM((row_count, width), F32),
+            pltpu.VMEM((chunks, row_count, LANES), F32),
+            pltpu.VMEM(grad_shape, BF16),
+            pltpu.VMEM((width, expand * width), BF16),
             pltpu.VMEM((chunks, LEAD + row_count + TAIL, LANES), F32),
             pltpu.VMEM((chunks, row_count, LANES), F32),
             pltpu.VMEM((chunks, LEAD + row_count + TAIL, LANES), F32),
@@ -663,6 +784,7 @@
             pltpu.VMEM((tile, expand * width), BF16),
             pltpu.VMEM((4, 8, width), F32),
             pltpu.VMEM((2 * expand, width, width), F32),
+            pltpu.SemaphoreType.DMA((8,)),
         ],
         compiler_params=pltpu.CompilerParams(vmem_limit_bytes=VMEM_LIMIT),
         name="feed_forward",
@@ -675,19 +797,25 @@
     input_ref,
     weight_ref,
     table_ref,
+    x1_hbm,
+    qkv_hbm,
+    mixed_hbm,
+    scores_hbm,
+    attention_hbm,
+    u_hbm,
+    bn_ref,
+    dx2_hbm,
+    dn_hbm,
+    back_ref,
+    out_ref,
+    weight_grad_ref,
+    grads_ref,
     x1_ref,
     qkv_ref,
     mixed_ref,
     scores_ref,
     attention_ref,
-    u_hbm,
-    bn_ref,
     dx2_ref,
-    dn_hbm,
-    back_ref,
-    out_ref,
-    weight_grad_ref,
-    grads_ref,
     head_weights,
     out_weight,
     pool,
@@ -699,6 +827,8 @@
     spread,
     out_sum,
     sharp_sums,
+    order_ref,
+    start_ref,
     load_sems,
 ):
     row_count, width = input_ref.shape
@@ -706,12 +836,23 @@
     u_ref, dn_ref = pool.at[0:chunks], pool.at[chunks : 2 * chunks]
     conv_in, attention_out = pool.at[2 * chunks : 3 * chunks], pool.at[3 * chunks : 4 * chunks]
     loads = [
-        pltpu.make_async_copy(u_hbm, u_ref, load_sems.at[0]),
-        pltpu.make_async_copy(dn_hbm, dn_ref, load_sems.at[1]),
+        pltpu.make_async_copy(source, target, load_sems.at[index])
+        for index, (source, target) in enumerate(
+            (
+                (x1_hbm, x1_ref),
+                (u_hbm, u_ref),
+                (dn_hbm, dn_ref),
+                (mixed_hbm, mixed_ref),
+                (dx2_hbm, dx2_ref),
+                (qkv_hbm, qkv_ref),
+                (scores_hbm, scores_ref),
+                (attention_hbm, attention_ref),
+            )
+        )
     ]
     for load in loads:
         load.start()
-    tile = tile_rows(row_count)
+    tile = tile_rows(row_count, 2)
     total_live = live_total(sides_ref)
     batch = [batch_vectors(bn_ref, chunk, chunks) for chunk in range(chunks)]
     zero = jnp.zeros((8, LANES), F32)
@@ -724,7 +865,7 @@
     out_weight[...] = dot_rows(mapping, weight_ref[3]).astype(BF16)
     spread[...] = jnp.zeros_like(spread)
 
-    for load in loads:
+    for load in loads[0:3]:
         load.wait()
 
     def batch_back(first, size, _):
@@ -773,6 +914,9 @@
                 value, axis=0, keepdims=True
             )
 
+    for load in loads[3:5]:
+        load.wait()
+
     @pl.loop(0, row_count // tile)
     def _(step):
         rows = pl.ds(pl.multiple_of(step * tile, 16), tile)
@@ -814,17 +958,21 @@
     weight_grad_ref[3] = dot(mapping, low).astype(BF16)
     sharp_sums[...] = jnp.zeros_like(sharp_sums)
 
-    def crop_step(crop, rows, keep):
-        for half in range(2):
-            lanes = [
-                slice(part * PAD_WIDTH + half * HALF_WIDTH, part * PAD_WIDTH + (half + 1) * HALF_WIDTH)
-                for part in range(3)
-            ]
-            query, query_scale = units(jnp.where(keep, qkv_ref[rows, lanes[0]], 0.0))
-            key, key_scale = units(jnp.where(keep, qkv_ref[rows, lanes[1]], 0.0))
+    for load in loads[5:]:
+        load.wait()
+
+    def crop_step(members):
+        units_of = [(member, half) for member in range(len(members)) for half in range(2)]
+        grads, blocks, sums, results = [], [], [], []
+        for member, half in units_of:
+            crop, rows, keep = members[member]
+            lanes = half_lanes(half)
             value = split(jnp.where(keep, qkv_ref[rows, lanes[2]], 0.0))
             grad = split(jnp.where(keep, mixed_grad[rows, lanes[0]], 0.0))
-            block = dot_split(dot_rows, value, grad)
+            grads.append(grad)
+            blocks.append(dot_split(dot_rows, value, grad))
+        for (member, half), block in zip(units_of, blocks):
+            crop = members[member][0]
             query_sums = []
             for pair in range(2):
                 index = 2 * half + pair
@@ -832,34 +980,44 @@
                 scores = scores_ref[crop, index]
                 part = pair_part(block, pair)
                 part = shares * (part - jnp.sum(part * shares, axis=0, keepdims=True))
-                spread_pair(spread, half, pair, shares)
-                sharp_sums[index : index + 1, :] += jnp.sum(part * scores, axis=0, keepdims=True)
-                part = part * pair_sharpness(sharp_ref, index)
-                query_sums.append(jnp.sum(part * scores, axis=0, keepdims=True))
-                spread_pair(spread, 2 + half, pair, part)
-            shares = (spread[half, 0], spread[half, 1])
-            slopes = (spread[2 + half, 0], spread[2 + half, 1])
-            value_grad = dot_split(dot_lanes, grad, shares)
+                spread_pair(spread, member, half, pair, shares)
+                total = jnp.sum(part * scores, axis=0, keepdims=True)
+                sharp_sums[index, pl.ds(crop, 1), :] = total
+                sharpness = pair_sharpness(sharp_ref, index)
+                query_sums.append(total * sharpness)
+                spread_pair(spread, member, 2 + half, pair, part * sharpness)
+            sums.append(jnp.concatenate(query_sums, axis=1))
+        for index, (member, half) in enumerate(units_of):
+            crop, rows, keep = members[member]
+            lanes = half_lanes(half)
+            query, query_scale = units(jnp.where(keep, qkv_ref[rows, lanes[0]], 0.0))
+            key, key_scale = units(jnp.where(keep, qkv_ref[rows, lanes[1]], 0.0))
+            shares = (spread[member, half, 0], spread[member, half, 1])
+            slopes = (spread[member, 2 + half, 0], spread[member, 2 + half, 1])
+            value_grad = dot_split(dot_lanes, grads[index], shares)
             query_grad = dot_split(dot, split(key), slopes)
-            query_grad = query_scale * (query_grad - query * jnp.concatenate(query_sums, axis=1))
+            query_grad = query_scale * (query_grad - query * sums[index])
             key_grad = dot_split(dot_lanes, split(query), slopes)
             key_grad = key_scale * (
                 key_grad - key * jnp.sum(key_grad * key, axis=0, keepdims=True)
             )
-            for part, result in enumerate((query_grad, key_grad, value_grad)):
+            results.append((query_grad, key_grad, value_grad))
+        for (member, half), grads in zip(units_of, results):
+            _, rows, keep = members[member]
+            for part, result in enumerate(grads):
                 for side in range(HALF_WIDTH // LANES):
                     chunk = (part * PAD_WIDTH + half * HALF_WIDTH) // LANES + side
                     pool[chunk, rows, :] = jnp.where(
                         keep[:, 0:LANES], result[:, chunk_lanes(side)], pool[chunk, rows, :]
                     )
 
-    for_crops(sides_ref, row_count, crop_step)
+    for_crops(sides_ref, row_count, order_ref, start_ref, crop_step)
 
     grads_ref[14:16, :] = jnp.zeros((2, width), F32)
     lane = lax.broadcasted_iota(jnp.int32, (1, LANES), 1)
     total = jnp.zeros((1, LANES), F32)
     for head in range(HEAD_NUMBER):
-        row = sharp_sums[head // 2 : head // 2 + 1, :]
+        row = jnp.sum(sharp_sums[head // 2], axis=0, keepdims=True)
         row = jnp.where((lane >> 6) == head % 2, row, 0.0)
         total = jnp.where(lane == head, jnp.sum(row, axis=1, keepdims=True), total)
     grads_ref[14:15, 0:LANES] = total
@@ -911,6 +1069,7 @@
 def mixing_backward(sides, sharpness, inputs, weights, table, saved, batch_sums, dx2, dn, back_sums):
     row_count, width = inputs.shape
     chunks = width // LANES
+    crops = sides.shape[0]
     shape = jax.ShapeDtypeStruct
     x1, qkv, mixed, scores, attention, u = saved
     return pl.pallas_call(
@@ -921,10 +1080,17 @@
             shape((16, width), F32),
         ),
         in_specs=[SMEM_SPEC, SMEM_SPEC]
-        + [VMEM_SPEC] * 8
-        + [ANY_SPEC, VMEM_SPEC, VMEM_SPEC, ANY_SPEC, VMEM_SPEC],
+        + [VMEM_SPEC] * 3
+        + [ANY_SPEC] * 6
+        + [VMEM_SPEC, ANY_SPEC, ANY_SPEC, VMEM_SPEC],
         out_specs=(VMEM_SPEC,) * 3,
         scratch_shapes=[
+            pltpu.VMEM((row_count, width), F32),
+            pltpu.VMEM((row_count, 3 * PAD_WIDTH), F32),
+            pltpu.VMEM((row_count, PAD_WIDTH), BF16),
+            pltpu.VMEM((crops, HEAD_PAIRS, HDIM, LANES), F32),
+            pltpu.VMEM((crops, HEAD_PAIRS, HDIM, LANES), F32),
+            pltpu.VMEM((row_count, width), F32),
             pltpu.VMEM((width, 3 * PAD_WIDTH), BF16),
             pltpu.VMEM((PAD_WIDTH, width), BF16),
             pltpu.VMEM((3 * PAD_WIDTH // LANES, row_count, LANES), F32),
@@ -933,10 +1099,12 @@
             pltpu.VMEM((row_count, PAD_WIDTH), F32),
             pltpu.VMEM((row_count, width), BF16),
             pltpu.VMEM((row_count, PAD_WIDTH), BF16),
-            pltpu.VMEM((4, 2, HALF_WIDTH, HALF_WIDTH), BF16),
+            pltpu.VMEM((CROP_GROUP, 4, 2, HALF_WIDTH, HALF_WIDTH), BF16),
             pltpu.VMEM((PAD_WIDTH, width), F32),
-            pltpu.VMEM((HEAD_PAIRS, LANES), F32),
-            pltpu.SemaphoreType.DMA((2,)),
+            pltpu.VMEM((HEAD_PAIRS, crops, LANES), F32),
+            pltpu.SMEM((2 * crops,), jnp.int32),
+            pltpu.SMEM((crops,), jnp.int32),
+            pltpu.SemaphoreType.DMA((8,)),
         ],
         compiler_params=pltpu.CompilerParams(vmem_limit_bytes=VMEM_LIMIT),
         name="mixing_backward",
@@ -997,52 +1165,53 @@
     )
 
 
-def sum_all_kernel(
-    counts, part_ref, total_ref, outer, inner, middle, outer_send, outer_recv, inner_send, inner_recv
-):
+def flip(value, bits):
+    for bit in (1, 2, 4):
+        if bits & bit:
+            value = value + bit - 2 * bit * lax.rem(lax.div(value, bit), 2)
+    return value
+
+
+def flip_peers(axis, count):
+    place = lax.axis_index(axis)
+    return [{axis: flip(place, bits)} for bits in range(1, count)]
+
+
+def sum_all_kernel(counts, part_ref, total_ref, parts, send, receive):
     n_dp, n_fsdp = counts
     dp, fsdp = lax.axis_index("dp"), lax.axis_index("fsdp")
-    inner_peers, outer_peers = ring_peers("fsdp", n_fsdp), ring_peers("dp", n_dp)
-    greet(inner_peers + outer_peers)
-    inner[fsdp] = part_ref[...]
+    place = dp * n_fsdp + fsdp
+    peers = [
+        {"dp": flip(dp, outer), "fsdp": flip(fsdp, inner)}
+        for inner in reversed(range(n_fsdp))
+        for outer in reversed(range(n_dp))
+        if inner or outer
+    ]
+    greet(peers)
+    parts[place] = part_ref[...]
     copies = [
-        push(part_ref, inner.at[fsdp], inner_send.at[k], inner_recv.at[k], peer)
-        for k, peer in enumerate(inner_peers)
+        push(part_ref, parts.at[place], send.at[k], receive.at[k], peer)
+        for k, peer in enumerate(peers)
     ]
     for copy in copies:
         copy.wait()
-    total = inner[0]
-    for k in range(1, n_fsdp):
-        total = total + inner[k]
-    middle[...] = total
-    outer[dp] = total
-    copies = [
-        push(middle, outer.at[dp], outer_send.at[k], outer_recv.at[k], peer)
-        for k, peer in enumerate(outer_peers)
-    ]
-    for copy in copies:
-        copy.wait()
-    total = outer[0]
-    for k in range(1, n_dp):
-        total = total + outer[k]
+    total = parts[0]
+    for k in range(1, n_dp * n_fsdp):
+        total = total + parts[k]
     total_ref[...] = total
 
 
 def sum_all(part, counts, identity):
-    n_dp, n_fsdp = counts
+    size = counts[0] * counts[1]
     return pl.pallas_call(
         functools.partial(sum_all_kernel, counts),
         out_shape=jax.ShapeDtypeStruct(part.shape, F32),
         in_specs=[VMEM_SPEC],
         out_specs=VMEM_SPEC,
         scratch_shapes=[
-            pltpu.VMEM((n_dp, *part.shape), F32),
-            pltpu.VMEM((n_fsdp, *part.shape), F32),
-            pltpu.VMEM(part.shape, F32),
-            pltpu.SemaphoreType.DMA((n_dp - 1,)),
-            pltpu.SemaphoreType.DMA((n_dp - 1,)),
-            pltpu.SemaphoreType.DMA((n_fsdp - 1,)),
-            pltpu.SemaphoreType.DMA((n_fsdp - 1,)),
+            pltpu.VMEM((size, *part.shape), F32),
+            pltpu.SemaphoreType.DMA((size - 1,)),
+            pltpu.SemaphoreType.DMA((size - 1,)),
         ],
         compiler_params=comm_params(identity),
         name="sum_all",
@@ -1073,14 +1242,14 @@
     columns = table_ref.shape[1]
     across = lax.rem(dp + 2, 4)
     pair = dp + 1 - 2 * lax.rem(dp, 2)
-    peers = ring_peers("fsdp", n_fsdp)
+    peers = flip_peers("fsdp", n_fsdp)
     greet(peers + [{"dp": across}, {"dp": pair}])
 
     def piece(block, owner):
         return blocks.at[block, pl.ds(pl.multiple_of(owner * shard, 16), shard), :]
 
     def origin(step):
-        return lax.rem(fsdp + n_fsdp - step, n_fsdp)
+        return flip(fsdp, step)
 
     stage[...] = jnp.zeros_like(stage)
     stage[0 : table_ref.shape[0], 0:columns] = table_ref[...]
@@ -1158,42 +1327,56 @@
     return pl.ds(pl.multiple_of(owner * shard, 16), shard)
 
 
-def reduce_kernel(
+TABLE_ROWS = (
+    [(0, row) for row in range(5)]
+    + [(1, 13), (1, 14)]
+    + [(1, row) for row in range(4)]
+    + [(0, row) for row in range(5, 14)]
+    + [(1, row) for row in range(4, 13)]
+)
+
+
+def settle_kernel(
     counts,
     place_ref,
     mix_ref,
     feed_ref,
     mix_table_ref,
     feed_table_ref,
-    energy_ref,
-    coefficient_ref,
-    sharp_ref,
+    left_hbm,
+    right_hbm,
     grad_ref,
     slots_ref,
-    table_grad_ref,
-    energy_out_ref,
-    coefficient_out_ref,
-    sharp_out_ref,
+    rows_ref,
+    table_ref,
+    left,
+    right,
     pair_buf,
     cross_out,
     cross_buf,
     ring_out,
     ring_buf,
+    feed_in,
     feed_buf,
     dp_buf,
     slot_out,
     slots,
+    steps,
+    rows_buf,
     table_stage,
     table_out,
     table_buf,
     table_part,
     table_dp,
+    load_sems,
     pair_send,
     pair_recv,
     cross_send,
     cross_recv,
     ring_send,
     ring_recv,
+    feed_in_send,
+    feed_in_recv,
     feed_send,
     feed_recv,
     dp_send,
@@ -1202,6 +1385,10 @@
     slot_recv,
     twin_send,
     twin_recv,
+    back_send,
+    back_recv,
+    last_send,
+    last_recv,
     table_send,
     table_recv,
     table_dp_send,
@@ -1212,31 +1399,91 @@
     width = mix_ref.shape[2]
     shard = width // n_fsdp
     core = lax.rem(dp, 2)
-    across = lax.rem(dp + 2, 4)
-    pair = dp + 1 - 2 * core
-    pair_across = lax.rem(pair + 2, 4)
-    peers, dp_peers = ring_peers("fsdp", n_fsdp), ring_peers("dp", n_dp)
+    across, pair, pair_across = flip(dp, 2), flip(dp, 1), flip(dp, 3)
+    peers, dp_peers = flip_peers("fsdp", n_fsdp), flip_peers("dp", n_dp)
     to_pair, to_across = {"dp": pair}, {"dp": across}
+    loads = [
+        pltpu.make_async_copy(left_hbm.at[core], left, load_sems.at[0]),
+        pltpu.make_async_copy(right_hbm.at[core], right, load_sems.at[1]),
+    ]
+    for load in loads:
+        load.start()
     greet(peers + dp_peers)
 
-    parts = 4
-    deep = width // parts
-    pairing = []
-    for part in range(parts):
-        rows = pl.ds(part * deep, deep)
+    parts = list(reversed(range(n_fsdp // 2)))
+    deep = 2 * shard
+
+    def part_rows(part):
+        first = lax.div(flip(fsdp, 2 * part), 2)
+        return pl.ds(pl.multiple_of(first * deep, 16), deep)
+
+    def owner_rows(owner):
+        return pl.ds(pl.multiple_of(owner * shard, 16), shard)
+
+    pairing = {}
+    for part in parts:
+        rows = part_rows(part)
         for side, block in enumerate((pair_across, pair)):
-            pairing.append(
-                push(
-                    mix_ref.at[block, rows],
-                    pair_buf.at[side, rows],
-                    pair_send.at[side, part],
-                    pair_recv.at[side, part],
-                    to_pair,
+            pairing[part, side] = push(
+                mix_ref.at[block, rows],
+                pair_buf.at[side, rows],
+                pair_send.at[side, part],
+                pair_recv.at[side, part],
+                to_pair,
+            )
+    pieces = feed_ref.shape[0] // n_dp
+    feeding = [
+        push(
+            feed_ref.at[pl.ds(flip(dp, k + 1) * pieces, pieces)],
+            feed_in.at[k],
+            feed_in_send.at[k],
+            feed_in_recv.at[k],
+            peer,
+        )
+        for k, peer in enumerate(dp_peers)
+    ]
+    crossing = {}
+    for part in parts:
+        rows = part_rows(part)
+        pairing[part, 0].wait_recv()
+        cross_out[rows, :] = (
+            mix_ref[across, rows, :].astype(F32) + pair_buf[0, rows, :].astype(F32)
+        ).astype(BF16)
+        crossing[part] = push(
+            cross_out.at[rows],
+            cross_buf.at[rows],
+            cross_send.at[part],
+            cross_recv.at[part],
+            to_across,
+        )
+    ring = {}
+    for part in parts:
+        rows = part_rows(part)
+        pairing[part, 1].wait_recv()
+        crossing[part].wait_recv()
+        ring_out[rows, :] = (
+            mix_ref[dp, rows, :].astype(F32)
+            + pair_buf[1, rows, :].astype(F32)
+            + cross_buf[rows, :].astype(F32)
+        ).astype(BF16)
+        for bits in (2 * part + 1, 2 * part):
+            if bits:
+                ring[bits] = push(
+                    ring_out.at[owner_rows(flip(fsdp, bits))],
+                    ring_buf.at[bits],
+                    ring_send.at[bits - 1],
+                    ring_recv.at[bits - 1],
+                    peers[bits - 1],
                 )
-            )
-    feed_buf[dp] = feed_ref[...]
-    feeding = [
-        push(feed_ref, feed_buf.at[dp], feed_send.at[k], feed_recv.at[k], peer)
+
+    for copy in feeding:
+        copy.wait_recv()
+    total = feed_ref[pl.ds(dp * pieces, pieces)].astype(F32)
+    for k in range(n_dp - 1):
+        total = total + feed_in[k].astype(F32)
+    feed_buf[dp] = total.astype(BF16)
+    feeds = [
+        push(feed_buf.at[dp], feed_buf.at[dp], feed_send.at[k], feed_recv.at[k], peer)
         for k, peer in enumerate(dp_peers)
     ]
 
@@ -1249,6 +1496,7 @@
         term = rest.astype(BF16)
         terms.append(term)
         rest = rest - term.astype(F32)
+    terms = jnp.concatenate(terms, axis=0)
     columns = width // n_fsdp
     sharp_row = lax.broadcasted_iota(jnp.int32, (32, LANES), 0) == 31
     sharp_values = jnp.broadcast_to(mix_table_ref[14:15, 0:LANES], (32, LANES))
@@ -1256,12 +1504,13 @@
         lane = lax.broadcasted_iota(jnp.int32, (width, LANES), 1)
         source = lax.broadcasted_iota(jnp.int32, (width, LANES), 0)
         hit = ((lane < columns) & (lane + owner * columns == source)).astype(F32).astype(BF16)
-        value = dot(terms[0], hit) + dot(terms[1], hit) + dot(terms[2], hit)
+        value = dot(terms, hit)
+        value = value[0:32] + value[32:64] + value[64:96]
         table_out[owner] = jnp.where(sharp_row, sharp_values, value)
     table_buf[fsdp] = table_out[fsdp]
     tabling = [
         push(
-            table_out.at[turned(fsdp, k + 1, n_fsdp)],
+            table_out.at[flip(fsdp, k + 1)],
             table_buf.at[fsdp],
             table_send.at[k],
             table_recv.at[k],
@@ -1270,43 +1519,15 @@
         for k, peer in enumerate(peers)
     ]
 
-    crossing = []
-    for part in range(parts):
-        rows = pl.ds(part * deep, deep)
-        pairing[2 * part].wait_recv()
-        cross_out[rows, :] = (
-            mix_ref[across, rows, :].astype(F32) + pair_buf[0, rows, :].astype(F32)
-        ).astype(BF16)
-        crossing.append(
-            push(
-                cross_out.at[rows],
-                cross_buf.at[rows],
-                cross_send.at[part],
-                cross_recv.at[part],
-                to_across,
-            )
-        )
-    for part in range(parts):
-        rows = pl.ds(part * deep, deep)
-        pairing[2 * part + 1].wait_recv()
-        crossing[part].wait_recv()
-        ring_out[rows, :] = (
-            mix_ref[dp, rows, :].astype(F32)
-            + pair_buf[1, rows, :].astype(F32)
-            + cross_buf[rows, :].astype(F32)
-        ).astype(BF16)
-    ring = [
-        push(
-            ring_out.at[owner_rows(turned(fsdp, k + 1, n_fsdp), shard)],
-            ring_buf.at[fsdp],
-            ring_send.at[k],
-            ring_recv.at[k],
-            peer,
-        )
-        for k, peer in enumerate(peers)
+    total = ring_out[owner_rows(fsdp), :].astype(F32)
+    for bits in range(1, n_fsdp):
+        ring[bits].wait_recv()
+        total = total + ring_buf[bits].astype(F32)
+    dp_buf[dp] = total
+    gathering = [
+        push(dp_buf.at[dp], dp_buf.at[dp], dp_send.at[k], dp_recv.at[k], peer)
+        for k, peer in enumerate(dp_peers)
     ]
-    ring_buf[fsdp] = ring_out[owner_rows(fsdp, shard), :]
-
     for copy in tabling:
         copy.wait_recv()
     total = table_buf[0]
@@ -1318,20 +1539,8 @@
         push(table_part, table_dp.at[dp], table_dp_send.at[k], table_dp_recv.at[k], peer)
         for k, peer in enumerate(dp_peers)
     ]
-
-    for copy in ring:
+    for copy in feeds:
         copy.wait_recv()
-    total = ring_buf[0].astype(F32)
-    for owner in range(1, n_fsdp):
-        total = total + ring_buf[owner].astype(F32)
-    dp_buf[dp] = total
-    gathering = [
-        push(dp_buf.at[dp], dp_buf.at[dp], dp_send.at[k], dp_recv.at[k], peer)
-        for k, peer in enumerate(dp_peers)
-    ]
-    for copy in feeding:
-        copy.wait_recv()
-    pieces = feed_ref.shape[0]
     for place in range(n_dp):
         for piece in range(pieces):
             grad_ref[n_dp + place * pieces + piece] = feed_buf[place, piece].astype(F32)
@@ -1340,49 +1549,201 @@
     for place in range(n_dp):
         grad_ref[place] = dp_buf[place]
 
-    slot_count = 2 * n_fsdp
-    block_count = grad_ref.shape[0]
-    for slot in range(slot_count):
+    slotting = {}
+    for bits in reversed(range(n_fsdp)):
+        slot = 2 * flip(fsdp, bits) + core
         block, filled = jnp.int32(0), jnp.int32(0)
-        for index in range(block_count):
+        for index in range(grad_ref.shape[0]):
             here = place_ref[index] == slot
             block = jnp.where(here, index, block)
             filled = jnp.where(here, 1, filled)
-        rows = grad_ref[block]
-        slot_out[slot] = (rows * filled.astype(F32)).astype(BF16)
-    slots[core, owner_rows(fsdp, shard), :] = slot_out[2 * fsdp + core]
-    slotting = [
-        push(
-            slot_out.at[2 * turned(fsdp, k + 1, n_fsdp) + core],
-            slots.at[core, owner_rows(fsdp, shard), :],
-            slot_send.at[k],
-            slot_recv.at[k],
-            peer,
+        value = (grad_ref[block] * filled.astype(F32)).astype(BF16)
+        if bits:
+            slot_out[bits - 1] = value
+            slotting[bits] = push(
+                slot_out.at[bits - 1],
+                slots.at[core, owner_rows(fsdp), :],
+                slot_send.at[bits - 1],
+                slot_recv.at[bits - 1],
+                peers[bits - 1],
+            )
+        else:
+            slots[core, owner_rows(fsdp), :] = value
+    for load in loads:
+        load.wait()
+    left_parts, right_parts = split(left[...]), split(right[...])
+    twins = []
+    for bits in range(n_fsdp):
+        if bits:
+            slotting[bits].wait_recv()
+        part = slots.at[core, owner_rows(flip(fsdp, bits)), :]
+        twins.append(push(part, part, twin_send.at[bits], twin_recv.at[bits], to_pair))
+
+    grad = slots[core]
+    half = split(dot(left_parts[0], grad) + dot(left_parts[1], grad))
+    steps[...] = dot_split(dot, half, right_parts).astype(BF16)
+    back = {}
+    for bits in reversed(range(1, n_fsdp)):
+        back[bits] = push(
+            steps.at[owner_rows(flip(fsdp, bits))],
+            rows_buf.at[2 * fsdp + core],
+            back_send.at[bits - 1],
+            back_recv.at[bits - 1],
+            peers[bits - 1],
         )
-        for k, peer in enumerate(peers)
-    ]
-    twins = []
-    for step in range(n_fsdp):
-        if step:
-            slotting[step - 1].wait_recv()
-        owner = lax.rem(fsdp + n_fsdp - step, n_fsdp)
-        part = slots.at[core, owner_rows(owner, shard), :]
-        twins.append(push(part, part, twin_send.at[step], twin_recv.at[step], to_pair))
-
+    rows_buf[2 * fsdp + core] = steps[owner_rows(fsdp), :]
     for copy in table_dps:
         copy.wait_recv()
     total = table_dp[0]
     for place in range(1, n_dp):
         total = total + table_dp[place]
-    count = energy_ref.shape[0]
-    grad = total[0:count, 0:columns]
+    table_ref[...] = total
+    lasts = []
+    for bits in range(n_fsdp):
+        if bits:
+            back[bits].wait_recv()
+        part = rows_buf.at[2 * flip(fsdp, bits) + core]
+        lasts.append(push(part, part, last_send.at[bits], last_recv.at[bits], to_pair))
+    for copy in twins:
+        copy.wait_recv()
+    slots_ref[...] = slots[...]
+    for copy in lasts:
+        copy.wait_recv()
+    rows_ref[...] = rows_buf[...]
+    copies = [*pairing.values(), *crossing.values(), *ring.values(), *slotting.values()]
+    copies += [*back.values(), *feeding, *feeds, *tabling, *table_dps, *gathering]
+    for copy in copies + twins + lasts:
+        copy.wait_send()
+
+
+def settle(places, mix, feed, mix_table, feed_table, left, right, counts, identity):
+    n_dp, n_fsdp = counts
+    width = mix.shape[2]
+    shard = width // n_fsdp
+    blocks = n_dp + feed.shape[0]
+    pieces = feed.shape[0] // n_dp
+    inner, outer = n_fsdp - 1, n_dp - 1
+    shape = jax.ShapeDtypeStruct
+    dma = pltpu.SemaphoreType.DMA
+    sizes = [(2, n_fsdp // 2), (n_fsdp // 2,), (inner,), (outer,), (outer,), (outer,)]
+    sizes += [(inner,), (n_fsdp,), (inner,), (n_fsdp,), (inner,), (outer,)]
+    return pl.pallas_call(
+        functools.partial(settle_kernel, counts),
+        out_shape=(
+            shape((blocks, shard, width), F32),
+            shape((2, width, width), BF16),
+            shape((2 * n_fsdp, shard, width), BF16),
+            shape((32, LANES), F32),
+        ),
+        in_specs=[SMEM_SPEC] + [VMEM_SPEC] * 4 + [ANY_SPEC] * 2,
+        out_specs=(VMEM_SPEC,) * 4,
+        scratch_shapes=[
+            pltpu.VMEM((width, width), F32),
+            pltpu.VMEM((width, width), F32),
+            pltpu.VMEM((2, width, width), BF16),
+            pltpu.VMEM((width, width), BF16),
+            pltpu.VMEM((width, width), BF16),
+            pltpu.VMEM((width, width), BF16),
+            pltpu.VMEM((n_fsdp, shard, width), BF16),
+            pltpu.VMEM((outer, pieces, shard, width), BF16),
+            pltpu.VMEM((n_dp, pieces, shard, width), BF16),
+            pltpu.VMEM((n_dp, shard, width), F32),
+            pltpu.VMEM((inner, shard, width), BF16),
+            pltpu.VMEM((2, width, width), BF16),
+            pltpu.VMEM((width, width), BF16),
+            pltpu.VMEM((2 * n_fsdp, shard, width), BF16),
+            pltpu.VMEM((32, width), F32),
+            pltpu.VMEM((n_fsdp, 32, LANES), F32),
+            pltpu.VMEM((n_fsdp, 32, LANES), F32),
+            pltpu.VMEM((32, LANES), F32),
+            pltpu.VMEM((n_dp, 32, LANES), F32),
+            dma((2,)),
+        ]
+        + [dma(size) for size in sizes for _ in range(2)],
+        compiler_params=comm_params(identity),
+        name="settle",
+    )(places, mix, feed, mix_table, feed_table, left, right)
+
+
+def finish_kernel(
+    place_ref,
+    grad_ref,
+    slots_ref,
+    rows_ref,
+    table_ref,
+    energy_ref,
+    coefficient_ref,
+    sharp_ref,
+    left_hbm,
+    right_hbm,
+    masters_hbm,
+    grad_hbm,
+    left_out_hbm,
+    right_out_hbm,
+    masters_out_hbm,
+    low_hbm,
+    table_grad_ref,
+    energy_out_ref,
+    coefficient_out_ref,
+    sharp_out_ref,
+    left,
+    right,
+    masters,
+    low,
+    sems,
+):
+    slot_count = slots_ref.shape[0]
+    load_left = pltpu.make_async_copy(left_hbm, left, sems.at[0])
+    load_right = pltpu.make_async_copy(right_hbm, right, sems.at[1])
+    load_masters = pltpu.make_async_copy(masters_hbm, masters, sems.at[2])
+    saves = [
+        pltpu.make_async_copy(source, target, sems.at[3 + index])
+        for index, (source, target) in enumerate(
+            (
+                (grad_ref, grad_hbm),
+                (left, left_out_hbm),
+                (right, right_out_hbm),
+                (masters, masters_out_hbm),
+                (low, low_hbm),
+            )
+        )
+    ]
+    load_left.start()
+    load_right.start()
+    load_masters.start()
+    saves[0].start()
+    load_left.wait()
+    for slot in range(slot_count):
+        grad = slots_ref[slot]
+        left[slot] = (
+            covariance_forgetting * left[slot]
+            + (1.0 - covariance_forgetting) * dot_lanes(grad, grad)
+        )
+    saves[1].start()
+    load_right.wait()
+    for slot in range(slot_count):
+        grad = slots_ref[slot]
+        right[slot] = (
+            covariance_forgetting * right[slot]
+            + (1.0 - covariance_forgetting) * dot_rows(grad, grad)
+        )
+    saves[2].start()
+    load_masters.wait()
+    for block in range(masters.shape[0]):
+        value = masters[block] - weight_rate * rows_ref[place_ref[block]].astype(F32)
+        masters[block] = value
+        low[block] = value.astype(BF16)
+    saves[3].start()
+    saves[4].start()
+    count, columns = energy_ref.shape
+    grad = table_ref[0:count, 0:columns]
     table_grad_ref[...] = grad
     energy = covariance_forgetting * energy_ref[...] + (1.0 - covariance_forgetting) * grad * grad
     energy_out_ref[...] = energy
     coefficient_out_ref[...] = coefficient_ref[...] - vector_rate * grad / (
         jnp.sqrt(energy) + energy_epsilon
     )
-    grad = total[31:32, 0:HEAD_NUMBER]
+    grad = table_ref[31:32, 0:HEAD_NUMBER]
     energy = (
         covariance_forgetting * sharp_ref[1:2, :] + (1.0 - covariance_forgetting) * grad * grad
     )
@@ -1391,172 +1752,37 @@
     sharp_out_ref[2:3, :] = sharp_ref[0:1, :] - sharpness_step_size * grad / (
         jnp.sqrt(energy) + energy_epsilon
     )
-    for copy in twins:
-        copy.wait_recv()
-    slots_ref[...] = slots[...]
-    for copy in (
-        pairing + feeding + tabling + crossing + ring + table_dps + gathering + slotting + twins
-    ):
-        copy.wait_send()
-
-
-TABLE_ROWS = (
-    [(0, row) for row in range(5)]
-    + [(1, 13), (1, 14)]
-    + [(1, row) for row in range(4)]
-    + [(0, row) for row in range(5, 14)]
-    + [(1, row) for row in range(4, 13)]
-)
-
-
-def reduce_gradients(
-    places, mix, feed, mix_table, feed_table, energy, coefficients, sharps, counts, identity
-):
-    n_dp, n_fsdp = counts
-    width = mix.shape[2]
-    shard = width // n_fsdp
-    blocks = n_dp + feed.shape[0] * n_dp
+    for save in saves:
+        save.wait()
+
+
+def finish(places, grads, slots, rows, table, energy, coefficients, sharps, left, right, masters):
     shape = jax.ShapeDtypeStruct
-    dma = pltpu.SemaphoreType.DMA
     return pl.pallas_call(
-        functools.partial(reduce_kernel, counts),
+        finish_kernel,
         out_shape=(
-            shape((blocks, shard, width), F32),
-            shape((2, width, width), BF16),
+            shape(grads.shape, F32),
+            shape(left.shape, F32),
+            shape(right.shape, F32),
+            shape(masters.shape, F32),
+            shape(masters.shape, BF16),
             shape(energy.shape, F32),
             shape(energy.shape, F32),
             shape(energy.shape, F32),
             shape((3, sharps.shape[1]), F32),
         ),
-        in_specs=[SMEM_SPEC] + [VMEM_SPEC] * 7,
-        out_specs=(VMEM_SPEC,) * 6,
+        in_specs=[SMEM_SPEC] + [VMEM_SPEC] * 7 + [ANY_SPEC] * 3,
+        out_specs=(ANY_SPEC,) * 5 + (VMEM_SPEC,) * 4,
         scratch_shapes=[
-            pltpu.VMEM((2, width, width), BF16),
-            pltpu.VMEM((width, width), BF16),
-            pltpu.VMEM((width, width), BF16),
-            pltpu.VMEM((width, width), BF16),
-            pltpu.VMEM((n_fsdp, shard, width), BF16),
-            pltpu.VMEM((n_dp, *feed.shape), BF16),
-            pltpu.VMEM((n_dp, shard, width), F32),
-            pltpu.VMEM((2 * n_fsdp, shard, width), BF16),
-            pltpu.VMEM((2, width, width), BF16),
-            pltpu.VMEM((32, width), F32),
-            pltpu.VMEM((n_fsdp, 32, LANES), F32),
-            pltpu.VMEM((n_fsdp, 32, LANES), F32),
-            pltpu.VMEM((32, LANES), F32),
-            pltpu.VMEM((n_dp, 32, LANES), F32),
-            dma((2, 4)),
-            dma((2, 4)),
-            dma((4,)),
-            dma((4,)),
-            dma((n_fsdp - 1,)),
-            dma((n_fsdp - 1,)),
-            dma((n_dp - 1,)),
-            dma((n_dp - 1,)),
-            dma((n_dp - 1,)),
-            dma((n_dp - 1,)),
-            dma((n_fsdp - 1,)),
-            dma((n_fsdp - 1,)),
-            dma((n_fsdp,)),
-            dma((n_fsdp,)),
-            dma((n_fsdp - 1,)),
-            dma((n_fsdp - 1,)),
-            dma((n_dp - 1,)),
-            dma((n_dp - 1,)),
+            pltpu.VMEM(left.shape, F32),
+            pltpu.VMEM(right.shape, F32),
+            pltpu.VMEM(masters.shape, F32),
+            pltpu.VMEM(masters.shape, BF16),
+            pltpu.SemaphoreType.DMA((8,)),
         ],
-        compiler_params=comm_params(identity),
-        name="reduce_gradients",
-    )(places, mix, feed, mix_table, feed_table, energy, coefficients, sharps)
-
-
-def shampoo_kernel(grad_ref, left_ref, right_ref, left_root, right_root, left_out, right_out, step_ref):
-    grad = grad_ref[...]
-    left_out[...] = covariance_forgetting * left_ref[...] + (
-        1.0 - covariance_forgetting
-    ) * dot_lanes(grad, grad)
-    right_out[...] = covariance_forgetting * right_ref[...] + (
-        1.0 - covariance_forgetting
-    ) * dot_rows(grad, grad)
-    root = split(left_root[...])
-    half = split(dot(root[0], grad) + dot(root[1], grad))
-    step_ref[...] = dot_split(dot, half, split(right_root[...])).astype(BF16)
-
-
-def shampoo(grads, left, right, left_root, right_root):
-    slots, width, _ = grads.shape
-    shape = jax.ShapeDtypeStruct
-    spec = pl.BlockSpec((pl.Squeezed(), width, width), lambda slot: (slot, 0, 0))
-    return pl.pallas_call(
-        shampoo_kernel,
-        grid=(slots,),
-        out_shape=(
-            shape(grads.shape, F32),
-            shape(grads.shape, F32),
-            shape(grads.shape, BF16),
-        ),
-        in_specs=[spec] * 5,
-        out_specs=(spec,) * 3,
         compiler_params=pltpu.CompilerParams(vmem_limit_bytes=VMEM_LIMIT),
-        name="shampoo",
-    )(grads, left, right, left_root, right_root)
-
-
-def return_kernel(
-    counts, steps_ref, rows_ref, rows_buf, ring_send, ring_recv, twin_send, twin_recv
-):
-    n_dp, n_fsdp = counts
-    dp, fsdp = lax.axis_index("dp"), lax.axis_index("fsdp")
-    width = steps_ref.shape[2]
-    shard = width // n_fsdp
-    core = lax.rem(dp, 2)
-    to_pair = {"dp": dp + 1 - 2 * core}
-    peers = ring_peers("fsdp", n_fsdp)
-    greet(peers + [to_pair])
-    ring = [
-        push(
-            steps_ref.at[core, owner_rows(turned(fsdp, k + 1, n_fsdp), shard)],
-            rows_buf.at[2 * fsdp + core],
-            ring_send.at[k],
-            ring_recv.at[k],
-            peer,
-        )
-        for k, peer in enumerate(peers)
-    ]
-    rows_buf[2 * fsdp + core] = steps_ref[core, owner_rows(fsdp, shard), :]
-    twins = []
-    for step in range(n_fsdp):
-        if step:
-            ring[step - 1].wait_recv()
-        owner = lax.rem(fsdp + n_fsdp - step, n_fsdp)
-        part = rows_buf.at[2 * owner + core]
-        twins.append(push(part, part, twin_send.at[step], twin_recv.at[step], to_pair))
-    for copy in twins:
-        copy.wait_recv()
-    rows_ref[...] = rows_buf[...]
-    for copy in ring + twins:
-        copy.wait_send()
-
-
-def return_steps(steps, counts, identity):
-    n_dp, n_fsdp = counts
-    width = steps.shape[2]
-    shard = width // n_fsdp
-    dma = pltpu.SemaphoreType.DMA
-    return pl.pallas_call(
-        functools.partial(return_kernel, counts),
-        out_shape=jax.ShapeDtypeStruct((2 * n_fsdp, shard, width), BF16),
-        in_specs=[VMEM_SPEC],
-        out_specs=VMEM_SPEC,
-        scratch_shapes=[
-            pltpu.VMEM((2 * n_fsdp, shard, width), BF16),
-            dma((n_fsdp - 1,)),
-            dma((n_fsdp - 1,)),
-            dma((n_fsdp,)),
-            dma((n_fsdp,)),
-        ],
-        compiler_params=comm_params(identity),
-        name="return_steps",
-    )(steps)
+        name="finish",
+    )(places, grads, slots, rows, table, energy, coefficients, sharps, left, right, masters)
 
 
 def shards(
@@ -1582,7 +1808,7 @@
     direct = counts[0] == 4 and slot_count == 2 and shard_rows % 16 == 0
     if direct:
         mixing_blocks, table = gather_start(projection_masters, channel_coefficients, counts, 0)
-        grad_shape = (counts[0] * counts[1], (block_count - 4) // counts[0], shard_rows, feature_count)
+        grad_shape = (counts[1], block_count - 4, shard_rows, feature_count)
     else:
         full_table = lax.all_gather(channel_coefficients.astype(BF16), "fsdp", axis=1, tiled=True)
         table = full_table.astype(F32)
@@ -1618,51 +1844,32 @@
         back_sums,
     )
     if direct:
-        feed_grad = lax.psum_scatter(
-            feed_grad, ("dp", "fsdp"), scatter_dimension=0, tiled=True
-        )[0]
-        (
-            portion_derivative,
-            owned_grad,
-            catalog_portion,
-            channel_energy_renewed,
-            channel_params_updated,
-            sharps,
-        ) = reduce_gradients(
+        feed_grad = lax.psum_scatter(feed_grad, "fsdp", scatter_dimension=0, tiled=True)[0]
+        grads, owned_grad, my_rows, table_total = settle(
             storage_position_map,
             mixing_grad,
             feed_grad,
             mixing_table,
             feed_table,
+            leading_root_preconditioner,
+            trailing_root_preconditioner,
+            counts,
+            3,
+        )
+        *results, sharps = finish(
+            storage_position_map,
+            grads,
+            owned_grad,
+            my_rows,
+            table_total,
             channel_energy_average,
             channel_coefficients,
             jnp.stack([head_sharpness, sharpness_energy_average]),
-            counts,
-            3,
-        )
-        leading_covariance_renewed, trailing_covariance_renewed, steps = shampoo(
-            owned_grad,
             leading_covariance,
             trailing_covariance,
-            leading_root_preconditioner,
-            trailing_root_preconditioner,
+            projection_masters,
         )
-        my_rows = return_steps(steps, counts, 4)
-        update = jnp.take(my_rows, storage_position_map, axis=0).astype(F32)
-        projection_updated = projection_masters - weight_rate * update
-        return (
-            layer_output,
-            incoming_tokens_grad,
-            portion_derivative,
-            leading_covariance_renewed,
-            trailing_covariance_renewed,
-            projection_updated,
-            projection_updated.astype(BF16),
-            catalog_portion,
-            channel_energy_renewed,
-            channel_params_updated,
-            *sharps,
-        )
+        return (layer_output, incoming_tokens_grad, *results, *sharps)
     sharpness_share = mixing_table[14, 0:HEAD_NUMBER]
     table_grad = jnp.stack([(mixing_table, feed_table)[source][row] for source, row in TABLE_ROWS])
     block_grad = jnp.concatenate([mixing_grad, feed_grad[0]], axis=0).astype(F32)

time: 319 us -> 249 us (0.78)
  Pallas kernels: 275 us -> 222 us
  waiting for transfers between devices: 19.3 us -> 6.85 us
  local copies, waits for them, and re-layouts: 7.43 us -> 3.76 us
    pallas_call x1, Pallas kernels: 41.7 us -> 25 us  [mixing_forward(): pl.pallas_call(mixing_forward_kernel, out_shape=(shape((row_count, width)...]
    pallas_call x1, Pallas kernels: 66 us -> 49.5 us  [mixing_backward(): pl.pallas_call(mixing_backward_kernel, out_shape=(shape((row_count, width...]
    reduce_scatter x1, waiting for transfers between devices: 19.2 us -> 6.8 us  [shards(): lax.psum_scatter(feed_grad, 'fsdp', scatter_dimension=0, tiled=True)[0]]
    pallas_call x1, Pallas kernels: 51 us -> 41.9 us  [feed_forward(): pl.pallas_call(feed_kernel, out_shape=(shape((row_count, width), BF16), s...]
    pallas_call x2, Pallas kernels: 38.4 us -> 32 us  [sum_all(): pl.pallas_call(functools.partial(sum_all_kernel, counts), out_shape=jax.S...]
    pallas_call x3 -> x2, Pallas kernels: 58.1 us -> 51.9 us  [the longest x1 45.4 us: settle(): pl.pallas_call(functools.partial(settle_kernel, counts), out_shape=(shape...]
where the time goes in v4:
time: 249 us; the launch traced here: 247 us
  Pallas kernels  222 us (89%)
  between operations  14.1 us (6%)
  waiting for transfers between devices  6.85 us (3%)
  local copies, waits for them, and re-layouts  3.76 us (2%)
    pallas_call x1, Pallas kernels, mixing_backward(): pl.pallas_call(mixing_backward_kernel, out_shape=(shape((row_count, width...  49.5 us
    pallas_call x1, Pallas kernels, settle(): pl.pallas_call(functools.partial(settle_kernel, counts), out_shape=(shape...  45.4 us
    pallas_call x1, Pallas kernels, feed_forward(): pl.pallas_call(feed_kernel, out_shape=(shape((row_count, width), BF16), s...  41.9 us
    pallas_call x2, Pallas kernels, sum_all(): pl.pallas_call(functools.partial(sum_all_kernel, counts), out_shape=jax.S...  32 us
    pallas_call x1, Pallas kernels, mixing_forward(): pl.pallas_call(mixing_forward_kernel, out_shape=(shape((row_count, width)...  25 us
    pallas_call x1, Pallas kernels, gather_start(): pl.pallas_call(functools.partial(gather_kernel, counts), out_shape=(shape...  21.6 us
    reduce_scatter x1, waiting for transfers between devices, shards(): lax.psum_scatter(feed_grad, 'fsdp', scatter_dimension=0, tiled=True)[0]  6.8 us
    pallas_call x1, Pallas kernels, finish(): pl.pallas_call(finish_kernel, out_shape=(shape(grads.shape, F32), shape(l...  6.43 us
  transfers between devices with their start and end apart: 2, of which 1 were waited for; matrix products, arithmetic and copies ran while one was open for 0% of the time, Pallas kernels for 52%

profile of v4, /device:TPU:1, one launch (start us, length us, event | category | flops | bytes accessed | tf_op | source)
XLA Modules:
  0.0 247.3 jit_solution(17091636920048803018)
XLA Ops:
  7.2 0.0 all-gather.2.cloned.1.call-start
  7.2 1.8 slice.7
  9.0 0.0 all-gather.2.cloned.1.call-update
  9.1 0.0 reduce-scatter.2.cloned.1.call-start
  9.1 21.6 %gather_start.1 = (bf16[4,384,384]{2,1,0:T(8,128)(2,1)}, f32[32,384]{1,0:T(8,128)}) custom-call(f32[12,48,384]{2,1,0:T(8,128)} %masters_hbm.1, f32[29,48]{1,0:T(8,128)} %coefficient_ref.1), custom_call_target="tpu_custom_call" | custom-call | tf_op jit(solution)/shard_map/gather_start/pallas_call | solution.py:1303
  30.7 25.0 %mixing_forward.1 = (f32[1856,384]{1,0:T(8,128)}, f32[1856,1536]{1,0:T(8,128)}, bf16[1856,512]{1,0:T(8,128)(2,1)}, f32[16,4,48,128]{3,2,1,0:T(8,128)}, f32[16,4,...) custom-call(s32[16]{0:T(128)} %sides_ref.5, f32[8]{0:T(128)} %sharp_ref.3, ...), custom_call_target="tpu_custom_call" | custom-call | tf_op jit(solution)/shard_map/mixing_forward/pallas_call | solution.py:476
  55.7 15.2 %sum_all.2.bn_ref = f32[8,128]{1,0:T(8,128)} custom-call(f32[8,128]{1,0:T(8,128)} %get-tuple-element.49.part_ref), custom_call_target="tpu_custom_call" | custom-call | tf_op jit(solution)/shard_map/sum_all/pallas_call | solution.py:1206
  71.0 0.0 all-gather.2.cloned.1.call-done.weight_hbm
  71.0 41.9 %feed_forward.1 = (bf16[1856,384]{1,0:T(8,128)(2,1)}, f32[1856,384]{1,0:T(8,128)}, f32[3,1856,128]{2,1,0:T(8,128)}, bf16[8,8,48,384]{3,2,1,0:T(8,128)(2,1)}, f32[16,384]{1,0:T(8,128)}, /*index=5*/f32[8,128]{1,0:T(8,128)}) custom-call(s32[16]{0:T(128)} %sides_ref.5, f32[1856,384]{1,0:T(8,128)} %get-tuple-element.47.x1_hbm, ...), custom_call_target="tpu_custom_call" | custom-call | tf_op jit(solution)/shard_map/feed_forward/pallas_call | solution.py:751
  112.9 0.0 copy-start
  112.9 0.0 copy-start.1
  112.9 0.0 reduce-scatter.2.cloned.1.call-update
  113.0 0.6 copy-done
  113.6 0.0 copy-done.1
  113.6 0.6 pad_maximum_fusion.sharp_ref
  114.2 16.8 %sum_all.3.back_ref = f32[8,128]{1,0:T(8,128)} custom-call(f32[8,128]{1,0:T(8,128)} %get-tuple-element.58.part_ref), custom_call_target="tpu_custom_call" | custom-call | tf_op jit(solution)/shard_map/sum_all/pallas_call | solution.py:1206
  131.0 49.5 %mixing_backward.1 = (bf16[1856,384]{1,0:T(8,128)(2,1)}, bf16[4,384,384]{2,1,0:T(8,128)(2,1)}, f32[16,384]{1,0:T(8,128)}) custom-call(s32[16]{0:T(128)} %sides_ref.5, f32[8]{0:T(128)} %sharp_ref.3, bf16[1856,384]{1,0:T(8,128)(2,1)} %input_ref.3, bf16[4,384,384]{2,1,0:T(8,128)(2,1)} %get-tuple-element.45.weight_ref, f32[32,384]{1,0:T(8,128)} %get-tuple-element.46.table_ref, ...), custom_call_target="tpu_custom_call" | custom-call | tf_op jit(solution)/shard_map/mixing_backward/pallas_call | solution.py:1075
  180.5 6.8 %reduce-scatter.2.cloned.1.call-done = bf16[1,8,48,384]{3,2,1,0:T(8,128)(2,1)} async-done(((bf16[8,8,48,384]{3,2,1,0:T(8,128)(2,1)}), bf16[1,8,48,384]{3,2,1,0:T(8,128)(2,1)}) %reduce-scatter.2.cloned.1.call-update) | async-done | bytes 294928 | tf_op jit(solution)/shard_map/reduce_scatter | solution.py:1847
  187.3 45.4 %settle.1 = (f32[12,48,384]{2,1,0:T(8,128)}, bf16[2,384,384]{2,1,0:T(8,128)(2,1)}, bf16[16,48,384]{2,1,0:T(8,128)(2,1)}, f32[32,128]{1,0:T(8,128)}) custom-call(s32[12]{0:T(128)} %place_ref.3, bf16[4,384,384]{2,1,0:T(8,128)(2,1)} %get-tuple-element.60.mix_ref, bf16[8,48,384]{2,1,0:T(8,128)(2,1)} %bitcast.9, f32[16,384]{1,0:T(8,128)} %get-tuple-element.62.mix_table_ref, ...), custom_call_target="tpu_custom_call" | custom-call | tf_op jit(solution)/shard_map/settle/pallas_call | solution.py:1630
  232.7 6.4 %finish.1 = (f32[12,48,384]{2,1,0:T(8,128)}, f32[2,384,384]{2,1,0:T(8,128)}, f32[2,384,384]{2,1,0:T(8,128)}, f32[12,48,384]{2,1,0:T(8,128)}, bf16[12,48,384]{2,1...) custom-call(s32[12]{0:T(128)} %place_ref.3, ...), custom_call_target="tpu_custom_call" | custom-call | tf_op jit(solution)/shard_map/finish/pallas_call | solution.py:1761
  239.2 1.3 slice_bitcast_fusion
Async XLA Ops:
  7.2 63.8 %all-gather.2.cloned.1.call-start = ((), (), s32[]{:S(2)}) async-start(), calls=%async_computation.1 | async-start | bytes 2654208 | tf_op jit(solution)/shard_map/all_gather | solution.py:1819
  9.1 178.2 %reduce-scatter.2.cloned.1.call-start = ((), (), s32[]{:S(2)}) async-start(), calls=%async_computation.2 | async-start | bytes 2654208 | tf_op jit(solution)/shard_map/reduce_scatter | solution.py:1847
  112.9 0.7 copy-start
  112.9 0.7 copy-start.1
Sparse Core Ops, SparseCore 0:
  10.8 52.9 all-gather.1
  113.1 74.1 reduce-scatter.1

commit v5 on v4

--- a/solution.py
+++ b/solution.py
@@ -21,8 +21,8 @@
 LARGE_WINDOW = 208
 CROP_GROUP = 2
 ROW_TILE = 464
-GELU_TILE = 128
-VMEM_LIMIT = 58 * 2**20
+HIDDEN_PARTS = 6
+VMEM_LIMIT = 60 * 2**20
 
 norm_epsilon = 1e-06
 batch_epsilon = 1e-05
@@ -318,7 +318,7 @@
     mixed_hbm,
     scores_hbm,
     attention_hbm,
-    u_hbm,
+    slope_hbm,
     e_hbm,
     sums_ref,
     x1_ref,
@@ -326,7 +326,7 @@
     mixed_ref,
     scores_ref,
     attention_ref,
-    u_ref,
+    slope_ref,
     e_ref,
     head_weights,
     out_weight,
@@ -351,7 +351,7 @@
                 (attention_ref, attention_hbm),
                 (mixed_ref, mixed_hbm),
                 (x1_ref, x1_hbm),
-                (u_ref, u_hbm),
+                (slope_ref, slope_hbm),
                 (e_ref, e_hbm),
             )
         )
@@ -433,7 +433,7 @@
         value = unit * table_ref[3:4, :] + table_ref[4:5, :]
         for chunk in range(chunks):
             conv_in[chunk, pl.ds(LEAD + first, size), :] = value[:, chunk_lanes(chunk)]
-            u_ref[chunk, rows, :] = jnp.zeros((size, LANES), F32)
+            slope_ref[chunk, rows, :] = jnp.zeros((size, LANES), F32)
             e_ref[chunk, rows, :] = jnp.zeros((size, LANES), F32)
         return 0
 
@@ -449,9 +449,10 @@
         carry = list(carry)
         for chunk in range(chunks):
             value = conv_forward(conv_in, chunk, row, side, masks, taps[chunk])
-            share, _ = gelu_parts(value)
+            share, bell = gelu_parts(value)
             active = value * share
-            u_ref[chunk, rows, :] = jnp.where(masks[0], value, u_ref[chunk, rows, :])
+            slope = gelu_slope(value, share, bell)
+            slope_ref[chunk, rows, :] = jnp.where(masks[0], slope, slope_ref[chunk, rows, :])
             e_ref[chunk, rows, :] = jnp.where(masks[0], active, e_ref[chunk, rows, :])
             active = jnp.where(masks[0], active, 0.0)
             carry[chunk] = carry[chunk] + active
@@ -548,9 +549,9 @@
     unit,
     spread,
     third_low,
-    pre,
     hidden_low,
     feed,
+    third_grad,
     feed_grad,
     pre_grad,
     grads,
@@ -630,69 +631,69 @@
     def z_rows(rows):
         return jnp.concatenate([z_ref[chunk, rows, :] for chunk in range(chunks)], axis=1)
 
+    def before(base):
+        rows = pl.ds(base, tile)
+        value = x1_ref[rows, :] + table_ref[7:8, :] * z_rows(rows)
+        x2[...] = value
+        value, scale = centered(value)
+        unit[...] = value
+        spread[...] = jnp.broadcast_to(scale, (tile, LANES))
+        third_low[...] = (value * table_ref[8:9, :] + table_ref[9:10, :]).astype(BF16)
+        feed_grad[...] = (entry_rows(base) * table_ref[10:11, :]).astype(BF16)
+
+    def entry_rows(base):
+        live = row_mask(base, tile, width, total_live)
+        return jnp.where(live, adjoint_ref[pl.ds(base, tile), :].astype(F32), 0.0)
+
     @pl.loop(0, row_count // tile)
     def _(step):
         base = pl.multiple_of(step * tile, 16)
-
-        def before(inner, size, _):
-            near, rows = pl.ds(inner, size), pl.ds(base + inner, size)
-            value = x1_ref[rows, :] + table_ref[7:8, :] * z_rows(rows)
-            x2[near, :] = value
-            value, scale = centered(value)
-            unit[near, :] = value
-            spread[near, :] = jnp.broadcast_to(scale, (size, LANES))
-            third_low[near, :] = (value * table_ref[8:9, :] + table_ref[9:10, :]).astype(BF16)
-            return 0
-
-        for_rows(tile, ROW_TILE, before)
-        for part in range(2):
-            lanes = slice(part * hidden // 2, (part + 1) * hidden // 2)
-            value = dot(third_low[...], up_weight[:, lanes])
+        rows = pl.ds(base, tile)
+        before(base)
+
+        def hidden_lanes(part):
+            return slice(part * hidden // HIDDEN_PARTS, (part + 1) * hidden // HIDDEN_PARTS)
+
+        def products(part):
+            lanes = hidden_lanes(part)
+            return (
+                dot(third_low[...], up_weight[:, lanes]),
+                dot_lanes(feed_grad[...], down_weight()[lanes]),
+            )
+
+        ahead = products(0)
+        for part in range(HIDDEN_PARTS):
+            lanes = hidden_lanes(part)
+            value, hidden_grad = ahead
+            if part + 1 < HIDDEN_PARTS:
+                ahead = products(part + 1)
             share, bell = gelu_parts(value)
             hidden_low[:, lanes] = (value * share).astype(BF16)
-            pre[:, lanes] = gelu_slope(value, share, bell)
+            pre_grad[:, lanes] = (hidden_grad * gelu_slope(value, share, bell)).astype(BF16)
         feed[...] = dot(hidden_low[...], down_weight())
-
-        def output(inner, size, carry):
-            near, rows = pl.ds(inner, size), pl.ds(base + inner, size)
-            live = row_mask(base + inner, size, width, total_live)
-            value = x2[near, :] + table_ref[10:11, :] * feed[near, :]
-            out_ref[rows, :] = jnp.where(live, value, 0.0).astype(BF16)
-            entry = jnp.where(live, adjoint_ref[rows, :].astype(F32), 0.0)
-            feed_grad[near, :] = (entry * table_ref[10:11, :]).astype(BF16)
-            return carry + fold(entry * feed[near, :])
-
-        grads[0] += for_rows(tile, ROW_TILE, output, jnp.zeros((8, width), F32))
-        pre_grad[...] = (dot_lanes(feed_grad[...], down_weight()) * pre[...]).astype(BF16)
+        third_grad[...] = dot_lanes(pre_grad[...], up_weight[...])
         weight_sums[expand : 2 * expand] += dot_rows(hidden_low[...], feed_grad[...]).reshape(
             expand, width, width
         )
         up_grad = dot_rows(third_low[...], pre_grad[...])
         for part in range(expand):
             weight_sums[part] += up_grad[:, part * width : (part + 1) * width]
-        feed[...] = dot_lanes(pre_grad[...], up_weight[...])
-
-        def after(inner, size, carry):
-            near, rows = pl.ds(inner, size), pl.ds(base + inner, size)
-            live = row_mask(base + inner, size, width, total_live)
-            entry = jnp.where(live, adjoint_ref[rows, :].astype(F32), 0.0)
-            grad = feed[near, :]
-            value = unit[near, :]
-            total = entry + norm_back(grad * table_ref[8:9, :], value, spread[near, 0:1])
-            dx2_ref[rows, :] = total
-            scaled = total * table_ref[7:8, :]
-            for chunk in range(chunks):
-                dw_ref[chunk, pl.ds(LEAD + base + inner, size), :] = scaled[:, chunk_lanes(chunk)]
-            return (
-                carry[0] + fold(total * z_rows(rows)),
-                carry[1] + fold(grad * value),
-                carry[2] + fold(grad),
-            )
-
-        wide = jnp.zeros((8, width), F32)
-        sums = for_rows(tile, ROW_TILE, after, (wide, wide, wide))
-        for index in range(3):
-            grads[1 + index] += sums[index]
+
+        value = x2[...] + table_ref[10:11, :] * feed[...]
+        live = row_mask(base, tile, width, total_live)
+        out_ref[rows, :] = jnp.where(live, value, 0.0).astype(BF16)
+        entry = entry_rows(base)
+        grads[0] += fold(entry * feed[...])
+        grad = third_grad[...]
+        value = unit[...]
+        total = entry + norm_back(grad * table_ref[8:9, :], value, spread[:, 0:1])
+        dx2_ref[rows, :] = total
+        scaled = total * table_ref[7:8, :]
+        for chunk in range(chunks):
+            dw_ref[chunk, pl.ds(LEAD + base, tile), :] = scaled[:, chunk_lanes(chunk)]
+        grads[1] += fold(total * z_rows(rows))
+        grads[2] += fold(grad * value)
+        grads[3] += fold(grad)
 
     saves[0].start()
     saves[1].start()
@@ -777,8 +778,8 @@
             pltpu.VMEM((tile, width), F32),
             pltpu.VMEM((tile, LANES), F32),
             pltpu.VMEM((tile, width), BF16),
-            pltpu.VMEM((tile, expand * width), F32),
             pltpu.VMEM((tile, expand * width), BF16),
+            pltpu.VMEM((tile, width), F32),
             pltpu.VMEM((tile, width), F32),
             pltpu.VMEM((tile, width), BF16),
             pltpu.VMEM((tile, expand * width), BF16),
@@ -794,7 +795,7 @@
 def mixing_backward_kernel(
     sides_ref,
     sharp_ref,
-    input_ref,
+    input_hbm,
     weight_ref,
     table_ref,
     x1_hbm,
@@ -802,12 +803,15 @@
     mixed_hbm,
     scores_hbm,
     attention_hbm,
-    u_hbm,
+    slope_hbm,
+    e_hbm,
     bn_ref,
     dx2_hbm,
     dn_hbm,
     back_ref,
-    out_ref,
+    head_low_hbm,
+    dx1_hbm,
+    head_weights_hbm,
     weight_grad_ref,
     grads_ref,
     x1_ref,
@@ -820,9 +824,8 @@
     out_weight,
     pool,
     conv_grad,
-    dx1,
     mixed_grad,
-    low_rows,
+    first_low,
     head_low,
     spread,
     out_sum,
@@ -831,22 +834,39 @@
     start_ref,
     load_sems,
 ):
-    row_count, width = input_ref.shape
+    row_count, width = input_hbm.shape
+    low_rows, input_ref = head_low.at[0, :, 0:width], head_low.at[1, :, 0:width]
+    input_load = pltpu.make_async_copy(input_hbm, input_ref, load_sems.at[14])
+    input_load.start()
     chunks = width // LANES
-    u_ref, dn_ref = pool.at[0:chunks], pool.at[chunks : 2 * chunks]
-    conv_in, attention_out = pool.at[2 * chunks : 3 * chunks], pool.at[3 * chunks : 4 * chunks]
+    slope_ref, e_ref = pool.at[0:chunks], pool.at[chunks : 2 * chunks]
+    dn_ref, conv_in = pool.at[2 * chunks : 3 * chunks], pool.at[3 * chunks : 4 * chunks]
+    attention_out = slope_ref
     loads = [
         pltpu.make_async_copy(source, target, load_sems.at[index])
         for index, (source, target) in enumerate(
             (
                 (x1_hbm, x1_ref),
-                (u_hbm, u_ref),
+                (slope_hbm, slope_ref),
+                (e_hbm, e_ref),
                 (dn_hbm, dn_ref),
                 (mixed_hbm, mixed_ref),
                 (dx2_hbm, dx2_ref),
                 (qkv_hbm, qkv_ref),
                 (scores_hbm, scores_ref),
                 (attention_hbm, attention_ref),
+            )
+        )
+    ]
+    saves = [
+        pltpu.make_async_copy(source, target, load_sems.at[len(loads) + index])
+        for index, (source, target) in enumerate(
+            (
+                (head_weights, head_weights_hbm),
+                (dx2_ref, dx1_hbm),
+                (head_low.at[0], head_low_hbm.at[0]),
+                (head_low.at[1], head_low_hbm.at[1]),
+                (head_low.at[2], head_low_hbm.at[2]),
             )
         )
     ]
@@ -862,10 +882,20 @@
         head_weights[:, part * PAD_WIDTH : (part + 1) * PAD_WIDTH] = dot(
             weight_ref[part], mapping
         ).astype(BF16)
+    saves[0].start()
     out_weight[...] = dot_rows(mapping, weight_ref[3]).astype(BF16)
     spread[...] = jnp.zeros_like(spread)
 
-    for load in loads[0:3]:
+    def first_norm(first, size, _):
+        rows = pl.ds(first, size)
+        unit, _ = centered(input_ref[rows, :].astype(F32))
+        first_low[rows, :] = (unit * table_ref[0:1, :] + table_ref[1:2, :]).astype(BF16)
+        return 0
+
+    input_load.wait()
+    for_rows(row_count, ROW_TILE, first_norm)
+
+    for load in loads[0:4]:
         load.wait()
 
     def batch_back(first, size, _):
@@ -877,15 +907,13 @@
             lanes = chunk_lanes(chunk)
             mean, scale = batch[chunk]
             count = bn_ref[2 * chunks : 2 * chunks + 1, :]
-            u = u_ref[chunk, rows, :]
-            share, bell = gelu_parts(u)
-            standard = (u * share - mean) * scale
+            standard = (e_ref[chunk, rows, :] - mean) * scale
             inner = (
                 back_ref[chunk : chunk + 1, :]
                 + standard * back_ref[chunks + chunk : chunks + chunk + 1, :]
             ) / count
             grad = scale * table_ref[5:6, lanes] * (dn_ref[chunk, rows, :] - inner)
-            grad = grad * gelu_slope(u, share, bell)
+            grad = grad * slope_ref[chunk, rows, :]
             conv_grad[chunk, pl.ds(LEAD + first, size), :] = jnp.where(live, grad, 0.0)
             conv_in[chunk, pl.ds(first, size), :] = value[:, lanes]
         return 0
@@ -914,7 +942,7 @@
                 value, axis=0, keepdims=True
             )
 
-    for load in loads[3:5]:
+    for load in loads[4:6]:
         load.wait()
 
     @pl.loop(0, row_count // tile)
@@ -931,7 +959,7 @@
         grad = jnp.where(live, grad, 0.0)
         unit, scale = centered(x1_ref[rows, :])
         total = dx2_ref[rows, :] + norm_back(grad * table_ref[3:4, :], unit, scale)
-        dx1[rows, :] = total
+        dx2_ref[rows, :] = total
         low_rows[rows, :] = (total * table_ref[2:3, :]).astype(BF16)
         held = jnp.concatenate([attention_out[chunk, rows, :] for chunk in range(chunks)], axis=1)
         return (
@@ -941,6 +969,7 @@
         )
 
     sums = for_rows(row_count, ROW_TILE, second_back, (wide, wide, wide))
+    saves[1].start()
     for index in range(3):
         grads_ref[2 + index : 3 + index, :] = jnp.sum(sums[index], axis=0, keepdims=True)
 
@@ -958,7 +987,7 @@
     weight_grad_ref[3] = dot(mapping, low).astype(BF16)
     sharp_sums[...] = jnp.zeros_like(sharp_sums)
 
-    for load in loads[5:]:
+    for load in loads[6:]:
         load.wait()
 
     def crop_step(members):
@@ -1013,6 +1042,7 @@
 
     for_crops(sides_ref, row_count, order_ref, start_ref, crop_step)
 
+    grads_ref[0:2, :] = jnp.zeros((2, width), F32)
     grads_ref[14:16, :] = jnp.zeros((2, width), F32)
     lane = lax.broadcasted_iota(jnp.int32, (1, LANES), 1)
     total = jnp.zeros((1, LANES), F32)
@@ -1022,48 +1052,24 @@
         total = jnp.where(lane == head, jnp.sum(row, axis=1, keepdims=True), total)
     grads_ref[14:15, 0:LANES] = total
 
-    def first_norm(first, size, _):
-        rows = pl.ds(first, size)
-        unit, _ = centered(input_ref[rows, :].astype(F32))
-        low_rows[rows, :] = (unit * table_ref[0:1, :] + table_ref[1:2, :]).astype(BF16)
-        return 0
-
-    for_rows(row_count, ROW_TILE, first_norm)
-
     for part in range(3):
-        lanes = slice(part * PAD_WIDTH, (part + 1) * PAD_WIDTH)
         out_sum[...] = jnp.zeros_like(out_sum)
 
         @pl.loop(0, row_count // tile)
-        def _(step, lanes=lanes, part=part):
+        def _(step, part=part):
             rows = pl.ds(pl.multiple_of(step * tile, 16), tile)
             first = part * PAD_WIDTH // LANES
             for chunk in range(PAD_WIDTH // LANES):
-                head_low[rows, chunk_lanes(chunk)] = pool[first + chunk, rows, :].astype(BF16)
-            term = dot_lanes(head_low[rows, :], head_weights[:, lanes])
-            mixed_grad[rows, 0:width] = term if part == 0 else mixed_grad[rows, 0:width] + term
-
-        @pl.loop(0, row_count // tile)
-        def _(step, lanes=lanes):
-            rows = pl.ds(pl.multiple_of(step * tile, 16), tile)
-            out_sum[...] += dot_rows(head_low[rows, :], low_rows[rows, :])
-
+                head_low[part, rows, chunk_lanes(chunk)] = pool[first + chunk, rows, :].astype(BF16)
+            out_sum[...] += dot_rows(head_low[part, rows, :], first_low[rows, :])
+
+        saves[2 + part].start()
         low = out_sum[...].astype(BF16)
         weight_grad_ref[part] = lax.dot_general(
             low, mapping, (((0,), (1,)), ((), ())), preferred_element_type=F32
         ).astype(BF16)
-
-    def first_back(first, size, carry):
-        rows = pl.ds(first, size)
-        unit, scale = centered(input_ref[rows, :].astype(F32))
-        grad = mixed_grad[rows, 0:width]
-        total = dx1[rows, :] + norm_back(grad * table_ref[0:1, :], unit, scale)
-        out_ref[rows, :] = total.astype(BF16)
-        return carry[0] + fold(grad * unit), carry[1] + fold(grad)
-
-    sums = for_rows(row_count, ROW_TILE, first_back, (wide, wide))
-    for index in range(2):
-        grads_ref[index : index + 1, :] = jnp.sum(sums[index], axis=0, keepdims=True)
+    for save in saves:
+        save.wait()
 
 
 def mixing_backward(sides, sharpness, inputs, weights, table, saved, batch_sums, dx2, dn, back_sums):
@@ -1071,19 +1077,21 @@
     chunks = width // LANES
     crops = sides.shape[0]
     shape = jax.ShapeDtypeStruct
-    x1, qkv, mixed, scores, attention, u = saved
+    x1, qkv, mixed, scores, attention, slope, e = saved
     return pl.pallas_call(
         mixing_backward_kernel,
         out_shape=(
-            shape((row_count, width), BF16),
+            shape((3, row_count, PAD_WIDTH), BF16),
+            shape((row_count, width), F32),
+            shape((width, 3 * PAD_WIDTH), BF16),
             shape((4, width, width), BF16),
             shape((16, width), F32),
         ),
         in_specs=[SMEM_SPEC, SMEM_SPEC]
-        + [VMEM_SPEC] * 3
-        + [ANY_SPEC] * 6
+        + [ANY_SPEC, VMEM_SPEC, VMEM_SPEC]
+        + [ANY_SPEC] * 7
         + [VMEM_SPEC, ANY_SPEC, ANY_SPEC, VMEM_SPEC],
-        out_specs=(VMEM_SPEC,) * 3,
+        out_specs=(ANY_SPEC,) * 3 + (VMEM_SPEC,) * 2,
         scratch_shapes=[
             pltpu.VMEM((row_count, width), F32),
             pltpu.VMEM((row_count, 3 * PAD_WIDTH), F32),
@@ -1095,16 +1103,15 @@
             pltpu.VMEM((PAD_WIDTH, width), BF16),
             pltpu.VMEM((3 * PAD_WIDTH // LANES, row_count, LANES), F32),
             pltpu.VMEM((chunks, LEAD + row_count + TAIL, LANES), F32),
-            pltpu.VMEM((row_count, width), F32),
             pltpu.VMEM((row_count, PAD_WIDTH), F32),
             pltpu.VMEM((row_count, width), BF16),
-            pltpu.VMEM((row_count, PAD_WIDTH), BF16),
+            pltpu.VMEM((3, row_count, PAD_WIDTH), BF16),
             pltpu.VMEM((CROP_GROUP, 4, 2, HALF_WIDTH, HALF_WIDTH), BF16),
             pltpu.VMEM((PAD_WIDTH, width), F32),
             pltpu.VMEM((HEAD_PAIRS, crops, LANES), F32),
             pltpu.SMEM((2 * crops,), jnp.int32),
             pltpu.SMEM((crops,), jnp.int32),
-            pltpu.SemaphoreType.DMA((8,)),
+            pltpu.SemaphoreType.DMA((15,)),
         ],
         compiler_params=pltpu.CompilerParams(vmem_limit_bytes=VMEM_LIMIT),
         name="mixing_backward",
@@ -1119,7 +1126,8 @@
         mixed,
         scores,
         attention,
-        u,
+        slope,
+        e,
         batch_sums,
         dx2,
         dn,
@@ -1216,6 +1224,69 @@
         compiler_params=comm_params(identity),
         name="sum_all",
     )(part)
+
+
+def sum_pair_kernel(
+    counts, part_ref, blocks_hbm, total_ref, sums_ref, parts, own, other, send, receive, sems
+):
+    n_dp, n_fsdp = counts
+    dp, fsdp = lax.axis_index("dp"), lax.axis_index("fsdp")
+    core = lax.rem(dp, 2)
+    place = dp * n_fsdp + fsdp
+    peers = [
+        {"dp": flip(dp, outer), "fsdp": flip(fsdp, inner)}
+        for inner in reversed(range(n_fsdp))
+        for outer in reversed(range(n_dp))
+        if inner or outer
+    ]
+    load = pltpu.make_async_copy(blocks_hbm.at[pl.ds(core * n_fsdp, n_fsdp)], own, sems.at[0])
+    load.start()
+    greet(peers)
+    parts[place] = part_ref[...]
+    copies = [
+        push(part_ref, parts.at[place], send.at[k], receive.at[k], peer)
+        for k, peer in enumerate(peers)
+    ]
+    blocks = push(
+        blocks_hbm.at[pl.ds((1 - core) * n_fsdp, n_fsdp)],
+        other,
+        sems.at[1],
+        sems.at[2],
+        {"dp": flip(dp, 1)},
+    )
+    load.wait()
+    blocks.wait_recv()
+    for owner in range(n_fsdp):
+        sums_ref[owner] = (own[owner].astype(F32) + other[owner].astype(F32)).astype(BF16)
+    for copy in copies:
+        copy.wait()
+    total = parts[0]
+    for k in range(1, n_dp * n_fsdp):
+        total = total + parts[k]
+    total_ref[...] = total
+    blocks.wait_send()
+
+
+def sum_pair(part, blocks, counts, identity):
+    size = counts[0] * counts[1]
+    half = (counts[1], *blocks.shape[1:])
+    shape = jax.ShapeDtypeStruct
+    return pl.pallas_call(
+        functools.partial(sum_pair_kernel, counts),
+        out_shape=(shape(part.shape, F32), shape(half, BF16)),
+        in_specs=[VMEM_SPEC, ANY_SPEC],
+        out_specs=(VMEM_SPEC, VMEM_SPEC),
+        scratch_shapes=[
+            pltpu.VMEM((size, *part.shape), F32),
+            pltpu.VMEM(half, BF16),
+            pltpu.VMEM(half, BF16),
+            pltpu.SemaphoreType.DMA((size - 1,)),
+            pltpu.SemaphoreType.DMA((size - 1,)),
+            pltpu.SemaphoreType.DMA((3,)),
+        ],
+        compiler_params=comm_params(identity),
+        name="sum_pair",
+    )(part, blocks)
 
 
 def gather_kernel(
@@ -1345,12 +1416,24 @@
     feed_table_ref,
     left_hbm,
     right_hbm,
+    head_low_hbm,
+    dx1_hbm,
+    input_hbm,
+    head_weights_hbm,
+    coefficient_ref,
     grad_ref,
     slots_ref,
     rows_ref,
     table_ref,
+    out_hbm,
     left,
     right,
+    head_low,
+    dx1,
+    inputs,
+    head_weights,
+    out,
+    first_sums,
     pair_buf,
     cross_out,
     cross_buf,
@@ -1368,6 +1451,7 @@
     table_buf,
     table_part,
     table_dp,
+    feed_sum,
     load_sems,
     pair_send,
     pair_recv,
@@ -1406,8 +1490,50 @@
         pltpu.make_async_copy(left_hbm.at[core], left, load_sems.at[0]),
         pltpu.make_async_copy(right_hbm.at[core], right, load_sems.at[1]),
     ]
+    row_count = dx1.shape[0]
+    tile = tile_rows(row_count, 4)
+    tiles = row_count // tile
+    weight_load = pltpu.make_async_copy(head_weights_hbm, head_weights, load_sems.at[2])
+    weight_load.start()
+    tile_loads, tile_saves = [], []
+    for step in range(tiles):
+        rows = pl.ds(step * tile, tile)
+        sems = [load_sems.at[3 + 6 * step + index] for index in range(6)]
+        tile_loads.append(
+            [
+                pltpu.make_async_copy(head_low_hbm.at[part, rows], head_low.at[part, rows], sems[part])
+                for part in range(3)
+            ]
+            + [
+                pltpu.make_async_copy(dx1_hbm.at[rows], dx1.at[rows], sems[3]),
+                pltpu.make_async_copy(input_hbm.at[rows], inputs.at[rows], sems[4]),
+            ]
+        )
+        tile_saves.append(pltpu.make_async_copy(out.at[rows], out_hbm.at[rows], sems[5]))
+        for load in tile_loads[step]:
+            load.start()
     for load in loads:
         load.start()
+    first_sums[...] = jnp.zeros_like(first_sums)
+
+    def first_back(step):
+        rows = pl.ds(step * tile, tile)
+        if step == 0:
+            weight_load.wait()
+        for load in tile_loads[step]:
+            load.wait()
+        grad = None
+        for part in range(3):
+            lanes = slice(part * PAD_WIDTH, (part + 1) * PAD_WIDTH)
+            term = dot_lanes(head_low[part, rows, :], head_weights[:, lanes])
+            grad = term if grad is None else grad + term
+        unit, scale = centered(inputs[rows, :].astype(F32))
+        total = dx1[rows, :] + norm_back(grad * coefficient_ref[0:1, :], unit, scale)
+        out[rows, :] = total.astype(BF16)
+        tile_saves[step].start()
+        first_sums[0] += fold(grad * unit)
+        first_sums[1] += fold(grad)
+
     greet(peers + dp_peers)
 
     parts = list(reversed(range(n_fsdp // 2)))
@@ -1431,17 +1557,6 @@
                 pair_recv.at[side, part],
                 to_pair,
             )
-    pieces = feed_ref.shape[0] // n_dp
-    feeding = [
-        push(
-            feed_ref.at[pl.ds(flip(dp, k + 1) * pieces, pieces)],
-            feed_in.at[k],
-            feed_in_send.at[k],
-            feed_in_recv.at[k],
-            peer,
-        )
-        for k, peer in enumerate(dp_peers)
-    ]
     crossing = {}
     for part in parts:
         rows = part_rows(part)
@@ -1476,21 +1591,80 @@
                     peers[bits - 1],
                 )
 
-    for copy in feeding:
-        copy.wait_recv()
-    total = feed_ref[pl.ds(dp * pieces, pieces)].astype(F32)
-    for k in range(n_dp - 1):
-        total = total + feed_in[k].astype(F32)
+    pieces = feed_sum.shape[0] // 2
+    side = lax.div(dp, 2)
+    for piece in range(2 * pieces):
+        total = feed_ref[0, piece].astype(F32)
+        for owner in range(1, n_fsdp):
+            total = total + feed_ref[owner, piece].astype(F32)
+        feed_sum[piece] = total.astype(BF16)
+    feeding = push(
+        feed_sum.at[pl.ds((1 - side) * pieces, pieces)],
+        feed_in,
+        feed_in_send.at[0],
+        feed_in_recv.at[0],
+        to_across,
+    )
+    for step in range(tiles - tiles // 2):
+        first_back(step)
+    feeding.wait_recv()
+    total = feed_sum[pl.ds(side * pieces, pieces)].astype(F32) + feed_in[...].astype(F32)
     feed_buf[dp] = total.astype(BF16)
     feeds = [
         push(feed_buf.at[dp], feed_buf.at[dp], feed_send.at[k], feed_recv.at[k], peer)
         for k, peer in enumerate(dp_peers)
     ]
 
+    total = ring_out[owner_rows(fsdp), :].astype(F32)
+    for bits in range(1, n_fsdp):
+        ring[bits].wait_recv()
+        total = total + ring_buf[bits].astype(F32)
+    dp_buf[dp] = total
+    gathering = [
+        push(dp_buf.at[dp], dp_buf.at[dp], dp_send.at[k], dp_recv.at[k], peer)
+        for k, peer in enumerate(dp_peers)
+    ]
+    for step in range(tiles - tiles // 2, tiles - tiles // 4):
+        first_back(step)
+    for copy in feeds:
+        copy.wait_recv()
+    for place in range(n_dp):
+        for piece in range(pieces):
+            block = n_dp + (place % 2 * 2 + place // 2) * pieces + piece
+            grad_ref[block] = feed_buf[place, piece].astype(F32)
+    for copy in gathering:
+        copy.wait_recv()
+    for place in range(n_dp):
+        grad_ref[place] = dp_buf[place]
+
+    slotting = {}
+    for bits in reversed(range(n_fsdp)):
+        slot = 2 * flip(fsdp, bits) + core
+        block, filled = jnp.int32(0), jnp.int32(0)
+        for index in range(grad_ref.shape[0]):
+            here = place_ref[index] == slot
+            block = jnp.where(here, index, block)
+            filled = jnp.where(here, 1, filled)
+        value = (grad_ref[block] * filled.astype(F32)).astype(BF16)
+        if bits:
+            slot_out[bits - 1] = value
+            slotting[bits] = push(
+                slot_out.at[bits - 1],
+                slots.at[core, owner_rows(fsdp), :],
+                slot_send.at[bits - 1],
+                slot_recv.at[bits - 1],
+                peers[bits - 1],
+            )
+        else:
+            slots[core, owner_rows(fsdp), :] = value
+    for step in range(tiles - tiles // 4, tiles):
+        first_back(step)
     table_stage[...] = jnp.zeros_like(table_stage)
     for row, (source, first) in enumerate(TABLE_ROWS):
         ref = mix_table_ref if source == 0 else feed_table_ref
         table_stage[row : row + 1, :] = ref[first : first + 1, :]
+    for row in range(2):
+        table_stage[row : row + 1, :] = jnp.sum(first_sums[row], axis=0, keepdims=True)
     terms, rest = [], table_stage[...]
     for _ in range(3):
         term = rest.astype(BF16)
@@ -1519,56 +1693,6 @@
         for k, peer in enumerate(peers)
     ]
 
-    total = ring_out[owner_rows(fsdp), :].astype(F32)
-    for bits in range(1, n_fsdp):
-        ring[bits].wait_recv()
-        total = total + ring_buf[bits].astype(F32)
-    dp_buf[dp] = total
-    gathering = [
-        push(dp_buf.at[dp], dp_buf.at[dp], dp_send.at[k], dp_recv.at[k], peer)
-        for k, peer in enumerate(dp_peers)
-    ]
-    for copy in tabling:
-        copy.wait_recv()
-    total = table_buf[0]
-    for owner in range(1, n_fsdp):
-        total = total + table_buf[owner]
-    table_part[...] = total
-    table_dp[dp] = total
-    table_dps = [
-        push(table_part, table_dp.at[dp], table_dp_send.at[k], table_dp_recv.at[k], peer)
-        for k, peer in enumerate(dp_peers)
-    ]
-    for copy in feeds:
-        copy.wait_recv()
-    for place in range(n_dp):
-        for piece in range(pieces):
-            grad_ref[n_dp + place * pieces + piece] = feed_buf[place, piece].astype(F32)
-    for copy in gathering:
-        copy.wait_recv()
-    for place in range(n_dp):
-        grad_ref[place] = dp_buf[place]
-
-    slotting = {}
-    for bits in reversed(range(n_fsdp)):
-        slot = 2 * flip(fsdp, bits) + core
-        block, filled = jnp.int32(0), jnp.int32(0)
-        for index in range(grad_ref.shape[0]):
-            here = place_ref[index] == slot
-            block = jnp.where(here, index, block)
-            filled = jnp.where(here, 1, filled)
-        value = (grad_ref[block] * filled.astype(F32)).astype(BF16)
-        if bits:
-            slot_out[bits - 1] = value
-            slotting[bits] = push(
-                slot_out.at[bits - 1],
-                slots.at[core, owner_rows(fsdp), :],
-                slot_send.at[bits - 1],
-                slot_recv.at[bits - 1],
-                peers[bits - 1],
-            )
-        else:
-            slots[core, owner_rows(fsdp), :] = value
     for load in loads:
         load.wait()
     left_parts, right_parts = split(left[...]), split(right[...])
@@ -1592,18 +1716,29 @@
             peers[bits - 1],
         )
     rows_buf[2 * fsdp + core] = steps[owner_rows(fsdp), :]
+    for copy in tabling:
+        copy.wait_recv()
+    total = table_buf[0]
+    for owner in range(1, n_fsdp):
+        total = total + table_buf[owner]
+    table_part[...] = total
+    table_dp[dp] = total
+    table_dps = [
+        push(table_part, table_dp.at[dp], table_dp_send.at[k], table_dp_recv.at[k], peer)
+        for k, peer in enumerate(dp_peers)
+    ]
+    lasts = []
+    for bits in range(n_fsdp):
+        if bits:
+            back[bits].wait_recv()
+        part = rows_buf.at[2 * flip(fsdp, bits) + core]
+        lasts.append(push(part, part, last_send.at[bits], last_recv.at[bits], to_pair))
     for copy in table_dps:
         copy.wait_recv()
     total = table_dp[0]
     for place in range(1, n_dp):
         total = total + table_dp[place]
     table_ref[...] = total
-    lasts = []
-    for bits in range(n_fsdp):
-        if bits:
-            back[bits].wait_recv()
-        part = rows_buf.at[2 * flip(fsdp, bits) + core]
-        lasts.append(push(part, part, last_send.at[bits], last_recv.at[bits], to_pair))
     for copy in twins:
         copy.wait_recv()
     slots_ref[...] = slots[...]
@@ -1611,21 +1746,28 @@
         copy.wait_recv()
     rows_ref[...] = rows_buf[...]
     copies = [*pairing.values(), *crossing.values(), *ring.values(), *slotting.values()]
-    copies += [*back.values(), *feeding, *feeds, *tabling, *table_dps, *gathering]
+    copies += [*back.values(), feeding, *feeds, *tabling, *table_dps, *gathering]
     for copy in copies + twins + lasts:
         copy.wait_send()
-
-
-def settle(places, mix, feed, mix_table, feed_table, left, right, counts, identity):
+    for save in tile_saves:
+        save.wait()
+
+
+def settle(
+    places, mix, feed, mix_table, feed_table, left, right, back, coefficients, counts, identity
+):
+    head_low, dx1, inputs, head_weights = back
+    row_count = dx1.shape[0]
+    tiles = row_count // tile_rows(row_count, 4)
     n_dp, n_fsdp = counts
     width = mix.shape[2]
     shard = width // n_fsdp
-    blocks = n_dp + feed.shape[0]
-    pieces = feed.shape[0] // n_dp
+    blocks = n_dp + 2 * feed.shape[1]
+    pieces = feed.shape[1] // 2
     inner, outer = n_fsdp - 1, n_dp - 1
     shape = jax.ShapeDtypeStruct
     dma = pltpu.SemaphoreType.DMA
-    sizes = [(2, n_fsdp // 2), (n_fsdp // 2,), (inner,), (outer,), (outer,), (outer,)]
+    sizes = [(2, n_fsdp // 2), (n_fsdp // 2,), (inner,), (1,), (outer,), (outer,)]
     sizes += [(inner,), (n_fsdp,), (inner,), (n_fsdp,), (inner,), (outer,)]
     return pl.pallas_call(
         functools.partial(settle_kernel, counts),
@@ -1634,18 +1776,25 @@
             shape((2, width, width), BF16),
             shape((2 * n_fsdp, shard, width), BF16),
             shape((32, LANES), F32),
+            shape(inputs.shape, BF16),
         ),
-        in_specs=[SMEM_SPEC] + [VMEM_SPEC] * 4 + [ANY_SPEC] * 2,
-        out_specs=(VMEM_SPEC,) * 4,
+        in_specs=[SMEM_SPEC] + [VMEM_SPEC] * 4 + [ANY_SPEC] * 6 + [VMEM_SPEC],
+        out_specs=(VMEM_SPEC,) * 4 + (ANY_SPEC,),
         scratch_shapes=[
             pltpu.VMEM((width, width), F32),
             pltpu.VMEM((width, width), F32),
+            pltpu.VMEM(head_low.shape, BF16),
+            pltpu.VMEM(dx1.shape, F32),
+            pltpu.VMEM(inputs.shape, BF16),
+            pltpu.VMEM(head_weights.shape, BF16),
+            pltpu.VMEM(inputs.shape, BF16),
+            pltpu.VMEM((2, 8, width), F32),
             pltpu.VMEM((2, width, width), BF16),
             pltpu.VMEM((width, width), BF16),
             pltpu.VMEM((width, width), BF16),
             pltpu.VMEM((width, width), BF16),
             pltpu.VMEM((n_fsdp, shard, width), BF16),
-            pltpu.VMEM((outer, pieces, shard, width), BF16),
+            pltpu.VMEM((pieces, shard, width), BF16),
             pltpu.VMEM((n_dp, pieces, shard, width), BF16),
             pltpu.VMEM((n_dp, shard, width), F32),
             pltpu.VMEM((inner, shard, width), BF16),
@@ -1657,12 +1806,13 @@
             pltpu.VMEM((n_fsdp, 32, LANES), F32),
             pltpu.VMEM((32, LANES), F32),
             pltpu.VMEM((n_dp, 32, LANES), F32),
-            dma((2,)),
+            pltpu.VMEM(feed.shape[1:], BF16),
+            dma((3 + 6 * tiles,)),
         ]
         + [dma(size) for size in sizes for _ in range(2)],
         compiler_params=comm_params(identity),
         name="settle",
-    )(places, mix, feed, mix_table, feed_table, left, right)
+    )(places, mix, feed, mix_table, feed_table, left, right, *back, coefficients)
 
 
 def finish_kernel(
@@ -1677,11 +1827,13 @@
     left_hbm,
     right_hbm,
     masters_hbm,
+    tokens_hbm,
     grad_hbm,
     left_out_hbm,
     right_out_hbm,
     masters_out_hbm,
     low_hbm,
+    tokens_out_hbm,
     table_grad_ref,
     energy_out_ref,
     coefficient_out_ref,
@@ -1690,6 +1842,7 @@
     right,
     masters,
     low,
+    tokens,
     sems,
 ):
     slot_count = slots_ref.shape[0]
@@ -1705,12 +1858,15 @@
                 (right, right_out_hbm),
                 (masters, masters_out_hbm),
                 (low, low_hbm),
+                (tokens, tokens_out_hbm),
             )
         )
     ]
     load_left.start()
     load_right.start()
     load_masters.start()
+    load_tokens = pltpu.make_async_copy(tokens_hbm, tokens, sems.at[9])
+    load_tokens.start()
     saves[0].start()
     load_left.wait()
     for slot in range(slot_count):
@@ -1728,6 +1884,8 @@
             + (1.0 - covariance_forgetting) * dot_rows(grad, grad)
         )
     saves[2].start()
+    load_tokens.wait()
+    saves[5].start()
     load_masters.wait()
     for block in range(masters.shape[0]):
         value = masters[block] - weight_rate * rows_ref[place_ref[block]].astype(F32)
@@ -1756,7 +1914,9 @@
         save.wait()
 
 
-def finish(places, grads, slots, rows, table, energy, coefficients, sharps, left, right, masters):
+def finish(
+    places, grads, slots, rows, table, energy, coefficients, sharps, left, right, masters, tokens
+):
     shape = jax.ShapeDtypeStruct
     return pl.pallas_call(
         finish_kernel,
@@ -1766,23 +1926,25 @@
             shape(right.shape, F32),
             shape(masters.shape, F32),
             shape(masters.shape, BF16),
+            shape(tokens.shape, BF16),
             shape(energy.shape, F32),
             shape(energy.shape, F32),
             shape(energy.shape, F32),
             shape((3, sharps.shape[1]), F32),
         ),
-        in_specs=[SMEM_SPEC] + [VMEM_SPEC] * 7 + [ANY_SPEC] * 3,
-        out_specs=(ANY_SPEC,) * 5 + (VMEM_SPEC,) * 4,
+        in_specs=[SMEM_SPEC] + [VMEM_SPEC] * 7 + [ANY_SPEC] * 4,
+        out_specs=(ANY_SPEC,) * 6 + (VMEM_SPEC,) * 4,
         scratch_shapes=[
             pltpu.VMEM(left.shape, F32),
             pltpu.VMEM(right.shape, F32),
             pltpu.VMEM(masters.shape, F32),
             pltpu.VMEM(masters.shape, BF16),
-            pltpu.SemaphoreType.DMA((8,)),
+            pltpu.VMEM(tokens.shape, BF16),
+            pltpu.SemaphoreType.DMA((10,)),
         ],
         compiler_params=pltpu.CompilerParams(vmem_limit_bytes=VMEM_LIMIT),
         name="finish",
-    )(places, grads, slots, rows, table, energy, coefficients, sharps, left, right, masters)
+    )(places, grads, slots, rows, table, energy, coefficients, sharps, left, right, masters, tokens)
 
 
 def shards(
@@ -1808,7 +1970,7 @@
     direct = counts[0] == 4 and slot_count == 2 and shard_rows % 16 == 0
     if direct:
         mixing_blocks, table = gather_start(projection_masters, channel_coefficients, counts, 0)
-        grad_shape = (counts[1], block_count - 4, shard_rows, feature_count)
+        grad_shape = (2 * counts[1], (block_count - 4) // 2, shard_rows, feature_count)
     else:
         full_table = lax.all_gather(channel_coefficients.astype(BF16), "fsdp", axis=1, tiled=True)
         table = full_table.astype(F32)
@@ -1818,34 +1980,32 @@
         grad_shape = (1, block_count - 4, feature_count, feature_count)
     feed_blocks = lax.all_gather(projection_masters[4:].astype(BF16), "fsdp", axis=1, tiled=True)
 
-    def batch_total(part, identity):
-        if direct:
-            return sum_all(part, counts, identity)
-        return lax.psum(part, ("dp", "fsdp"))
-
-    x1, qkv, mixed, scores, attention, u, e, sums = mixing_forward(
+    x1, qkv, mixed, scores, attention, slope, e, sums = mixing_forward(
         view_side_tokens, head_sharpness, patch_embeddings, mixing_blocks, table
     )
-    batch_sums = batch_total(sums, 1)
+    batch_sums = sum_all(sums, counts, 1) if direct else lax.psum(sums, ("dp", "fsdp"))
     layer_output, dx2, dn, feed_grad, feed_table, back_part = feed_forward(
         view_side_tokens, x1, e, batch_sums, feed_blocks, table, output_adjoint, grad_shape
     )
-    back_sums = batch_total(back_part, 2)
-    incoming_tokens_grad, mixing_grad, mixing_table = mixing_backward(
+    if direct:
+        back_sums, feed_grad = sum_pair(back_part, feed_grad, counts, 2)
+        feed_grad = lax.all_to_all(feed_grad, "fsdp", 0, 0, tiled=True)
+    else:
+        back_sums = lax.psum(back_part, ("dp", "fsdp"))
+    head_low, dx1, head_weights, mixing_grad, mixing_table = mixing_backward(
         view_side_tokens,
         head_sharpness,
         patch_embeddings,
         mixing_blocks,
         table,
-        (x1, qkv, mixed, scores, attention, u),
+        (x1, qkv, mixed, scores, attention, slope, e),
         batch_sums,
         dx2,
         dn,
         back_sums,
     )
     if direct:
-        feed_grad = lax.psum_scatter(feed_grad, "fsdp", scatter_dimension=0, tiled=True)[0]
-        grads, owned_grad, my_rows, table_total = settle(
+        grads, owned_grad, my_rows, table_total, tokens_grad = settle(
             storage_position_map,
             mixing_grad,
             feed_grad,
@@ -1853,6 +2013,8 @@
             feed_table,
             leading_root_preconditioner,
             trailing_root_preconditioner,
+            (head_low, dx1, patch_embeddings, head_weights),
+            table,
             counts,
             3,
         )
@@ -1868,8 +2030,20 @@
             leading_covariance,
             trailing_covariance,
             projection_masters,
+            tokens_grad,
         )
-        return (layer_output, incoming_tokens_grad, *results, *sharps)
+        tokens_grad = results.pop(5)
+        return (layer_output, tokens_grad, *results, *sharps)
+    first_grad = jnp.einsum(
+        "stl,dsl->td",
+        head_low,
+        head_weights.reshape(feature_count, 3, PAD_WIDTH),
+        preferred_element_type=F32,
+    )
+    unit, scale = centered(patch_embeddings.astype(F32))
+    incoming_tokens_grad = (dx1 + norm_back(first_grad * table[0], unit, scale)).astype(BF16)
+    mixing_table = mixing_table.at[0].set(jnp.sum(first_grad * unit, axis=0))
+    mixing_table = mixing_table.at[1].set(jnp.sum(first_grad, axis=0))
     sharpness_share = mixing_table[14, 0:HEAD_NUMBER]
     table_grad = jnp.stack([(mixing_table, feed_table)[source][row] for source, row in TABLE_ROWS])
     block_grad = jnp.concatenate([mixing_grad, feed_grad[0]], axis=0).astype(F32)

time: 249 us -> 243 us (0.976)
  waiting for transfers between devices: 6.85 us -> 0.04 us
  starting transfers between devices: 0.08 us -> 3.83 us
  Pallas kernels: 222 us -> 219 us
    pallas_call x2 -> x1, Pallas kernels: 32 us -> 18.6 us  [sum_all(): pl.pallas_call(functools.partial(sum_all_kernel, counts), out_shape=jax.S...]
    pallas_call x1, Pallas kernels: 45.4 us -> 54.8 us  [settle(): pl.pallas_call(functools.partial(settle_kernel, counts), out_shape=(shape...]
    reduce_scatter x1 -> x0, waiting for transfers between devices: 6.8 us -> none  [shards(): lax.psum_scatter(feed_grad, 'fsdp', scatter_dimension=0, tiled=True)[0]]
    pallas_call x1 -> x2, Pallas kernels: 49.5 us -> 56 us  [the longest x1 37.5 us: mixing_backward(): pl.pallas_call(mixing_backward_kernel, out_shape=(shape((3, row_count, PA...]
    pallas_call x1, Pallas kernels: 41.9 us -> 37.9 us  [feed_forward(): pl.pallas_call(feed_kernel, out_shape=(shape((row_count, width), BF16), s...]
    all_to_all x0 -> x1, starting transfers between devices: none -> 3.8 us  [shards(): feed_grad = lax.all_to_all(feed_grad, 'fsdp', 0, 0, tiled=True)]
  transfers between devices with their start and end apart: 2 -> 2, of which waited for: 1 -> 0; matrix products, arithmetic and copies ran while one was open for 0% -> 0% of each run, Pallas kernels for 52% -> 42%
where the time goes in v5:
time: 243 us; the launch traced here: 242 us
  Pallas kernels  219 us (90%)
  between operations  14.2 us (6%)
  local copies, waits for them, and re-layouts  4.14 us (2%)
  starting transfers between devices  3.83 us (2%)
    pallas_call x1, Pallas kernels, settle(): pl.pallas_call(functools.partial(settle_kernel, counts), out_shape=(shape...  54.8 us
    pallas_call x1, Pallas kernels, feed_forward(): pl.pallas_call(feed_kernel, out_shape=(shape((row_count, width), BF16), s...  37.9 us
    pallas_call x1, Pallas kernels, mixing_backward(): pl.pallas_call(mixing_backward_kernel, out_shape=(shape((3, row_count, PA...  37.5 us
    pallas_call x1, Pallas kernels, mixing_forward(): pl.pallas_call(mixing_forward_kernel, out_shape=(shape((row_count, width)...  23.1 us
    pallas_call x1, Pallas kernels, gather_start(): pl.pallas_call(functools.partial(gather_kernel, counts), out_shape=(shape...  21.6 us
    pallas_call x1, Pallas kernels, sum_all(): pl.pallas_call(functools.partial(sum_all_kernel, counts), out_shape=jax.S...  18.6 us
    pallas_call x1, Pallas kernels, sum_pair(): pl.pallas_call(functools.partial(sum_pair_kernel, counts), out_shape=(sha...  18.5 us
    pallas_call x1, Pallas kernels, finish(): pl.pallas_call(finish_kernel, out_shape=(shape(grads.shape, F32), shape(l...  6.9 us
  transfers between devices with their start and end apart: 2, of which 0 were waited for; matrix products, arithmetic and copies ran while one was open for 0% of the time, Pallas kernels for 42%

profile of v5, /device:TPU:1, one launch (start us, length us, event | category | flops | bytes accessed | tf_op | source)
XLA Modules:
  0.0 241.7 jit_solution(1587991476281026323)
XLA Ops:
  7.2 0.0 all-gather.2.cloned.1.call-start
  7.2 1.8 slice.7
  9.0 0.0 all-gather.2.cloned.1.call-update
  9.1 21.6 %gather_start.1 = (bf16[4,384,384]{2,1,0:T(8,128)(2,1)}, f32[32,384]{1,0:T(8,128)}) custom-call(f32[12,48,384]{2,1,0:T(8,128)} %masters_hbm.1, f32[29,48]{1,0:T(8,128)} %coefficient_ref.1), custom_call_target="tpu_custom_call" | custom-call | tf_op jit(solution)/shard_map/gather_start/pallas_call | solution.py:1374
  30.7 23.1 %mixing_forward.1 = (f32[1856,384]{1,0:T(8,128)}, f32[1856,1536]{1,0:T(8,128)}, bf16[1856,512]{1,0:T(8,128)(2,1)}, f32[16,4,48,128]{3,2,1,0:T(8,128)}, f32[16,4,...) custom-call(s32[16]{0:T(128)} %sides_ref.5, f32[8]{0:T(128)} %sharp_ref.3, ...), custom_call_target="tpu_custom_call" | custom-call | tf_op jit(solution)/shard_map/mixing_forward/pallas_call | solution.py:477
  53.8 18.6 %sum_all.1.bn_ref = f32[8,128]{1,0:T(8,128)} custom-call(f32[8,128]{1,0:T(8,128)} %get-tuple-element.55.part_ref), custom_call_target="tpu_custom_call" | custom-call | tf_op jit(solution)/shard_map/sum_all/pallas_call | solution.py:1214
  72.4 0.0 all-gather.2.cloned.1.call-done.weight_hbm
  72.5 37.9 %feed_forward.1 = (bf16[1856,384]{1,0:T(8,128)(2,1)}, f32[1856,384]{1,0:T(8,128)}, f32[3,1856,128]{2,1,0:T(8,128)}, bf16[16,4,48,384]{3,2,1,0:T(8,128)(2,1)}, f32[16,384]{1,0:T(8,128)}, /*index=5*/f32[8,128]{1,0:T(8,128)}) custom-call(s32[16]{0:T(128)} %sides_ref.5, f32[1856,384]{1,0:T(8,128)} %get-tuple-element.53.x1_hbm, ...), custom_call_target="tpu_custom_call" | custom-call | tf_op jit(solution)/shard_map/feed_forward/pallas_call | solution.py:752
  110.4 18.5 %sum_pair.1 = (f32[8,128]{1,0:T(8,128)}, bf16[8,4,48,384]{3,2,1,0:T(8,128)(2,1)}) custom-call(f32[8,128]{1,0:T(8,128)} %get-tuple-element.64.part_ref, bf16[16,4,48,384]{3,2,1,0:T(8,128)(2,1)} %get-tuple-element.65.blocks_hbm), custom_call_target="tpu_custom_call" | custom-call | tf_op jit(solution)/shard_map/sum_pair/pallas_call | solution.py:1274
  128.9 0.0 copy-start.1
  128.9 0.0 copy-start.2
  128.9 3.8 %all-to-all-start = ((bf16[8,4,48,384]{3,2,1,0:T(8,128)(2,1)}), bf16[8,4,48,384]{3,2,1,0:T(8,128)(2,1)S(1)}, u32[]{:S(2)}, u32[]{:S(2)}) async-start(bf16[8,4,48,384]{3,2,1,0:T(8,128)(2,1)} %get-tuple-element.68), calls=%async_computation | async-start | bytes 2359296 | tf_op jit(solution)/shard_map/all_to_all | solution.py:1992
  132.7 0.0 copy-done.1
  132.7 0.0 copy-done.2
  132.7 0.6 pad_maximum_fusion.sharp_ref
  133.3 37.5 %mixing_backward.1 = (bf16[3,1856,512]{2,1,0:T(8,128)(2,1)}, f32[1856,384]{1,0:T(8,128)}, bf16[384,1536]{1,0:T(8,128)(2,1)}, bf16[4,384,384]{2,1,0:T(8,128)(2,1)}, f32[16,384]{1,0:T(8,128)}) custom-call(s32[16]{0:T(128)} %sides_ref.5, f32[8]{0:T(128)} %sharp_ref.3, bf16[1856,384]{1,0:T(8,128)(2,1)} %input_hbm.3, ...), custom_call_target="tpu_custom_call" | custom-call | tf_op jit(solution)/shard_map/mixing_backward/pallas_call | solution.py:1081
  170.8 0.0 all-to-all-done.feed_ref
  170.8 0.0 copy-start
  170.8 1.0 copy-done
  171.8 54.8 %settle.1 = (f32[12,48,384]{2,1,0:T(8,128)}, bf16[2,384,384]{2,1,0:T(8,128)(2,1)}, bf16[16,48,384]{2,1,0:T(8,128)(2,1)}, f32[32,128]{1,0:T(8,128)}, bf16[1856,384]{1,0:T(8,128)(2,1)}) custom-call(s32[12]{0:T(128)} %place_ref.3, bf16[4,384,384]{2,1,0:T(8,128)(2,1)} %get-tuple-element.67.mix_ref, bf16[8,4,48,384]{3,2,1,0:T(8,128)(2,1)} %copy-done, ...), custom_call_target="tpu_custom_call" | custom-call | tf_op jit(solution)/shard_map/settle/pallas_call | solution.py:1772
  226.6 6.9 %finish.1 = (f32[12,48,384]{2,1,0:T(8,128)}, f32[2,384,384]{2,1,0:T(8,128)}, f32[2,384,384]{2,1,0:T(8,128)}, f32[12,48,384]{2,1,0:T(8,128)}, bf16[12,48,384]{2,1...) custom-call(s32[12]{0:T(128)} %place_ref.3, ...), custom_call_target="tpu_custom_call" | custom-call | tf_op jit(solution)/shard_map/finish/pallas_call | solution.py:1921
  233.5 1.3 slice_bitcast_fusion
Async XLA Ops:
  7.2 65.3 %all-gather.2.cloned.1.call-start = ((), (), s32[]{:S(2)}) async-start(), calls=%async_computation.1 | async-start | bytes 2654208 | tf_op jit(solution)/shard_map/all_gather | solution.py:1981
  128.9 3.8 %copy-start.1 = (f32[8]{0:T(128)S(1)}, f32[8]{0:T(128)}, u32[]{:S(2)}) copy-start(f32[8]{0:T(128)} %sharp_ref.3) | copy-start | bytes 100
  128.9 3.8 %copy-start.2 = (f32[8]{0:T(128)S(1)}, f32[8]{0:T(128)}, u32[]{:S(2)}) copy-start(f32[8]{0:T(128)} %param.24) | copy-start | bytes 100
  128.9 41.9 %all-to-all-start = ((bf16[8,4,48,384]{3,2,1,0:T(8,128)(2,1)}), bf16[8,4,48,384]{3,2,1,0:T(8,128)(2,1)S(1)}, u32[]{:S(2)}, u32[]{:S(2)}) async-start(bf16[8,4,48,384]{3,2,1,0:T(8,128)(2,1)} %get-tuple-element.68), calls=%async_computation | async-start | bytes 2359296 | tf_op jit(solution)/shard_map/all_to_all | solution.py:1992
  170.8 1.0 copy-start
Sparse Core Ops, SparseCore 0:
  10.8 52.9 all-gather.1

commit v6 on v5

--- a/solution.py
+++ b/solution.py
@@ -829,14 +829,16 @@
     head_low,
     spread,
     out_sum,
+    head_sum,
     sharp_sums,
     order_ref,
     start_ref,
     load_sems,
 ):
     row_count, width = input_hbm.shape
-    low_rows, input_ref = head_low.at[0, :, 0:width], head_low.at[1, :, 0:width]
-    input_load = pltpu.make_async_copy(input_hbm, input_ref, load_sems.at[14])
+    low_rows, input_ref = head_low.at[:, 0:width], head_low.at[:, PAD_WIDTH : PAD_WIDTH + width]
+    tile = tile_rows(row_count, 2)
+    input_load = pltpu.make_async_copy(input_hbm, input_ref, load_sems.at[11 + row_count // tile])
     input_load.start()
     chunks = width // LANES
     slope_ref, e_ref = pool.at[0:chunks], pool.at[chunks : 2 * chunks]
@@ -864,12 +866,16 @@
             (
                 (head_weights, head_weights_hbm),
                 (dx2_ref, dx1_hbm),
-                (head_low.at[0], head_low_hbm.at[0]),
-                (head_low.at[1], head_low_hbm.at[1]),
-                (head_low.at[2], head_low_hbm.at[2]),
             )
         )
     ]
+    for step in range(row_count // tile):
+        rows = pl.ds(step * tile, tile)
+        saves.append(
+            pltpu.make_async_copy(
+                head_low.at[rows], head_low_hbm.at[rows], load_sems.at[len(loads) + 3 + step]
+            )
+        )
     for load in loads:
         load.start()
     tile = tile_rows(row_count, 2)
@@ -1000,6 +1006,13 @@
             grad = split(jnp.where(keep, mixed_grad[rows, lanes[0]], 0.0))
             grads.append(grad)
             blocks.append(dot_split(dot_rows, value, grad))
+        value_grads = []
+        for index, (member, half) in enumerate(units_of):
+            for pair in range(2):
+                shares = attention_ref[members[member][0], 2 * half + pair]
+                spread_pair(spread, member, half, pair, shares)
+            shares = (spread[member, half, 0], spread[member, half, 1])
+            value_grads.append(dot_split(dot_lanes, grads[index], shares))
         for (member, half), block in zip(units_of, blocks):
             crop = members[member][0]
             query_sums = []
@@ -1009,7 +1022,6 @@
                 scores = scores_ref[crop, index]
                 part = pair_part(block, pair)
                 part = shares * (part - jnp.sum(part * shares, axis=0, keepdims=True))
-                spread_pair(spread, member, half, pair, shares)
                 total = jnp.sum(part * scores, axis=0, keepdims=True)
                 sharp_sums[index, pl.ds(crop, 1), :] = total
                 sharpness = pair_sharpness(sharp_ref, index)
@@ -1021,16 +1033,14 @@
             lanes = half_lanes(half)
             query, query_scale = units(jnp.where(keep, qkv_ref[rows, lanes[0]], 0.0))
             key, key_scale = units(jnp.where(keep, qkv_ref[rows, lanes[1]], 0.0))
-            shares = (spread[member, half, 0], spread[member, half, 1])
             slopes = (spread[member, 2 + half, 0], spread[member, 2 + half, 1])
-            value_grad = dot_split(dot_lanes, grads[index], shares)
             query_grad = dot_split(dot, split(key), slopes)
             query_grad = query_scale * (query_grad - query * sums[index])
             key_grad = dot_split(dot_lanes, split(query), slopes)
             key_grad = key_scale * (
                 key_grad - key * jnp.sum(key_grad * key, axis=0, keepdims=True)
             )
-            results.append((query_grad, key_grad, value_grad))
+            results.append((query_grad, key_grad, value_grads[index]))
         for (member, half), grads in zip(units_of, results):
             _, rows, keep = members[member]
             for part, result in enumerate(grads):
@@ -1052,22 +1062,16 @@
         total = jnp.where(lane == head, jnp.sum(row, axis=1, keepdims=True), total)
     grads_ref[14:15, 0:LANES] = total
 
+    head_sum[...] = jnp.zeros_like(head_sum)
+    for step in range(row_count // tile):
+        rows = pl.ds(step * tile, tile)
+        for chunk in range(3 * PAD_WIDTH // LANES):
+            head_low[rows, chunk_lanes(chunk)] = pool[chunk, rows, :].astype(BF16)
+        saves[2 + step].start()
+        head_sum[...] += dot_rows(first_low[rows, :], head_low[rows, :])
     for part in range(3):
-        out_sum[...] = jnp.zeros_like(out_sum)
-
-        @pl.loop(0, row_count // tile)
-        def _(step, part=part):
-            rows = pl.ds(pl.multiple_of(step * tile, 16), tile)
-            first = part * PAD_WIDTH // LANES
-            for chunk in range(PAD_WIDTH // LANES):
-                head_low[part, rows, chunk_lanes(chunk)] = pool[first + chunk, rows, :].astype(BF16)
-            out_sum[...] += dot_rows(head_low[part, rows, :], first_low[rows, :])
-
-        saves[2 + part].start()
-        low = out_sum[...].astype(BF16)
-        weight_grad_ref[part] = lax.dot_general(
-            low, mapping, (((0,), (1,)), ((), ())), preferred_element_type=F32
-        ).astype(BF16)
+        low = head_sum[:, part * PAD_WIDTH : (part + 1) * PAD_WIDTH].astype(BF16)
+        weight_grad_ref[part] = dot_lanes(low, mapping).astype(BF16)
     for save in saves:
         save.wait()
 
@@ -1081,7 +1085,7 @@
     return pl.pallas_call(
         mixing_backward_kernel,
         out_shape=(
-            shape((3, row_count, PAD_WIDTH), BF16),
+            shape((row_count, 3 * PAD_WIDTH), BF16),
             shape((row_count, width), F32),
             shape((width, 3 * PAD_WIDTH), BF16),
             shape((4, width, width), BF16),
@@ -1105,13 +1109,14 @@
             pltpu.VMEM((chunks, LEAD + row_count + TAIL, LANES), F32),
             pltpu.VMEM((row_count, PAD_WIDTH), F32),
             pltpu.VMEM((row_count, width), BF16),
-            pltpu.VMEM((3, row_count, PAD_WIDTH), BF16),
+            pltpu.VMEM((row_count, 3 * PAD_WIDTH), BF16),
             pltpu.VMEM((CROP_GROUP, 4, 2, HALF_WIDTH, HALF_WIDTH), BF16),
             pltpu.VMEM((PAD_WIDTH, width), F32),
+            pltpu.VMEM((width, 3 * PAD_WIDTH), F32),
             pltpu.VMEM((HEAD_PAIRS, crops, LANES), F32),
             pltpu.SMEM((2 * crops,), jnp.int32),
             pltpu.SMEM((crops,), jnp.int32),
-            pltpu.SemaphoreType.DMA((15,)),
+            pltpu.SemaphoreType.DMA((12 + row_count // tile_rows(row_count, 2),)),
         ],
         compiler_params=pltpu.CompilerParams(vmem_limit_bytes=VMEM_LIMIT),
         name="mixing_backward",
@@ -1410,8 +1415,8 @@
 def settle_kernel(
     counts,
     place_ref,
-    mix_ref,
-    feed_ref,
+    mix_hbm,
+    feed_hbm,
     mix_table_ref,
     feed_table_ref,
     left_hbm,
@@ -1421,9 +1426,9 @@
     input_hbm,
     head_weights_hbm,
     coefficient_ref,
-    grad_ref,
-    slots_ref,
-    rows_ref,
+    grad_hbm,
+    slots_hbm,
+    rows_hbm,
     table_ref,
     out_hbm,
     left,
@@ -1447,11 +1452,16 @@
     steps,
     rows_buf,
     table_stage,
+    table_rows,
     table_out,
     table_buf,
     table_part,
     table_dp,
     feed_sum,
+    mix,
+    feed_ref,
+    left_parts,
+    grad_ref,
     load_sems,
     pair_send,
     pair_recv,
@@ -1473,6 +1483,8 @@
     back_recv,
     last_send,
     last_recv,
+    table_rows_send,
+    table_rows_recv,
     table_send,
     table_recv,
     table_dp_send,
@@ -1480,7 +1492,7 @@
 ):
     n_dp, n_fsdp = counts
     dp, fsdp = lax.axis_index("dp"), lax.axis_index("fsdp")
-    width = mix_ref.shape[2]
+    width = mix_hbm.shape[2]
     shard = width // n_fsdp
     core = lax.rem(dp, 2)
     across, pair, pair_across = flip(dp, 2), flip(dp, 1), flip(dp, 3)
@@ -1490,6 +1502,14 @@
         pltpu.make_async_copy(left_hbm.at[core], left, load_sems.at[0]),
         pltpu.make_async_copy(right_hbm.at[core], right, load_sems.at[1]),
     ]
+    mix_loads = [
+        pltpu.make_async_copy(mix_hbm.at[across], mix.at[0], load_sems.at[3]),
+        pltpu.make_async_copy(mix_hbm.at[dp], mix.at[1], load_sems.at[4]),
+    ]
+    feed_load = pltpu.make_async_copy(feed_hbm, feed_ref, load_sems.at[5])
+    for load in mix_loads:
+        load.start()
+    feed_load.start()
     row_count = dx1.shape[0]
     tile = tile_rows(row_count, 4)
     tiles = row_count // tile
@@ -1498,18 +1518,15 @@
     tile_loads, tile_saves = [], []
     for step in range(tiles):
         rows = pl.ds(step * tile, tile)
-        sems = [load_sems.at[3 + 6 * step + index] for index in range(6)]
+        sems = [load_sems.at[8 + 4 * step + index] for index in range(4)]
         tile_loads.append(
             [
-                pltpu.make_async_copy(head_low_hbm.at[part, rows], head_low.at[part, rows], sems[part])
-                for part in range(3)
-            ]
-            + [
-                pltpu.make_async_copy(dx1_hbm.at[rows], dx1.at[rows], sems[3]),
-                pltpu.make_async_copy(input_hbm.at[rows], inputs.at[rows], sems[4]),
+                pltpu.make_async_copy(head_low_hbm.at[rows], head_low.at[rows], sems[0]),
+                pltpu.make_async_copy(dx1_hbm.at[rows], dx1.at[rows], sems[1]),
+                pltpu.make_async_copy(input_hbm.at[rows], inputs.at[rows], sems[2]),
             ]
         )
-        tile_saves.append(pltpu.make_async_copy(out.at[rows], out_hbm.at[rows], sems[5]))
+        tile_saves.append(pltpu.make_async_copy(out.at[rows], out_hbm.at[rows], sems[3]))
         for load in tile_loads[step]:
             load.start()
     for load in loads:
@@ -1522,11 +1539,7 @@
             weight_load.wait()
         for load in tile_loads[step]:
             load.wait()
-        grad = None
-        for part in range(3):
-            lanes = slice(part * PAD_WIDTH, (part + 1) * PAD_WIDTH)
-            term = dot_lanes(head_low[part, rows, :], head_weights[:, lanes])
-            grad = term if grad is None else grad + term
+        grad = dot_lanes(head_low[rows, :], head_weights[...])
         unit, scale = centered(inputs[rows, :].astype(F32))
         total = dx1[rows, :] + norm_back(grad * coefficient_ref[0:1, :], unit, scale)
         out[rows, :] = total.astype(BF16)
@@ -1551,18 +1564,20 @@
         rows = part_rows(part)
         for side, block in enumerate((pair_across, pair)):
             pairing[part, side] = push(
-                mix_ref.at[block, rows],
+                mix_hbm.at[block, rows],
                 pair_buf.at[side, rows],
                 pair_send.at[side, part],
                 pair_recv.at[side, part],
                 to_pair,
             )
+    for load in mix_loads:
+        load.wait()
     crossing = {}
     for part in parts:
         rows = part_rows(part)
         pairing[part, 0].wait_recv()
         cross_out[rows, :] = (
-            mix_ref[across, rows, :].astype(F32) + pair_buf[0, rows, :].astype(F32)
+            mix[0, rows, :].astype(F32) + pair_buf[0, rows, :].astype(F32)
         ).astype(BF16)
         crossing[part] = push(
             cross_out.at[rows],
@@ -1577,7 +1592,7 @@
         pairing[part, 1].wait_recv()
         crossing[part].wait_recv()
         ring_out[rows, :] = (
-            mix_ref[dp, rows, :].astype(F32)
+            mix[1, rows, :].astype(F32)
             + pair_buf[1, rows, :].astype(F32)
             + cross_buf[rows, :].astype(F32)
         ).astype(BF16)
@@ -1593,6 +1608,7 @@
 
     pieces = feed_sum.shape[0] // 2
     side = lax.div(dp, 2)
+    feed_load.wait()
     for piece in range(2 * pieces):
         total = feed_ref[0, piece].astype(F32)
         for owner in range(1, n_fsdp):
@@ -1624,8 +1640,32 @@
         push(dp_buf.at[dp], dp_buf.at[dp], dp_send.at[k], dp_recv.at[k], peer)
         for k, peer in enumerate(dp_peers)
     ]
-    for step in range(tiles - tiles // 2, tiles - tiles // 4):
+    for step in range(tiles - tiles // 2, tiles):
         first_back(step)
+
+    table_stage[...] = jnp.zeros_like(table_stage)
+    for row, (source, first) in enumerate(TABLE_ROWS):
+        ref = mix_table_ref if source == 0 else feed_table_ref
+        table_stage[row : row + 1, :] = ref[first : first + 1, :]
+    for row in range(2):
+        table_stage[row : row + 1, :] = jnp.sum(first_sums[row], axis=0, keepdims=True)
+    table_stage[31:32, :] = mix_table_ref[14:15, :]
+    quarter = table_stage.shape[0] // n_dp
+
+    def quarter_rows(place):
+        return pl.ds(pl.multiple_of(place * quarter, 8), quarter)
+
+    table_rows[dp] = table_stage[quarter_rows(dp), :]
+    quartering = [
+        push(
+            table_stage.at[quarter_rows(flip(dp, step + 1))],
+            table_rows.at[dp],
+            table_rows_send.at[step],
+            table_rows_recv.at[step],
+            peer,
+        )
+        for step, peer in enumerate(dp_peers)
+    ]
     for copy in feeds:
         copy.wait_recv()
     for place in range(n_dp):
@@ -1636,6 +1676,8 @@
         copy.wait_recv()
     for place in range(n_dp):
         grad_ref[place] = dp_buf[place]
+    tile_saves.append(pltpu.make_async_copy(grad_ref, grad_hbm, load_sems.at[6 + 2 + 4 * tiles]))
+    tile_saves[-1].start()
 
     slotting = {}
     for bits in reversed(range(n_fsdp)):
@@ -1657,45 +1699,43 @@
             )
         else:
             slots[core, owner_rows(fsdp), :] = value
-    for step in range(tiles - tiles // 4, tiles):
-        first_back(step)
-    table_stage[...] = jnp.zeros_like(table_stage)
-    for row, (source, first) in enumerate(TABLE_ROWS):
-        ref = mix_table_ref if source == 0 else feed_table_ref
-        table_stage[row : row + 1, :] = ref[first : first + 1, :]
-    for row in range(2):
-        table_stage[row : row + 1, :] = jnp.sum(first_sums[row], axis=0, keepdims=True)
-    terms, rest = [], table_stage[...]
+    for copy in quartering:
+        copy.wait_recv()
+    rest = table_rows[0]
+    for place in range(1, n_dp):
+        rest = rest + table_rows[place]
+    sharp_row = lax.broadcasted_iota(jnp.int32, (quarter, LANES), 0) + dp * quarter == 31
+    sharp_values = jnp.broadcast_to(rest[quarter - 1 : quarter, 0:LANES], (quarter, LANES))
+    terms = []
     for _ in range(3):
-        term = rest.astype(BF16)
+        term = rest.astype(BF16).astype(F32)
         terms.append(term)
-        rest = rest - term.astype(F32)
-    terms = jnp.concatenate(terms, axis=0)
+        rest = rest - term
+    terms = jnp.concatenate(terms, axis=0).astype(BF16)
     columns = width // n_fsdp
-    sharp_row = lax.broadcasted_iota(jnp.int32, (32, LANES), 0) == 31
-    sharp_values = jnp.broadcast_to(mix_table_ref[14:15, 0:LANES], (32, LANES))
     for owner in range(n_fsdp):
         lane = lax.broadcasted_iota(jnp.int32, (width, LANES), 1)
         source = lax.broadcasted_iota(jnp.int32, (width, LANES), 0)
         hit = ((lane < columns) & (lane + owner * columns == source)).astype(F32).astype(BF16)
         value = dot(terms, hit)
-        value = value[0:32] + value[32:64] + value[64:96]
+        value = value[0:quarter] + value[quarter : 2 * quarter] + value[2 * quarter :]
         table_out[owner] = jnp.where(sharp_row, sharp_values, value)
     table_buf[fsdp] = table_out[fsdp]
     tabling = [
         push(
-            table_out.at[flip(fsdp, k + 1)],
+            table_out.at[flip(fsdp, step + 1)],
             table_buf.at[fsdp],
-            table_send.at[k],
-            table_recv.at[k],
+            table_send.at[step],
+            table_recv.at[step],
             peer,
         )
-        for k, peer in enumerate(peers)
+        for step, peer in enumerate(peers)
     ]
-
     for load in loads:
         load.wait()
-    left_parts, right_parts = split(left[...]), split(right[...])
+    right_parts = split(right[...])
+    for index, value in enumerate(split(left[...])):
+        left_parts[index] = value
     twins = []
     for bits in range(n_fsdp):
         if bits:
@@ -1704,17 +1744,20 @@
         twins.append(push(part, part, twin_send.at[bits], twin_recv.at[bits], to_pair))
 
     grad = slots[core]
-    half = split(dot(left_parts[0], grad) + dot(left_parts[1], grad))
-    steps[...] = dot_split(dot, half, right_parts).astype(BF16)
     back = {}
-    for bits in reversed(range(1, n_fsdp)):
-        back[bits] = push(
-            steps.at[owner_rows(flip(fsdp, bits))],
-            rows_buf.at[2 * fsdp + core],
-            back_send.at[bits - 1],
-            back_recv.at[bits - 1],
-            peers[bits - 1],
-        )
+    for part in parts:
+        rows = part_rows(part)
+        half = split(dot(left_parts[0, rows, :], grad) + dot(left_parts[1, rows, :], grad))
+        steps[rows, :] = dot_split(dot, half, right_parts).astype(BF16)
+        for bits in (2 * part + 1, 2 * part):
+            if bits:
+                back[bits] = push(
+                    steps.at[owner_rows(flip(fsdp, bits))],
+                    rows_buf.at[2 * fsdp + core],
+                    back_send.at[bits - 1],
+                    back_recv.at[bits - 1],
+                    peers[bits - 1],
+                )
     rows_buf[2 * fsdp + core] = steps[owner_rows(fsdp), :]
     for copy in tabling:
         copy.wait_recv()
@@ -1735,18 +1778,18 @@
         lasts.append(push(part, part, last_send.at[bits], last_recv.at[bits], to_pair))
     for copy in table_dps:
         copy.wait_recv()
-    total = table_dp[0]
-    for place in range(1, n_dp):
-        total = total + table_dp[place]
-    table_ref[...] = total
+    for place in range(n_dp):
+        table_ref[place * quarter : (place + 1) * quarter, :] = table_dp[place]
     for copy in twins:
         copy.wait_recv()
-    slots_ref[...] = slots[...]
+    tile_saves.append(pltpu.make_async_copy(slots, slots_hbm, load_sems.at[6]))
+    tile_saves[-1].start()
     for copy in lasts:
         copy.wait_recv()
-    rows_ref[...] = rows_buf[...]
+    tile_saves.append(pltpu.make_async_copy(rows_buf, rows_hbm, load_sems.at[7]))
+    tile_saves[-1].start()
     copies = [*pairing.values(), *crossing.values(), *ring.values(), *slotting.values()]
-    copies += [*back.values(), feeding, *feeds, *tabling, *table_dps, *gathering]
+    copies += [*back.values(), feeding, *feeds, *quartering, *tabling, *table_dps, *gathering]
     for copy in copies + twins + lasts:
         copy.wait_send()
     for save in tile_saves:
@@ -1768,7 +1811,7 @@
     shape = jax.ShapeDtypeStruct
     dma = pltpu.SemaphoreType.DMA
     sizes = [(2, n_fsdp // 2), (n_fsdp // 2,), (inner,), (1,), (outer,), (outer,)]
-    sizes += [(inner,), (n_fsdp,), (inner,), (n_fsdp,), (inner,), (outer,)]
+    sizes += [(inner,), (n_fsdp,), (inner,), (n_fsdp,), (outer,), (inner,), (outer,)]
     return pl.pallas_call(
         functools.partial(settle_kernel, counts),
         out_shape=(
@@ -1778,8 +1821,8 @@
             shape((32, LANES), F32),
             shape(inputs.shape, BF16),
         ),
-        in_specs=[SMEM_SPEC] + [VMEM_SPEC] * 4 + [ANY_SPEC] * 6 + [VMEM_SPEC],
-        out_specs=(VMEM_SPEC,) * 4 + (ANY_SPEC,),
+        in_specs=[SMEM_SPEC] + [ANY_SPEC] * 2 + [VMEM_SPEC] * 2 + [ANY_SPEC] * 6 + [VMEM_SPEC],
+        out_specs=(ANY_SPEC,) * 3 + (VMEM_SPEC, ANY_SPEC),
         scratch_shapes=[
             pltpu.VMEM((width, width), F32),
             pltpu.VMEM((width, width), F32),
@@ -1802,12 +1845,17 @@
             pltpu.VMEM((width, width), BF16),
             pltpu.VMEM((2 * n_fsdp, shard, width), BF16),
             pltpu.VMEM((32, width), F32),
-            pltpu.VMEM((n_fsdp, 32, LANES), F32),
-            pltpu.VMEM((n_fsdp, 32, LANES), F32),
-            pltpu.VMEM((32, LANES), F32),
-            pltpu.VMEM((n_dp, 32, LANES), F32),
+            pltpu.VMEM((n_dp, 32 // n_dp, width), F32),
+            pltpu.VMEM((n_fsdp, 32 // n_dp, LANES), F32),
+            pltpu.VMEM((n_fsdp, 32 // n_dp, LANES), F32),
+            pltpu.VMEM((32 // n_dp, LANES), F32),
+            pltpu.VMEM((n_dp, 32 // n_dp, LANES), F32),
             pltpu.VMEM(feed.shape[1:], BF16),
-            dma((3 + 6 * tiles,)),
+            pltpu.VMEM((2, width, width), BF16),
+            pltpu.VMEM(feed.shape, BF16),
+            pltpu.VMEM((2, width, width), BF16),
+            pltpu.VMEM((blocks, shard, width), F32),
+            dma((9 + 4 * tiles,)),
         ]
         + [dma(size) for size in sizes for _ in range(2)],
         compiler_params=comm_params(identity),
@@ -1817,13 +1865,14 @@
 
 def finish_kernel(
     place_ref,
-    grad_ref,
-    slots_ref,
-    rows_ref,
     table_ref,
     energy_ref,
     coefficient_ref,
     sharp_ref,
+    sharp_energy_ref,
+    grads_hbm,
+    slots_hbm,
+    rows_hbm,
     left_hbm,
     right_hbm,
     masters_hbm,
@@ -1837,15 +1886,24 @@
     table_grad_ref,
     energy_out_ref,
     coefficient_out_ref,
+    sharp_grad_ref,
+    sharp_energy_out_ref,
     sharp_out_ref,
     left,
     right,
     masters,
     low,
     tokens,
+    grad_ref,
+    slots_ref,
+    rows_ref,
     sems,
 ):
     slot_count = slots_ref.shape[0]
+    load_slots = pltpu.make_async_copy(slots_hbm, slots_ref, sems.at[10])
+    load_rows = pltpu.make_async_copy(rows_hbm, rows_ref, sems.at[11])
+    load_grads = pltpu.make_async_copy(grads_hbm, grad_ref, sems.at[12])
+    load_slots.start()
     load_left = pltpu.make_async_copy(left_hbm, left, sems.at[0])
     load_right = pltpu.make_async_copy(right_hbm, right, sems.at[1])
     load_masters = pltpu.make_async_copy(masters_hbm, masters, sems.at[2])
@@ -1864,10 +1922,12 @@
     ]
     load_left.start()
     load_right.start()
-    load_masters.start()
     load_tokens = pltpu.make_async_copy(tokens_hbm, tokens, sems.at[9])
     load_tokens.start()
-    saves[0].start()
+    load_grads.start()
+    load_masters.start()
+    load_rows.start()
+    load_slots.wait()
     load_left.wait()
     for slot in range(slot_count):
         grad = slots_ref[slot]
@@ -1886,7 +1946,10 @@
     saves[2].start()
     load_tokens.wait()
     saves[5].start()
+    load_grads.wait()
+    saves[0].start()
     load_masters.wait()
+    load_rows.wait()
     for block in range(masters.shape[0]):
         value = masters[block] - weight_rate * rows_ref[place_ref[block]].astype(F32)
         masters[block] = value
@@ -1902,12 +1965,11 @@
         jnp.sqrt(energy) + energy_epsilon
     )
     grad = table_ref[31:32, 0:HEAD_NUMBER]
-    energy = (
-        covariance_forgetting * sharp_ref[1:2, :] + (1.0 - covariance_forgetting) * grad * grad
-    )
-    sharp_out_ref[0:1, :] = grad
-    sharp_out_ref[1:2, :] = energy
-    sharp_out_ref[2:3, :] = sharp_ref[0:1, :] - sharpness_step_size * grad / (
+    grad = grad.reshape(HEAD_NUMBER)
+    energy = covariance_forgetting * sharp_energy_ref[...] + (1.0 - covariance_forgetting) * grad * grad
+    sharp_grad_ref[...] = grad
+    sharp_energy_out_ref[...] = energy
+    sharp_out_ref[...] = sharp_ref[...] - sharpness_step_size * grad / (
         jnp.sqrt(energy) + energy_epsilon
     )
     for save in saves:
@@ -1915,7 +1977,19 @@
 
 
 def finish(
-    places, grads, slots, rows, table, energy, coefficients, sharps, left, right, masters, tokens
+    places,
+    table,
+    energy,
+    coefficients,
+    sharpness,
+    sharpness_energy,
+    grads,
+    slots,
+    rows,
+    left,
+    right,
+    masters,
+    tokens,
 ):
     shape = jax.ShapeDtypeStruct
     return pl.pallas_call(
@@ -1930,21 +2004,40 @@
             shape(energy.shape, F32),
             shape(energy.shape, F32),
             shape(energy.shape, F32),
-            shape((3, sharps.shape[1]), F32),
+            shape(sharpness.shape, F32),
+            shape(sharpness.shape, F32),
+            shape(sharpness.shape, F32),
         ),
-        in_specs=[SMEM_SPEC] + [VMEM_SPEC] * 7 + [ANY_SPEC] * 4,
-        out_specs=(ANY_SPEC,) * 6 + (VMEM_SPEC,) * 4,
+        in_specs=[SMEM_SPEC] + [VMEM_SPEC] * 5 + [ANY_SPEC] * 7,
+        out_specs=(ANY_SPEC,) * 6 + (VMEM_SPEC,) * 6,
         scratch_shapes=[
             pltpu.VMEM(left.shape, F32),
             pltpu.VMEM(right.shape, F32),
             pltpu.VMEM(masters.shape, F32),
             pltpu.VMEM(masters.shape, BF16),
             pltpu.VMEM(tokens.shape, BF16),
-            pltpu.SemaphoreType.DMA((10,)),
+            pltpu.VMEM(grads.shape, F32),
+            pltpu.VMEM(slots.shape, BF16),
+            pltpu.VMEM(rows.shape, BF16),
+            pltpu.SemaphoreType.DMA((13,)),
         ],
         compiler_params=pltpu.CompilerParams(vmem_limit_bytes=VMEM_LIMIT),
         name="finish",
-    )(places, grads, slots, rows, table, energy, coefficients, sharps, left, right, masters, tokens)
+    )(
+        places,
+        table,
+        energy,
+        coefficients,
+        sharpness,
+        sharpness_energy,
+        grads,
+        slots,
+        rows,
+        left,
+        right,
+        masters,
+        tokens,
+    )
 
 
 def shards(
@@ -2018,28 +2111,26 @@
             counts,
             3,
         )
-        *results, sharps = finish(
-            storage_position_map,
-            grads,
-            owned_grad,
-            my_rows,
-            table_total,
-            channel_energy_average,
-            channel_coefficients,
-            jnp.stack([head_sharpness, sharpness_energy_average]),
-            leading_covariance,
-            trailing_covariance,
-            projection_masters,
-            tokens_grad,
+        results = list(
+            finish(
+                storage_position_map,
+                table_total,
+                channel_energy_average,
+                channel_coefficients,
+                head_sharpness,
+                sharpness_energy_average,
+                grads,
+                owned_grad,
+                my_rows,
+                leading_covariance,
+                trailing_covariance,
+                projection_masters,
+                tokens_grad,
+            )
         )
         tokens_grad = results.pop(5)
-        return (layer_output, tokens_grad, *results, *sharps)
-    first_grad = jnp.einsum(
-        "stl,dsl->td",
-        head_low,
-        head_weights.reshape(feature_count, 3, PAD_WIDTH),
-        preferred_element_type=F32,
-    )
+        return (layer_output, tokens_grad, *results)
+    first_grad = dot_lanes(head_low, head_weights)
     unit, scale = centered(patch_embeddings.astype(F32))
     incoming_tokens_grad = (dx1 + norm_back(first_grad * table[0], unit, scale)).astype(BF16)
     mixing_table = mixing_table.at[0].set(jnp.sum(first_grad * unit, axis=0))

time: 243 us -> 237 us (0.975)
  Pallas kernels: 219 us -> 215 us
    pallas_call x1, Pallas kernels: 37.5 us -> 34.8 us  [mixing_backward(): pl.pallas_call(mixing_backward_kernel, out_shape=(shape((row_count, 3 * P...]
where the time goes in v6:
time: 237 us; the launch traced here: 236 us
  Pallas kernels  215 us (91%)
  between operations  14.1 us (6%)
  starting transfers between devices  3.87 us (2%)
  local copies, waits for them, and re-layouts  2.82 us (1%)
    pallas_call x1, Pallas kernels, settle(): pl.pallas_call(functools.partial(settle_kernel, counts), out_shape=(shape...  55.6 us
    pallas_call x1, Pallas kernels, feed_forward(): pl.pallas_call(feed_kernel, out_shape=(shape((row_count, width), BF16), s...  37.9 us
    pallas_call x1, Pallas kernels, mixing_backward(): pl.pallas_call(mixing_backward_kernel, out_shape=(shape((row_count, 3 * P...  34.8 us
    pallas_call x1, Pallas kernels, mixing_forward(): pl.pallas_call(mixing_forward_kernel, out_shape=(shape((row_count, width)...  23.1 us
    pallas_call x1, Pallas kernels, gather_start(): pl.pallas_call(functools.partial(gather_kernel, counts), out_shape=(shape...  21.7 us
    pallas_call x1, Pallas kernels, sum_all(): pl.pallas_call(functools.partial(sum_all_kernel, counts), out_shape=jax.S...  18.6 us
    pallas_call x1, Pallas kernels, sum_pair(): pl.pallas_call(functools.partial(sum_pair_kernel, counts), out_shape=(sha...  17.4 us
    pallas_call x1, Pallas kernels, finish(): pl.pallas_call(finish_kernel, out_shape=(shape(grads.shape, F32), shape(l...  6.31 us
  transfers between devices with their start and end apart: 2, of which 0 were waited for; matrix products, arithmetic and copies ran while one was open for 0% of the time, Pallas kernels for 42%

profile of v6, /device:TPU:1, one launch (start us, length us, event | category | flops | bytes accessed | tf_op | source)
XLA Modules:
  0.0 236.2 jit_solution(16586238580392930629)
XLA Ops:
  7.2 0.0 all-gather.2.cloned.1.call-start
  7.2 1.8 slice.7
  9.0 0.0 all-gather.2.cloned.1.call-update
  9.1 21.7 %gather_start.1 = (bf16[4,384,384]{2,1,0:T(8,128)(2,1)}, f32[32,384]{1,0:T(8,128)}) custom-call(f32[12,48,384]{2,1,0:T(8,128)} %masters_hbm.1, f32[29,48]{1,0:T(8,128)} %coefficient_ref.1), custom_call_target="tpu_custom_call" | custom-call | tf_op jit(solution)/shard_map/gather_start/pallas_call | solution.py:1379
  30.7 23.1 %mixing_forward.1 = (f32[1856,384]{1,0:T(8,128)}, f32[1856,1536]{1,0:T(8,128)}, bf16[1856,512]{1,0:T(8,128)(2,1)}, f32[16,4,48,128]{3,2,1,0:T(8,128)}, f32[16,4,...) custom-call(s32[16]{0:T(128)} %sides_ref.5, f32[8]{0:T(128)} %sharp_ref.5, ...), custom_call_target="tpu_custom_call" | custom-call | tf_op jit(solution)/shard_map/mixing_forward/pallas_call | solution.py:477
  53.9 18.6 %sum_all.1.bn_ref = f32[8,128]{1,0:T(8,128)} custom-call(f32[8,128]{1,0:T(8,128)} %get-tuple-element.57.part_ref), custom_call_target="tpu_custom_call" | custom-call | tf_op jit(solution)/shard_map/sum_all/pallas_call | solution.py:1219
  72.4 0.0 all-gather.2.cloned.1.call-done.weight_hbm
  72.4 37.9 %feed_forward.1 = (bf16[1856,384]{1,0:T(8,128)(2,1)}, f32[1856,384]{1,0:T(8,128)}, f32[3,1856,128]{2,1,0:T(8,128)}, bf16[16,4,48,384]{3,2,1,0:T(8,128)(2,1)}, f32[16,384]{1,0:T(8,128)}, /*index=5*/f32[8,128]{1,0:T(8,128)}) custom-call(s32[16]{0:T(128)} %sides_ref.5, f32[1856,384]{1,0:T(8,128)} %get-tuple-element.55.x1_hbm, ...), custom_call_target="tpu_custom_call" | custom-call | tf_op jit(solution)/shard_map/feed_forward/pallas_call | solution.py:752
  110.4 17.4 %sum_pair.1 = (f32[8,128]{1,0:T(8,128)}, bf16[8,4,48,384]{3,2,1,0:T(8,128)(2,1)}) custom-call(f32[8,128]{1,0:T(8,128)} %get-tuple-element.66.part_ref, bf16[16,4,48,384]{3,2,1,0:T(8,128)(2,1)} %get-tuple-element.67.blocks_hbm), custom_call_target="tpu_custom_call" | custom-call | tf_op jit(solution)/shard_map/sum_pair/pallas_call | solution.py:1279
  127.8 3.8 %all-to-all-start = ((bf16[8,4,48,384]{3,2,1,0:T(8,128)(2,1)}), bf16[8,4,48,384]{3,2,1,0:T(8,128)(2,1)S(1)}, u32[]{:S(2)}, u32[]{:S(2)}) async-start(bf16[8,4,48,384]{3,2,1,0:T(8,128)(2,1)} %get-tuple-element.70), calls=%async_computation | async-start | bytes 2359296 | tf_op jit(solution)/shard_map/all_to_all | solution.py:2085
  131.6 34.8 %mixing_backward.1 = (bf16[1856,1536]{1,0:T(8,128)(2,1)}, f32[1856,384]{1,0:T(8,128)}, bf16[384,1536]{1,0:T(8,128)(2,1)}, bf16[4,384,384]{2,1,0:T(8,128)(2,1)}, f32[16,384]{1,0:T(8,128)}) custom-call(s32[16]{0:T(128)} %sides_ref.5, f32[8]{0:T(128)} %sharp_ref.5, bf16[1856,384]{1,0:T(8,128)(2,1)} %input_hbm.3, ...), custom_call_target="tpu_custom_call" | custom-call | tf_op jit(solution)/shard_map/mixing_backward/pallas_call | solution.py:1085
  166.4 0.0 all-to-all-done.feed_hbm
  166.4 0.0 copy-start
  166.5 1.0 copy-done
  167.5 55.6 %settle.1 = (f32[12,48,384]{2,1,0:T(8,128)}, bf16[2,384,384]{2,1,0:T(8,128)(2,1)}, bf16[16,48,384]{2,1,0:T(8,128)(2,1)}, f32[32,128]{1,0:T(8,128)}, bf16[1856,384]{1,0:T(8,128)(2,1)}) custom-call(s32[12]{0:T(128)} %place_ref.3, bf16[4,384,384]{2,1,0:T(8,128)(2,1)} %get-tuple-element.69.mix_hbm, bf16[8,4,48,384]{3,2,1,0:T(8,128)(2,1)} %copy-done, ...), custom_call_target="tpu_custom_call" | custom-call | tf_op jit(solution)/shard_map/settle/pallas_call | solution.py:1815
  223.0 6.3 %finish.1 = (f32[12,48,384]{2,1,0:T(8,128)}, f32[2,384,384]{2,1,0:T(8,128)}, f32[2,384,384]{2,1,0:T(8,128)}, f32[12,48,384]{2,1,0:T(8,128)}, bf16[12,48,384]{2,1...) custom-call(s32[12]{0:T(128)} %place_ref.3, ...), custom_call_target="tpu_custom_call" | custom-call | tf_op jit(solution)/shard_map/finish/pallas_call | solution.py:1995
Async XLA Ops:
  7.2 65.3 %all-gather.2.cloned.1.call-start = ((), (), s32[]{:S(2)}) async-start(), calls=%async_computation.1 | async-start | bytes 2654208 | tf_op jit(solution)/shard_map/all_gather | solution.py:2074
  127.8 38.6 %all-to-all-start = ((bf16[8,4,48,384]{3,2,1,0:T(8,128)(2,1)}), bf16[8,4,48,384]{3,2,1,0:T(8,128)(2,1)S(1)}, u32[]{:S(2)}, u32[]{:S(2)}) async-start(bf16[8,4,48,384]{3,2,1,0:T(8,128)(2,1)} %get-tuple-element.70), calls=%async_computation | async-start | bytes 2359296 | tf_op jit(solution)/shard_map/all_to_all | solution.py:2085
  166.4 1.0 copy-start
Sparse Core Ops, SparseCore 0:
  10.8 53.0 all-gather.1

commit v7 on v6

--- a/solution.py
+++ b/solution.py
@@ -20,6 +20,7 @@
 SMALL_WINDOW = 48
 LARGE_WINDOW = 208
 CROP_GROUP = 2
+SAVE_ROWS = 64
 ROW_TILE = 464
 HIDDEN_PARTS = 6
 VMEM_LIMIT = 60 * 2**20
@@ -137,6 +138,18 @@
     return carry
 
 
+def row_copies(pairs, first, size, sem):
+    rows = pl.ds(first, size)
+    return [
+        pltpu.make_async_copy(
+            source.at[:, rows] if chunked else source.at[rows],
+            target.at[:, rows] if chunked else target.at[rows],
+            sem,
+        )
+        for source, target, chunked in pairs
+    ]
+
+
 def live_total(sides_ref):
     return lax.fori_loop(
         0, sides_ref.shape[0], lambda c, t: t + sides_ref[c] * sides_ref[c], jnp.int32(0)
@@ -147,9 +160,24 @@
     return lax.broadcasted_iota(jnp.int32, (rows, width), 0) + first < limit
 
 
-def for_groups(sides_ref, step, carry):
+def save_rows(source, target, sem, first, rows):
+    rows = pl.ds(pl.multiple_of(first, 8), rows)
+    pltpu.make_async_copy(source.at[:, rows], target.at[:, rows], sem).start()
+
+
+def for_groups(sides_ref, step, carry, saves=()):
+    def save(first, last):
+        def body(part, _):
+            for source, target, sem in saves:
+                save_rows(source, target, sem, part * SAVE_ROWS, SAVE_ROWS)
+            return 0
+
+        if saves:
+            lax.fori_loop(first, last, body, 0)
+        return last
+
     def crop_body(crop, state):
-        start, carry = state
+        start, saved, carry = state
         side = sides_ref[crop]
         cells = side * side
         inverse = 1.0 / jnp.full((8, LANES), side, jnp.int32).astype(F32)
@@ -173,9 +201,18 @@
             return carry
 
         carry = lax.fori_loop(start // 16, (start + cells + 15) // 16, group_body, carry)
-        return start + cells, carry
-
-    return lax.fori_loop(0, sides_ref.shape[0], crop_body, (jnp.int32(0), carry))[1]
+        saved = save(saved, (start + cells) // 16 * 16 // SAVE_ROWS)
+        return start + cells, saved, carry
+
+    state = (jnp.int32(0), jnp.int32(0), carry)
+    _, saved, carry = lax.fori_loop(0, sides_ref.shape[0], crop_body, state)
+    for source, target, sem in saves:
+        done = source.shape[1] // SAVE_ROWS * SAVE_ROWS
+        if done < source.shape[1]:
+            save_rows(source, target, sem, done, source.shape[1] - done)
+    if saves:
+        save(saved, saves[0][0].shape[1] // SAVE_ROWS)
+    return carry
 
 
 def conv_forward(source, chunk, row, side, masks, taps):
@@ -459,9 +496,12 @@
             carry[chunks + chunk] = carry[chunks + chunk] + active * active
         return tuple(carry)
 
-    sums = for_groups(sides_ref, conv_step, (zero,) * (2 * chunks))
-    saves[5].start()
-    saves[6].start()
+    sums = for_groups(
+        sides_ref,
+        conv_step,
+        (zero,) * (2 * chunks),
+        ((slope_ref, slope_hbm, sems.at[5]), (e_ref, e_hbm, sems.at[6])),
+    )
     for index, value in enumerate(sums):
         sums_ref[index : index + 1, :] = jnp.sum(value, axis=0, keepdims=True)
     sums_ref[2 * chunks : 2 * chunks + 1, :] = jnp.full((1, LANES), total_live, jnp.int32).astype(F32)
@@ -555,14 +595,16 @@
     feed_grad,
     pre_grad,
     grads,
-    weight_sums,
+    up_sum,
+    down_sum,
+    weight_low,
     sems,
+    tile_sems,
 ):
     loads = [
         pltpu.make_async_copy(source, target, sems.at[index])
         for index, (source, target) in enumerate(
             (
-                (e_hbm, e_ref),
                 (x1_hbm, x1_ref),
                 (weight_hbm, weight_ref),
                 (adjoint_hbm, adjoint_ref),
@@ -580,6 +622,15 @@
             )
         )
     ]
+
+    tiled = [(e_hbm, e_ref, True)]
+
+    def start_tile(first, size, _):
+        for load in row_copies(tiled, first, size, tile_sems.at[lax.div(first, ROW_TILE)]):
+            load.start()
+        return 0
+
+    for_rows(x1_hbm.shape[0], ROW_TILE, start_tile)
     for load in loads:
         load.start()
     row_count, width = x1_ref.shape
@@ -595,6 +646,8 @@
         return weight_ref[expand : 2 * expand].reshape(hidden, width)
 
     def normalize(first, size, _):
+        for load in row_copies(tiled, first, size, tile_sems.at[lax.div(first, ROW_TILE)]):
+            load.wait()
         rows = pl.ds(first, size)
         live = row_mask(first, size, LANES, total_live)
         for chunk in range(chunks):
@@ -607,7 +660,6 @@
             dn_ref[chunk, rows, :] = jnp.zeros((size, LANES), F32)
         return 0
 
-    loads[0].wait()
     for_rows(row_count, ROW_TILE, normalize)
 
     taps = [tap_vectors(table_ref, 20, chunk) for chunk in range(chunks)]
@@ -621,11 +673,12 @@
 
     for_groups(sides_ref, conv_step, 0)
 
-    for load in loads[1:]:
+    for load in loads:
         load.wait()
     for part in range(expand):
         up_weight[:, part * width : (part + 1) * width] = weight_ref[part]
-    weight_sums[...] = jnp.zeros_like(weight_sums)
+    up_sum[...] = jnp.zeros_like(up_sum)
+    down_sum[...] = jnp.zeros_like(down_sum)
     grads[...] = jnp.zeros_like(grads)
 
     def z_rows(rows):
@@ -672,12 +725,8 @@
             pre_grad[:, lanes] = (hidden_grad * gelu_slope(value, share, bell)).astype(BF16)
         feed[...] = dot(hidden_low[...], down_weight())
         third_grad[...] = dot_lanes(pre_grad[...], up_weight[...])
-        weight_sums[expand : 2 * expand] += dot_rows(hidden_low[...], feed_grad[...]).reshape(
-            expand, width, width
-        )
-        up_grad = dot_rows(third_low[...], pre_grad[...])
-        for part in range(expand):
-            weight_sums[part] += up_grad[:, part * width : (part + 1) * width]
+        down_sum[...] += dot_rows(feed_grad[...], hidden_low[...])
+        up_sum[...] += dot_rows(third_low[...], pre_grad[...])
 
         value = x2[...] + table_ref[10:11, :] * feed[...]
         live = row_mask(base, tile, width, total_live)
@@ -698,14 +747,17 @@
     saves[0].start()
     saves[1].start()
 
+    for part in range(expand):
+        lanes = slice(part * width, (part + 1) * width)
+        weight_low[part] = up_sum[:, lanes].astype(BF16)
+        weight_low[expand + part] = down_sum[:, lanes].T.astype(BF16)
+
     owners, pieces, shard, _ = weight_grad_ref.shape
     inner = width // shard
     for owner in range(owners):
         rows = slice(owner % inner * shard, (owner % inner + 1) * shard)
         for piece in range(pieces):
-            weight_grad_ref[owner, piece] = weight_sums[
-                owner // inner * pieces + piece, rows, :
-            ].astype(BF16)
+            weight_grad_ref[owner, piece] = weight_low[owner // inner * pieces + piece, rows, :]
 
     saves[2].start()
 
@@ -728,8 +780,9 @@
             result.append((*tap_sums, sums[9] + total * standard, sums[10] + total))
         return tuple(result)
 
-    sums = for_groups(sides_ref, back_step, ((zero,) * 11,) * chunks)
-    saves[3].start()
+    sums = for_groups(
+        sides_ref, back_step, ((zero,) * 11,) * chunks, ((dn_ref, dn_hbm, sems.at[7]),)
+    )
     for chunk in range(chunks):
         lanes = chunk_lanes(chunk)
         for index, value in enumerate(sums[chunk]):
@@ -784,8 +837,11 @@
             pltpu.VMEM((tile, width), BF16),
             pltpu.VMEM((tile, expand * width), BF16),
             pltpu.VMEM((4, 8, width), F32),
-            pltpu.VMEM((2 * expand, width, width), F32),
+            pltpu.VMEM((width, expand * width), F32),
+            pltpu.VMEM((width, expand * width), F32),
+            pltpu.VMEM(weights.shape, BF16),
             pltpu.SemaphoreType.DMA((8,)),
+            pltpu.SemaphoreType.DMA(((row_count + ROW_TILE - 1) // ROW_TILE,)),
         ],
         compiler_params=pltpu.CompilerParams(vmem_limit_bytes=VMEM_LIMIT),
         name="feed_forward",
@@ -834,6 +890,7 @@
     order_ref,
     start_ref,
     load_sems,
+    tile_sems,
 ):
     row_count, width = input_hbm.shape
     low_rows, input_ref = head_low.at[:, 0:width], head_low.at[:, PAD_WIDTH : PAD_WIDTH + width]
@@ -848,10 +905,6 @@
         pltpu.make_async_copy(source, target, load_sems.at[index])
         for index, (source, target) in enumerate(
             (
-                (x1_hbm, x1_ref),
-                (slope_hbm, slope_ref),
-                (e_hbm, e_ref),
-                (dn_hbm, dn_ref),
                 (mixed_hbm, mixed_ref),
                 (dx2_hbm, dx2_ref),
                 (qkv_hbm, qkv_ref),
@@ -876,6 +929,19 @@
                 head_low.at[rows], head_low_hbm.at[rows], load_sems.at[len(loads) + 3 + step]
             )
         )
+    tiled = [
+        (x1_hbm, x1_ref, False),
+        (slope_hbm, slope_ref, True),
+        (e_hbm, e_ref, True),
+        (dn_hbm, dn_ref, True),
+    ]
+
+    def start_tile(first, size, _):
+        for load in row_copies(tiled, first, size, tile_sems.at[lax.div(first, ROW_TILE)]):
+            load.start()
+        return 0
+
+    for_rows(row_count, ROW_TILE, start_tile)
     for load in loads:
         load.start()
     tile = tile_rows(row_count, 2)
@@ -901,10 +967,10 @@
     input_load.wait()
     for_rows(row_count, ROW_TILE, first_norm)
 
-    for load in loads[0:4]:
-        load.wait()
 
     def batch_back(first, size, _):
+        for load in row_copies(tiled, first, size, tile_sems.at[lax.div(first, ROW_TILE)]):
+            load.wait()
         rows = pl.ds(first, size)
         live = row_mask(first, size, LANES, total_live)
         unit, _ = centered(x1_ref[rows, :])
@@ -948,7 +1014,7 @@
                 value, axis=0, keepdims=True
             )
 
-    for load in loads[4:6]:
+    for load in loads[0:2]:
         load.wait()
 
     @pl.loop(0, row_count // tile)
@@ -993,7 +1059,7 @@
     weight_grad_ref[3] = dot(mapping, low).astype(BF16)
     sharp_sums[...] = jnp.zeros_like(sharp_sums)
 
-    for load in loads[6:]:
+    for load in loads[2:]:
         load.wait()
 
     def crop_step(members):
@@ -1117,6 +1183,7 @@
             pltpu.SMEM((2 * crops,), jnp.int32),
             pltpu.SMEM((crops,), jnp.int32),
             pltpu.SemaphoreType.DMA((12 + row_count // tile_rows(row_count, 2),)),
+            pltpu.SemaphoreType.DMA(((row_count + ROW_TILE - 1) // ROW_TILE,)),
         ],
         compiler_params=pltpu.CompilerParams(vmem_limit_bytes=VMEM_LIMIT),
         name="mixing_backward",
@@ -1232,7 +1299,7 @@
 
 
 def sum_pair_kernel(
-    counts, part_ref, blocks_hbm, total_ref, sums_ref, parts, own, other, send, receive, sems
+    counts, part_ref, blocks_hbm, total_ref, sums_hbm, parts, own, other, sums_ref, send, receive, sems
 ):
     n_dp, n_fsdp = counts
     dp, fsdp = lax.axis_index("dp"), lax.axis_index("fsdp")
@@ -1263,6 +1330,8 @@
     blocks.wait_recv()
     for owner in range(n_fsdp):
         sums_ref[owner] = (own[owner].astype(F32) + other[owner].astype(F32)).astype(BF16)
+    save = pltpu.make_async_copy(sums_ref, sums_hbm, sems.at[3])
+    save.start()
     for copy in copies:
         copy.wait()
     total = parts[0]
@@ -1270,6 +1339,7 @@
         total = total + parts[k]
     total_ref[...] = total
     blocks.wait_send()
+    save.wait()
 
 
 def sum_pair(part, blocks, counts, identity):
@@ -1280,14 +1350,15 @@
         functools.partial(sum_pair_kernel, counts),
         out_shape=(shape(part.shape, F32), shape(half, BF16)),
         in_specs=[VMEM_SPEC, ANY_SPEC],
-        out_specs=(VMEM_SPEC, VMEM_SPEC),
+        out_specs=(VMEM_SPEC, ANY_SPEC),
         scratch_shapes=[
             pltpu.VMEM((size, *part.shape), F32),
             pltpu.VMEM(half, BF16),
             pltpu.VMEM(half, BF16),
+            pltpu.VMEM(half, BF16),
             pltpu.SemaphoreType.DMA((size - 1,)),
             pltpu.SemaphoreType.DMA((size - 1,)),
-            pltpu.SemaphoreType.DMA((3,)),
+            pltpu.SemaphoreType.DMA((4,)),
         ],
         compiler_params=comm_params(identity),
         name="sum_pair",
@@ -1296,11 +1367,12 @@
 
 def gather_kernel(
     counts,
-    masters_ref,
+    masters_hbm,
     table_ref,
-    blocks_ref,
+    blocks_hbm,
     full_table_ref,
     blocks,
+    masters,
     tables,
     stage,
     ring_send,
@@ -1311,11 +1383,14 @@
     cross_recv,
     pair_send,
     pair_recv,
+    local_sems,
 ):
     n_dp, n_fsdp = counts
     dp, fsdp = lax.axis_index("dp"), lax.axis_index("fsdp")
-    shard, width = masters_ref.shape[1:]
+    shard, width = masters_hbm.shape[1:]
     columns = table_ref.shape[1]
+    load = pltpu.make_async_copy(masters_hbm.at[dp], masters, local_sems.at[0])
+    load.start()
     across = lax.rem(dp + 2, 4)
     pair = dp + 1 - 2 * lax.rem(dp, 2)
     peers = flip_peers("fsdp", n_fsdp)
@@ -1330,7 +1405,8 @@
     stage[...] = jnp.zeros_like(stage)
     stage[0 : table_ref.shape[0], 0:columns] = table_ref[...]
     tables[fsdp] = stage[...].astype(BF16)
-    blocks[dp, pl.ds(pl.multiple_of(fsdp * shard, 16), shard), :] = masters_ref[dp].astype(BF16)
+    load.wait()
+    blocks[dp, pl.ds(pl.multiple_of(fsdp * shard, 16), shard), :] = masters[...].astype(BF16)
     own = piece(dp, fsdp)
     ring = [
         push(own, own, ring_send.at[k], ring_recv.at[k], peer) for k, peer in enumerate(peers)
@@ -1366,9 +1442,11 @@
     full_table_ref[...] = total
     for copy in pairing:
         copy.wait_recv()
-    blocks_ref[...] = blocks[...]
+    save = pltpu.make_async_copy(blocks, blocks_hbm, local_sems.at[1])
+    save.start()
     for copy in ring + table_copies + crossing + pairing:
         copy.wait_send()
+    save.wait()
 
 
 def gather_start(masters, coefficients, counts, identity):
@@ -1379,10 +1457,11 @@
     return pl.pallas_call(
         functools.partial(gather_kernel, counts),
         out_shape=(shape((4, width, width), BF16), shape((32, width), F32)),
-        in_specs=[VMEM_SPEC, VMEM_SPEC],
-        out_specs=(VMEM_SPEC, VMEM_SPEC),
+        in_specs=[ANY_SPEC, VMEM_SPEC],
+        out_specs=(ANY_SPEC, VMEM_SPEC),
         scratch_shapes=[
             pltpu.VMEM((4, width, width), BF16),
+            pltpu.VMEM(masters.shape[1:], F32),
             pltpu.VMEM((n_fsdp, 32, LANES), BF16),
             pltpu.VMEM((32, LANES), F32),
             dma((n_fsdp - 1,)),
@@ -1393,6 +1472,7 @@
             dma((n_fsdp,)),
             dma((2, n_fsdp)),
             dma((2, n_fsdp)),
+            dma((2,)),
         ],
         compiler_params=comm_params(identity),
         name="gather_start",

time: 237 us -> 230 us (0.970)
  Pallas kernels: 215 us -> 208 us
    pallas_call x1, Pallas kernels: 18.6 us -> 14.7 us  [sum_all(): pl.pallas_call(functools.partial(sum_all_kernel, counts), out_shape=jax.S...]
    pallas_call x1, Pallas kernels: 55.6 us -> 51.8 us  [settle(): pl.pallas_call(functools.partial(settle_kernel, counts), out_shape=(shape...]
where the time goes in v7:
time: 230 us; the launch traced here: 229 us
  Pallas kernels  208 us (90%)
  between operations  14.1 us (6%)
  starting transfers between devices  3.83 us (2%)
  local copies, waits for them, and re-layouts  2.82 us (1%)
    pallas_call x1, Pallas kernels, settle(): pl.pallas_call(functools.partial(settle_kernel, counts), out_shape=(shape...  51.8 us
    pallas_call x1, Pallas kernels, feed_forward(): pl.pallas_call(feed_kernel, out_shape=(shape((row_count, width), BF16), s...  36.9 us
    pallas_call x1, Pallas kernels, mixing_backward(): pl.pallas_call(mixing_backward_kernel, out_shape=(shape((row_count, 3 * P...  35.5 us
    pallas_call x1, Pallas kernels, mixing_forward(): pl.pallas_call(mixing_forward_kernel, out_shape=(shape((row_count, width)...  24.6 us
    pallas_call x1, Pallas kernels, gather_start(): pl.pallas_call(functools.partial(gather_kernel, counts), out_shape=(shape...  21.7 us
    pallas_call x1, Pallas kernels, sum_pair(): pl.pallas_call(functools.partial(sum_pair_kernel, counts), out_shape=(sha...  16.2 us
    pallas_call x1, Pallas kernels, sum_all(): pl.pallas_call(functools.partial(sum_all_kernel, counts), out_shape=jax.S...  14.7 us
    pallas_call x1, Pallas kernels, finish(): pl.pallas_call(finish_kernel, out_shape=(shape(grads.shape, F32), shape(l...  6.32 us
  transfers between devices with their start and end apart: 2, of which 0 were waited for; matrix products, arithmetic and copies ran while one was open for 0% of the time, Pallas kernels for 42%

profile of v7, /device:TPU:1, one launch (start us, length us, event | category | flops | bytes accessed | tf_op | source)
XLA Modules:
  0.0 228.6 jit_solution(4038549868489872330)
XLA Ops:
  7.2 0.0 all-gather.2.cloned.1.call-start
  7.2 1.8 slice.7
  9.0 0.0 all-gather.2.cloned.1.call-update
  9.1 21.7 %gather_start.1 = (bf16[4,384,384]{2,1,0:T(8,128)(2,1)}, f32[32,384]{1,0:T(8,128)}) custom-call(f32[12,48,384]{2,1,0:T(8,128)} %masters_hbm.3, f32[29,48]{1,0:T(8,128)} %coefficient_ref.1), custom_call_target="tpu_custom_call" | custom-call | tf_op jit(solution)/shard_map/gather_start/pallas_call | solution.py:1457
  30.7 24.6 %mixing_forward.1 = (f32[1856,384]{1,0:T(8,128)}, f32[1856,1536]{1,0:T(8,128)}, bf16[1856,512]{1,0:T(8,128)(2,1)}, f32[16,4,48,128]{3,2,1,0:T(8,128)}, f32[16,4,...) custom-call(s32[16]{0:T(128)} %sides_ref.5, f32[8]{0:T(128)} %sharp_ref.5, ...), custom_call_target="tpu_custom_call" | custom-call | tf_op jit(solution)/shard_map/mixing_forward/pallas_call | solution.py:517
  55.3 14.7 %sum_all.1.bn_ref = f32[8,128]{1,0:T(8,128)} custom-call(f32[8,128]{1,0:T(8,128)} %get-tuple-element.57.part_ref), custom_call_target="tpu_custom_call" | custom-call | tf_op jit(solution)/shard_map/sum_all/pallas_call | solution.py:1286
  70.0 0.0 all-gather.2.cloned.1.call-done.weight_hbm
  70.1 36.9 %feed_forward.1 = (bf16[1856,384]{1,0:T(8,128)(2,1)}, f32[1856,384]{1,0:T(8,128)}, f32[3,1856,128]{2,1,0:T(8,128)}, bf16[16,4,48,384]{3,2,1,0:T(8,128)(2,1)}, f32[16,384]{1,0:T(8,128)}, /*index=5*/f32[8,128]{1,0:T(8,128)}) custom-call(s32[16]{0:T(128)} %sides_ref.5, f32[1856,384]{1,0:T(8,128)} %get-tuple-element.55.x1_hbm, ...), custom_call_target="tpu_custom_call" | custom-call | tf_op jit(solution)/shard_map/feed_forward/pallas_call | solution.py:805
  107.0 16.2 %sum_pair.1 = (f32[8,128]{1,0:T(8,128)}, bf16[8,4,48,384]{3,2,1,0:T(8,128)(2,1)}) custom-call(f32[8,128]{1,0:T(8,128)} %get-tuple-element.66.part_ref, bf16[16,4,48,384]{3,2,1,0:T(8,128)(2,1)} %get-tuple-element.67.blocks_hbm), custom_call_target="tpu_custom_call" | custom-call | tf_op jit(solution)/shard_map/sum_pair/pallas_call | solution.py:1349
  123.2 3.8 %all-to-all-start = ((bf16[8,4,48,384]{3,2,1,0:T(8,128)(2,1)}), bf16[8,4,48,384]{3,2,1,0:T(8,128)(2,1)S(1)}, u32[]{:S(2)}, u32[]{:S(2)}) async-start(bf16[8,4,48,384]{3,2,1,0:T(8,128)(2,1)} %get-tuple-element.70), calls=%async_computation | async-start | bytes 2359296 | tf_op jit(solution)/shard_map/all_to_all | solution.py:2165
  127.0 35.5 %mixing_backward.1 = (bf16[1856,1536]{1,0:T(8,128)(2,1)}, f32[1856,384]{1,0:T(8,128)}, bf16[384,1536]{1,0:T(8,128)(2,1)}, bf16[4,384,384]{2,1,0:T(8,128)(2,1)}, f32[16,384]{1,0:T(8,128)}) custom-call(s32[16]{0:T(128)} %sides_ref.5, f32[8]{0:T(128)} %sharp_ref.5, bf16[1856,384]{1,0:T(8,128)(2,1)} %input_hbm.3, ...), custom_call_target="tpu_custom_call" | custom-call | tf_op jit(solution)/shard_map/mixing_backward/pallas_call | solution.py:1151
  162.6 0.0 all-to-all-done.feed_hbm
  162.6 0.0 copy-start
  162.6 1.0 copy-done
  163.6 51.8 %settle.1 = (f32[12,48,384]{2,1,0:T(8,128)}, bf16[2,384,384]{2,1,0:T(8,128)(2,1)}, bf16[16,48,384]{2,1,0:T(8,128)(2,1)}, f32[32,128]{1,0:T(8,128)}, bf16[1856,384]{1,0:T(8,128)(2,1)}) custom-call(s32[12]{0:T(128)} %place_ref.3, bf16[4,384,384]{2,1,0:T(8,128)(2,1)} %get-tuple-element.69.mix_hbm, bf16[8,4,48,384]{3,2,1,0:T(8,128)(2,1)} %copy-done, ...), custom_call_target="tpu_custom_call" | custom-call | tf_op jit(solution)/shard_map/settle/pallas_call | solution.py:1895
  215.4 6.3 %finish.1 = (f32[12,48,384]{2,1,0:T(8,128)}, f32[2,384,384]{2,1,0:T(8,128)}, f32[2,384,384]{2,1,0:T(8,128)}, f32[12,48,384]{2,1,0:T(8,128)}, bf16[12,48,384]{2,1...) custom-call(s32[12]{0:T(128)} %place_ref.3, ...), custom_call_target="tpu_custom_call" | custom-call | tf_op jit(solution)/shard_map/finish/pallas_call | solution.py:2075
Async XLA Ops:
  7.2 62.9 %all-gather.2.cloned.1.call-start = ((), (), s32[]{:S(2)}) async-start(), calls=%async_computation.1 | async-start | bytes 2654208 | tf_op jit(solution)/shard_map/all_gather | solution.py:2154
  123.2 39.4 %all-to-all-start = ((bf16[8,4,48,384]{3,2,1,0:T(8,128)(2,1)}), bf16[8,4,48,384]{3,2,1,0:T(8,128)(2,1)S(1)}, u32[]{:S(2)}, u32[]{:S(2)}) async-start(bf16[8,4,48,384]{3,2,1,0:T(8,128)(2,1)} %get-tuple-element.70), calls=%async_computation | async-start | bytes 2359296 | tf_op jit(solution)/shard_map/all_to_all | solution.py:2165
  162.6 1.0 copy-start
Sparse Core Ops, SparseCore 0:
  10.8 52.9 all-gather.1
